TPU v7x, 32 devices: a whole 2x2x4 slice. The times are simulated.
32 devices in a mesh: dp: 4 (over z), fsdp: 8 (over y, x, core).
Axes of the slice: x: 2, y: 2, z: 4, core: 2. Of those that a mesh axis runs over, the one named last changes fastest.
Arguments:
- hidden_in: bfloat16 [4096, 2048], P(('dp', 'fsdp')), may hold values from -6 to 6
- lengths: int32 [4], replicated, may hold values from 256 to 1024, as said below
- routes: int32 [4096, 8], P(('dp', 'fsdp')), may hold values from 0 to 15, all different within a row; in each aligned block of 128 rows (0 to 127, 128 to 255, ...) at most 80 rows name the same one
- attn_gain: bfloat16 [2048], P(('dp', 'fsdp')), may hold values from 0.25 to 1.75
- query_gain: bfloat16 [2048], P(('dp', 'fsdp')), may hold values from 0.25 to 1.75
- key_gain: bfloat16 [2048], P(('dp', 'fsdp')), may hold values from 0.25 to 1.75
- ffn_gain: bfloat16 [2048], P(('dp', 'fsdp')), may hold values from 0.25 to 1.75
- qkv_weight: bfloat16 [2048, 6144], P(('dp', 'fsdp')), may hold values from -0.125 to 0.125
- out_weight: bfloat16 [2048, 2048], P(('dp', 'fsdp')), may hold values from -1 to 1
- router_weight: bfloat16 [2048, 16], P(('dp', 'fsdp')), may hold values from -0.0625 to 0.0625
- expert_in: bfloat16 [2048, 16, 2048], P(('dp', 'fsdp')), may hold values from -0.125 to 0.125
- expert_out: bfloat16 [1024, 16, 2048], P(('dp', 'fsdp')), may hold values from -1.5 to 1.5
- cotangent: bfloat16 [4096, 2048], P(('dp', 'fsdp')), may hold values from -6 to 6
Outputs:
- block_out: bfloat16 [4096, 2048], P(('dp', 'fsdp'))
- hidden_grad: float32 [4096, 2048], P(('dp', 'fsdp'))
- attn_gain_grad: float32 [2048], P(('dp', 'fsdp'))
- query_gain_grad: float32 [2048], P(('dp', 'fsdp'))
- key_gain_grad: float32 [2048], P(('dp', 'fsdp'))
- ffn_gain_grad: float32 [2048], P(('dp', 'fsdp'))
- qkv_weight_grad: float32 [2048, 6144], P(('dp', 'fsdp'))
- out_weight_grad: float32 [2048, 2048], P(('dp', 'fsdp'))
- router_weight_grad: float32 [2048, 16], P(('dp', 'fsdp'))
- expert_in_grad: float32 [2048, 16, 2048], P(('dp', 'fsdp'))
- expert_out_grad: float32 [1024, 16, 2048], P(('dp', 'fsdp'))
- stats: float32 [3], replicated
Inputs may be any that keep to these rules, and one draw needn't show every extreme that they name: `lengths`: one sequence, chosen by the seed, has all 1024 slots valid and another has 256. `routes`: each token names 8 different experts; among the 128 tokens of one device no expert is named more than 80 times, a bound that some block reaches.
All inputs are finite; a program needn't handle non-finite values.
Results may differ from a plain program's by a relative error of at most 0.02.
Values may be sent and summed in bfloat16 or wider, within the bound.
A program may use at most 320 MiB of HBM per device.

v0:
```python
import jax
import jax.numpy as jnp
from jax import lax
from jax.sharding import PartitionSpec as P

HEADS = 16
HEAD_DIM = 128
CAP = 80


EPS = 1e-05


def rms_scale(values_in):
    return lax.rsqrt(jnp.mean(values_in * values_in, axis=-1, keepdims=True) + EPS)


def norm_back(grad_in, unit_rows, scaling):
    return scaling * (grad_in - unit_rows * jnp.mean(grad_in * unit_rows, axis=-1, keepdims=True))


def rotate(values_in, cosine, sine, direction):
    half_width = values_in.shape[-1] // 2
    first_half = values_in[..., :half_width]
    second_half = values_in[..., half_width:]
    return jnp.concatenate(
        [
            first_half * cosine - direction * second_half * sine,
            second_half * cosine + direction * first_half * sine,
        ],
        axis=-1,
    )


def fetch_shared(attn_gain, query_gain, key_gain, ffn_gain, router_weight, qkv_weight, out_weight):
    return (
        lax.all_gather(attn_gain, ("dp", "fsdp"), axis=0, tiled=True),
        lax.all_gather(query_gain, ("dp", "fsdp"), axis=0, tiled=True),
        lax.all_gather(key_gain, ("dp", "fsdp"), axis=0, tiled=True),
        lax.all_gather(ffn_gain, ("dp", "fsdp"), axis=0, tiled=True),
        lax.all_gather(router_weight, ("dp", "fsdp"), axis=0, tiled=True),
        lax.all_gather(qkv_weight, ("dp", "fsdp"), axis=0, tiled=True),
        lax.all_gather(out_weight, ("dp", "fsdp"), axis=0, tiled=True),
    )


def fetch_local(expert_in, expert_out):
    exchanged = (
        lax.all_to_all(expert_in, "fsdp", split_axis=1, concat_axis=0, tiled=True),
        lax.all_to_all(expert_out, "fsdp", split_axis=1, concat_axis=0, tiled=True),
    )
    return (
        lax.all_gather(exchanged[0], "dp", axis=0, tiled=True),
        lax.all_gather(exchanged[1], "dp", axis=0, tiled=True),
    )


def send_home(values_in):
    return lax.all_to_all(
        values_in.astype(jnp.bfloat16), "fsdp", split_axis=1, concat_axis=0, tiled=True
    ).astype(values_in.dtype)


def routing_tables(routes, experts, capacity):
    flat_routes = routes.reshape(-1)
    onehot = (flat_routes[:, None] == jnp.arange(experts, dtype=jnp.int32)[None, :]).astype(
        jnp.int32
    )
    slot_index = jnp.sum(onehot * (jnp.cumsum(onehot, axis=0) - 1), axis=1)
    slot_place = flat_routes * capacity + slot_index
    row_numbers = jnp.arange(flat_routes.shape[0], dtype=jnp.int32)
    slot_owner = jnp.zeros((experts * capacity,), jnp.int32).at[slot_place].set(row_numbers)
    filled = jnp.zeros((experts * capacity,), jnp.float32).at[slot_place].set(1.0)
    return (slot_place, slot_owner, filled)


def expert_gate_up(routed, inner_weight):
    return jnp.einsum("erd,dej->erj", routed, inner_weight, preferred_element_type=jnp.float32)


def expert_activation(gate_up):
    half_width = gate_up.shape[-1] // 2
    return (jax.nn.silu(gate_up[..., :half_width]) * gate_up[..., half_width:]).astype(jnp.bfloat16)


def expert_output(activation, outer_weight):
    return jnp.einsum("erf,fed->erd", activation, outer_weight, preferred_element_type=jnp.float32)


def expert_backward(routed, gate_up, grad_result, inner_weight, outer_weight):
    half_width = gate_up.shape[-1] // 2
    gate_part = gate_up[..., :half_width]
    up_part = gate_up[..., half_width:]
    sigmoid_gate = jax.nn.sigmoid(gate_part)
    activation = expert_activation(gate_up)
    grad_activation = jnp.einsum(
        "erd,fed->erf", grad_result, outer_weight, preferred_element_type=jnp.float32
    )
    grad_gate = grad_activation * up_part * sigmoid_gate * (1.0 + gate_part * (1.0 - sigmoid_gate))
    grad_up = grad_activation * jax.nn.silu(gate_part)
    grad_gate_up = jnp.concatenate([grad_gate, grad_up], axis=-1).astype(jnp.bfloat16)
    grad_routed = jnp.einsum(
        "erj,dej->erd", grad_gate_up, inner_weight, preferred_element_type=jnp.float32
    )
    grad_inner = jnp.einsum(
        "erd,erj->dej", routed, grad_gate_up, preferred_element_type=jnp.float32
    )
    grad_outer = jnp.einsum(
        "erf,erd->fed", activation, grad_result, preferred_element_type=jnp.float32
    )
    return (grad_routed, grad_inner, grad_outer)


def body(
    hidden_in,
    lengths,
    routes,
    attn_gain,
    query_gain,
    key_gain,
    ffn_gain,
    qkv_weight,
    out_weight,
    router_weight,
    expert_in,
    expert_out,
    cotangent,
):
    tokens_here, model_width = hidden_in.shape
    experts = router_weight.shape[1]
    topk = routes.shape[1]
    capacity = CAP
    head_count = HEADS
    head_size = HEAD_DIM
    seq_length = tokens_here * lax.axis_size("fsdp")
    valid_length = lengths[lax.axis_index("dp")]
    tok_pos = lax.axis_index("fsdp") * tokens_here + jnp.arange(tokens_here, dtype=jnp.int32)
    live_mask = (tok_pos < valid_length).astype(jnp.float32)
    key_pos = jnp.arange(seq_length, dtype=jnp.int32)
    allowed = ((key_pos[None, :] <= tok_pos[:, None]) & (key_pos[None, :] < valid_length))[None]
    frequency = jnp.power(10000.0, -jnp.arange(head_size // 2, dtype=jnp.float32) * 2.0 / head_size)
    angles = tok_pos.astype(jnp.float32)[:, None] * frequency[None, :]
    cosine = jnp.cos(angles)[:, None, :]
    sine = jnp.sin(angles)[:, None, :]
    scaling = head_size ** (-0.5)
    shape3 = (tokens_here, head_count, head_size)
    shared = fetch_shared(
        attn_gain, query_gain, key_gain, ffn_gain, router_weight, qkv_weight, out_weight
    )
    gain_attn = shared[0].astype(jnp.float32)
    gain_query = shared[1].astype(jnp.float32)
    gain_key = shared[2].astype(jnp.float32)
    gain_ffn = shared[3].astype(jnp.float32)
    router_full = shared[4]
    qkv_full = shared[5]
    out_full = shared[6]
    hidden = hidden_in.astype(jnp.float32)
    scale1 = rms_scale(hidden)
    unit1 = hidden * scale1
    normed = (unit1 * gain_attn).astype(jnp.bfloat16)
    qkv_mixed = jnp.dot(normed, qkv_full, preferred_element_type=jnp.float32)
    query_raw = qkv_mixed[:, :model_width]
    key_raw = qkv_mixed[:, model_width : 2 * model_width]
    value_raw = qkv_mixed[:, 2 * model_width :]
    query_scale = rms_scale(query_raw)
    query_unit = query_raw * query_scale
    key_scale = rms_scale(key_raw)
    key_unit = key_raw * key_scale
    query_rot = rotate((query_unit * gain_query).reshape(shape3), cosine, sine, 1.0).astype(
        jnp.bfloat16
    )
    key_rot = rotate((key_unit * gain_key).reshape(shape3), cosine, sine, 1.0).astype(jnp.bfloat16)
    value_low = value_raw.astype(jnp.bfloat16)
    key_all, value_all = (
        lax.all_gather(key_rot.reshape(tokens_here, model_width), "fsdp", axis=0, tiled=True),
        lax.all_gather(value_low, "fsdp", axis=0, tiled=True),
    )
    key_all = key_all.reshape(seq_length, head_count, head_size)
    value_all = value_all.reshape(seq_length, head_count, head_size)
    scores = (
        jnp.einsum("qhd,khd->hqk", query_rot, key_all, preferred_element_type=jnp.float32) * scaling
    )
    masked = jnp.where(allowed, scores, -1e30)
    row_max = jnp.max(masked, axis=-1, keepdims=True)
    weights = jnp.where(allowed, jnp.exp(masked - row_max), 0.0)
    attn_probs = weights / jnp.sum(weights, axis=-1, keepdims=True)
    probs_low = attn_probs.astype(jnp.bfloat16)
    attended = jnp.einsum("hqk,khd->qhd", probs_low, value_all, preferred_element_type=jnp.float32)
    attended = attended.reshape(tokens_here, model_width).astype(jnp.bfloat16)
    branch = jnp.dot(attended, out_full, preferred_element_type=jnp.float32)
    middle = hidden + branch
    scale2 = rms_scale(middle)
    unit2 = middle * scale2
    normed2 = (unit2 * gain_ffn).astype(jnp.bfloat16)
    logits = jnp.dot(normed2, router_full, preferred_element_type=jnp.float32)
    router_probs = jax.nn.softmax(logits, axis=-1)
    choose_hot = (routes[:, :, None] == jnp.arange(experts, dtype=jnp.int32)[None, None, :]).astype(
        jnp.float32
    )
    gates = jnp.sum(choose_hot * router_probs[:, None, :], axis=-1)
    slot_place, slot_owner, filled = routing_tables(routes, experts, capacity)
    source_rows = slot_owner // topk
    routed_rows = jnp.where(
        filled[:, None] > 0, jnp.take(normed2, source_rows, axis=0), jnp.zeros((), jnp.bfloat16)
    )
    routed_rows = routed_rows.reshape(experts, capacity, model_width)
    inner_local, outer_local = fetch_local(expert_in, expert_out)
    result = expert_output(
        expert_activation(
            expert_gate_up(
                lax.all_to_all(routed_rows, "fsdp", split_axis=0, concat_axis=1, tiled=True),
                inner_local,
            )
        ),
        outer_local,
    )
    expert_results = send_home(result)
    flat_results = expert_results.reshape(experts * capacity, model_width)
    picked = jnp.take(flat_results, slot_place, axis=0).reshape(tokens_here, topk, model_width)
    expert_sum = jnp.sum(gates[:, :, None] * picked, axis=1)
    block_total = middle + expert_sum
    square_sums = lax.psum(
        (
            jnp.sum(live_mask[:, None] * block_total * block_total),
            jnp.sum(live_mask[:, None] * branch * branch),
            jnp.sum(live_mask[:, None] * expert_sum * expert_sum),
        ),
        ("dp", "fsdp"),
    )
    valid_cells = jnp.sum(lengths).astype(jnp.float32) * model_width
    stats = jnp.sqrt(jnp.stack([square_sums[0], square_sums[1], square_sums[2]]) / valid_cells)
    grad_total = cotangent.astype(jnp.float32) * live_mask[:, None]
    grad_gates = jnp.sum(picked * grad_total[:, None, :], axis=-1)
    gate_rows = jnp.take(gates.reshape(-1), slot_owner) * filled
    grad_blocks = (jnp.take(grad_total, source_rows, axis=0) * gate_rows[:, None]).astype(
        jnp.bfloat16
    )
    grad_blocks = grad_blocks.reshape(experts, capacity, model_width)
    inner_back, outer_back = fetch_local(expert_in, expert_out)
    rows_here, grads_here = (
        lax.all_to_all(routed_rows, "fsdp", split_axis=0, concat_axis=1, tiled=True),
        lax.all_to_all(grad_blocks, "fsdp", split_axis=0, concat_axis=1, tiled=True),
    )
    gate_up_here = expert_gate_up(rows_here, inner_back)
    grad_local, inner_total, outer_total = expert_backward(
        rows_here, gate_up_here, grads_here, inner_back, outer_back
    )
    grad_routed = send_home(grad_local)
    inner_owned, outer_owned = (
        lax.psum_scatter(
            inner_total.astype(jnp.bfloat16), "dp", scatter_dimension=0, tiled=True
        ).astype(jnp.float32),
        lax.psum_scatter(
            outer_total.astype(jnp.bfloat16), "dp", scatter_dimension=0, tiled=True
        ).astype(jnp.float32),
    )
    expert_in_grad, expert_out_grad = (
        lax.all_to_all(
            inner_owned.astype(jnp.bfloat16), "fsdp", split_axis=0, concat_axis=1, tiled=True
        ).astype(inner_owned.dtype),
        lax.all_to_all(
            outer_owned.astype(jnp.bfloat16), "fsdp", split_axis=0, concat_axis=1, tiled=True
        ).astype(outer_owned.dtype),
    )
    grad_normed2 = jnp.sum(
        jnp.take(grad_routed.reshape(experts * capacity, model_width), slot_place, axis=0).reshape(
            tokens_here, topk, model_width
        ),
        axis=1,
    )
    shared_back = fetch_shared(
        attn_gain, query_gain, key_gain, ffn_gain, router_weight, qkv_weight, out_weight
    )
    router_back = shared_back[4]
    qkv_back = shared_back[5]
    out_back = shared_back[6]
    grad_router_probs = jnp.sum(choose_hot * grad_gates[:, :, None], axis=1)
    grad_logits = router_probs * (
        grad_router_probs - jnp.sum(router_probs * grad_router_probs, axis=-1, keepdims=True)
    )
    grad_logits = grad_logits.astype(jnp.bfloat16)
    router_term = lax.dot_general(
        normed2, grad_logits, (((0,), (0,)), ((), ())), preferred_element_type=jnp.float32
    )
    grad_normed2 = grad_normed2 + lax.dot_general(
        grad_logits, router_back, (((1,), (1,)), ((), ())), preferred_element_type=jnp.float32
    )
    ffn_term = jnp.sum(grad_normed2 * unit2, axis=0)
    grad_middle = grad_total + norm_back(grad_normed2 * gain_ffn, unit2, scale2)
    out_term = lax.dot_general(
        attended, grad_middle, (((0,), (0,)), ((), ())), preferred_element_type=jnp.float32
    )
    grad_attended = lax.dot_general(
        grad_middle, out_back, (((1,), (1,)), ((), ())), preferred_element_type=jnp.float32
    )
    grad_attended = grad_attended.astype(jnp.bfloat16).reshape(shape3)
    grad_probs = jnp.einsum(
        "qhd,khd->hqk", grad_attended, value_all, preferred_element_type=jnp.float32
    )
    grad_scores = attn_probs * (
        grad_probs - jnp.sum(attn_probs * grad_probs, axis=-1, keepdims=True)
    )
    grad_scores = grad_scores.astype(jnp.bfloat16)
    grad_query_rot = (
        jnp.einsum("hqk,khd->qhd", grad_scores, key_all, preferred_element_type=jnp.float32)
        * scaling
    )
    grad_key_all = (
        jnp.einsum("hqk,qhd->khd", grad_scores, query_rot, preferred_element_type=jnp.float32)
        * scaling
    )
    grad_value_all = jnp.einsum(
        "hqk,qhd->khd", probs_low, grad_attended, preferred_element_type=jnp.float32
    )
    grad_key_rot, grad_value = (
        lax.psum_scatter(
            grad_key_all.reshape(seq_length, model_width).astype(jnp.bfloat16),
            "fsdp",
            scatter_dimension=0,
            tiled=True,
        ).astype(jnp.float32),
        lax.psum_scatter(
            grad_value_all.reshape(seq_length, model_width).astype(jnp.bfloat16),
            "fsdp",
            scatter_dimension=0,
            tiled=True,
        ).astype(jnp.float32),
    )
    grad_query_norm = rotate(grad_query_rot, cosine, sine, -1.0).reshape(tokens_here, model_width)
    grad_key_norm = rotate(grad_key_rot.reshape(shape3), cosine, sine, -1.0).reshape(
        tokens_here, model_width
    )
    query_term = jnp.sum(grad_query_norm * query_unit, axis=0)
    key_term = jnp.sum(grad_key_norm * key_unit, axis=0)
    grad_query_raw = norm_back(grad_query_norm * gain_query, query_unit, query_scale)
    grad_key_raw = norm_back(grad_key_norm * gain_key, key_unit, key_scale)
    grad_qkv = jnp.concatenate([grad_query_raw, grad_key_raw, grad_value], axis=1).astype(
        jnp.bfloat16
    )
    qkv_term = lax.dot_general(
        normed, grad_qkv, (((0,), (0,)), ((), ())), preferred_element_type=jnp.float32
    )
    grad_normed = lax.dot_general(
        grad_qkv, qkv_back, (((1,), (1,)), ((), ())), preferred_element_type=jnp.float32
    )
    attn_term = jnp.sum(grad_normed * unit1, axis=0)
    hidden_grad = grad_middle + norm_back(grad_normed * gain_attn, unit1, scale1)
    grad_parts = (
        lax.psum_scatter(attn_term, ("dp", "fsdp"), scatter_dimension=0, tiled=True),
        lax.psum_scatter(query_term, ("dp", "fsdp"), scatter_dimension=0, tiled=True),
        lax.psum_scatter(key_term, ("dp", "fsdp"), scatter_dimension=0, tiled=True),
        lax.psum_scatter(ffn_term, ("dp", "fsdp"), scatter_dimension=0, tiled=True),
        lax.psum_scatter(router_term, ("dp", "fsdp"), scatter_dimension=0, tiled=True),
        lax.psum_scatter(qkv_term, ("dp", "fsdp"), scatter_dimension=0, tiled=True),
        lax.psum_scatter(out_term, ("dp", "fsdp"), scatter_dimension=0, tiled=True),
    )
    return (
        block_total.astype(jnp.bfloat16),
        hidden_grad,
        grad_parts[0],
        grad_parts[1],
        grad_parts[2],
        grad_parts[3],
        grad_parts[5],
        grad_parts[6],
        grad_parts[4],
        expert_in_grad,
        expert_out_grad,
        stats,
    )


def solution(mesh):
    in_specs = (
        P(("dp", "fsdp"), None),
        P(),
        P(("dp", "fsdp"), None),
        P(("dp", "fsdp")),
        P(("dp", "fsdp")),
        P(("dp", "fsdp")),
        P(("dp", "fsdp")),
        P(("dp", "fsdp"), None),
        P(("dp", "fsdp"), None),
        P(("dp", "fsdp"), None),
        P(("dp", "fsdp"), None, None),
        P(("dp", "fsdp"), None, None),
        P(("dp", "fsdp"), None),
    )
    out_specs = (
        P(("dp", "fsdp"), None),
        P(("dp", "fsdp"), None),
        P(("dp", "fsdp")),
        P(("dp", "fsdp")),
        P(("dp", "fsdp")),
        P(("dp", "fsdp")),
        P(("dp", "fsdp"), None),
        P(("dp", "fsdp"), None),
        P(("dp", "fsdp"), None),
        P(("dp", "fsdp"), None, None),
        P(("dp", "fsdp"), None, None),
        P(),
    )
    return jax.shard_map(body, mesh=mesh, in_specs=in_specs, out_specs=out_specs, check_vma=False)
```

profile of v0, /device:TPU:0, one launch (start us, length us, event | category | flops | bytes accessed | tf_op | source)
XLA Modules:
  0.0 2528.5 jit_solution(14310785183448132992)
XLA Ops:
  11.4 43.4 %all-reduce.9 = (bf16[2048]{0:T(1024)(128)(2,1)S(1)}, bf16[2048]{0:T(1024)(128)(2,1)S(1)}, bf16[2048]{0:T(1024)(128)(2,1)S(1)}, bf16[2048]{0:T(1024)(128)(2,1)S(1)}) all-reduce(bf16[2048]{0:T(1024)(128)(2,1)S(1)} %dynamic-update-slice, bf16[2048]{0:T(1024)(128)(2,1)S(1)} %dynamic-update-slice.2, ...), channel_id=1, replica_groups=mesh['dp'=4,'fsdp'=8] {'dp','fsdp'}, use_global_device_ids=true, to_apply=%add | all-reduce | flops 8192 | bytes 32768
  57.0 112.7 %all-gather.8.cloned.1.call-done = bf16[2048,6144]{1,0:T(8,128)(2,1)} async-done(((bf16[64,6144]{1,0:T(8,128)(2,1)}), bf16[2048,6144]{1,0:T(8,128)(2,1)}) %all-gather.8.cloned.1.call-update) | async-done | bytes 25165840 | tf_op jit(solution)/shard_map/all_gather | solution.py:42
  169.7 10.2 fusion.44
  193.6 65.2 %all_to_all.123 = bf16[64,16,2048]{2,0,1:T(8,128)(2,1)S(1)} all-to-all(bf16[64,16,2048]{2,0,1:T(8,128)(2,1)S(1)} %copy.185), channel_id=1, replica_groups=mesh['dp'=4,'fsdp'=8] {'fsdp'}, dimensions={1} | all-to-all | bytes 8388608 | tf_op jit(solution)/shard_map/all_to_all | solution.py:49
  277.3 24.9 all-to-all-done.2
  326.4 64.2 %all-gather.14.cloned.1.call-done = bf16[2048,2048]{1,0:T(8,128)(2,1)} async-done(((bf16[64,2048]{1,0:T(8,128)(2,1)}), bf16[2048,2048]{1,0:T(8,128)(2,1)}) %all-gather.14.cloned.1.call-update) | async-done | bytes 8388624 | tf_op jit(solution)/shard_map/all_gather | solution.py:43
  406.9 63.5 %all_to_all.124 = bf16[16,80,2048]{2,1,0:T(8,128)(2,1)S(1)} all-to-all(bf16[16,80,2048]{2,1,0:T(8,128)(2,1)S(1)} %select_select_fusion), channel_id=1, replica_groups=mesh['dp'=4,'fsdp'=8] {'fsdp'}, dimensions={0} | all-to-all | bytes 10485760 | tf_op jit(solution)/shard_map/all_to_all | solution.py:211
  473.4 204.6 %all-gather.16.cloned.1.call-done = bf16[2048,2,2048]{2,0,1:T(8,128)(2,1)} async-done(((bf16[512,2,2048]{2,0,1:T(8,128)(2,1)}), bf16[2048,2,2048]{2,0,1:T(8,128)(2,1)}) %all-gather.16.cloned.1.call-update) | async-done | bytes 16777232 | tf_op jit(solution)/shard_map/all_gather | solution.py:53
  678.0 15.4 fusion.70
  699.0 128.3 %all-gather.18.cloned.1.call-done = bf16[1024,2,2048]{2,0,1:T(8,128)(2,1)} async-done(((bf16[256,2,2048]{2,0,1:T(8,128)(2,1)}), bf16[1024,2,2048]{2,0,1:T(8,128)(2,1)}) %all-gather.18.cloned.1.call-update) | async-done | bytes 8388624 | tf_op jit(solution)/shard_map/all_gather | solution.py:54
  827.3 10.9 convolution_convert_fusion.1
  838.2 10.2 copy.189
  853.2 89.9 %all-gather = bf16[32,64,16]{1,2,0:T(8,128)(2,1)S(1)} all-gather(bf16[1,64,16]{1,2,0:T(8,128)(2,1)S(1)} %bitcast.209), channel_id=1, replica_groups=mesh['dp'=4,'fsdp'=8] {'dp','fsdp'}, dimensions={0}, use_global_device_ids=true | all-gather | bytes 67584 | tf_op jit(solution)/shard_map/all_gather | solution.py:41
  960.8 13.1 gather_fusion.3
  988.5 63.3 %all_to_all.125 = bf16[16,80,2048]{2,1,0:T(8,128)(2,1)S(1)} all-to-all(bf16[16,80,2048]{2,1,0:T(8,128)(2,1)S(1)} %multiply_convert_fusion), channel_id=1, replica_groups=mesh['dp'=4,'fsdp'=8] {'fsdp'}, dimensions={0} | all-to-all | bytes 10485760 | tf_op jit(solution)/shard_map/all_to_all | solution.py:242
  1055.9 13.4 multiply_convert_fusion.4
  1069.3 17.4 convolution_convert_fusion
  1101.7 60.3 %all-to-all-done.5 = bf16[2,640,2048]{2,0,1:T(2,128)(2,1)} async-done(((bf16[2,640,2048]{2,0,1:T(2,128)(2,1)}), bf16[2,640,2048]{2,0,1:T(2,128)(2,1)}, u32[]{:S(2)}, u32[]{:S(2)}) %all-to-all-start.5) | async-done | bytes 5242912 | tf_op jit(solution)/shard_map/all_to_all | solution.py:59
  1171.0 13.1 gather_fusion.4
  1184.1 10.3 bitcast_reduce_fusion
  1239.7 11.5 convert_bitcast_fusion.2
  1252.9 19.5 convert_bitcast_fusion
  1301.7 26.8 %reduce-scatter.12.cloned.1.call-done = bf16[128,2048]{1,0:T(8,128)(2,1)} async-done(((bf16[1024,2048]{1,0:T(8,128)(2,1)}), bf16[128,2048]{1,0:T(8,128)(2,1)}) %reduce-scatter.12.cloned.1.call-update) | async-done | bytes 524304 | tf_op jit(solution)/shard_map/reduce_scatter | solution.py:322
  1328.5 21.7 fusion.38
  1350.3 125.7 %reduce-scatter.20.cloned.1.call-done = bf16[256,2,2048]{0,2,1:T(8,128)(2,1)} async-done(((bf16[1024,2,2048]{0,2,1:T(8,128)(2,1)}), bf16[256,2,2048]{0,2,1:T(8,128)(2,1)}) %reduce-scatter.20.cloned.1.call-update) | async-done | bytes 2097168 | tf_op jit(solution)/shard_map/reduce_scatter | solution.py:253
  1486.5 272.7 %reduce-scatter.18.cloned.1.call-done = bf16[512,2,2048]{0,2,1:T(8,128)(2,1)} async-done(((bf16[2048,2,2048]{0,2,1:T(8,128)(2,1)}), bf16[512,2,2048]{0,2,1:T(8,128)(2,1)}) %reduce-scatter.18.cloned.1.call-update) | async-done | bytes 4194320 | tf_op jit(solution)/shard_map/reduce_scatter | solution.py:250
  1759.2 11.3 copy.207
  1776.6 121.8 %reduce-scatter.24.cloned.1.call-done = f32[64,16]{1,0:T(8,128)} async-done(((f32[2048,16]{1,0:T(8,128)}), f32[64,16]{1,0:T(8,128)}) %reduce-scatter.24.cloned.1.call-update) | async-done | bytes 4112
  1899.8 15.1 fusion.31
  1914.9 42.3 %all-reduce.8 = (f32[2048]{0:T(1024)S(1)}, f32[2048]{0:T(1024)S(1)}, f32[2048]{0:T(1024)S(1)}, f32[2048]{0:T(1024)S(1)}, f32[1]{0:T(128)}, /*index=5*/f32[1]{0:T(128)}, f32[1]{0:T(128)}) all-reduce(f32[2048]{0:T(1024)S(1)} %get-tuple-element.59, ...), channel_id=4, replica_groups=mesh['dp'=4,'fsdp'=8] {'dp','fsdp'}, use_global_device_ids=true, to_apply=%region_27.29.clone | all-reduce | flops 8195 | bytes 65560
  1987.1 94.3 %reduce-scatter.16.cloned.1.call-done = f32[64,2048]{1,0:T(8,128)} async-done(((f32[2048,2048]{1,0:T(8,128)}), f32[64,2048]{1,0:T(8,128)}) %reduce-scatter.16.cloned.1.call-update) | async-done | bytes 524304 | tf_op jit(solution)/shard_map/reduce_scatter | solution.py:355
  2081.3 440.3 %reduce-scatter.14.cloned.1.call-done = f32[64,6144]{1,0:T(8,128)} async-done(((f32[2048,6144]{1,0:T(8,128)}), f32[64,6144]{1,0:T(8,128)}) %reduce-scatter.14.cloned.1.call-update) | async-done | bytes 1572880 | tf_op jit(solution)/shard_map/reduce_scatter | solution.py:354
  (294 shorter events, 275.4 us)
Async XLA Ops:
  7.2 162.5 %all-gather.8.cloned.1.call-start = ((), (), s32[]{:S(2)}) async-start(), calls=%async_computation.15 | async-start | bytes 25952256 | tf_op jit(solution)/shard_map/all_gather | solution.py:42
  7.9 301.8 %all-gather.12.cloned.1.call-start = ((), (), s32[]{:S(2)}) async-start(), calls=%async_computation.17 | async-start | bytes 4718592 | tf_op jit(solution)/shard_map/all_gather | solution.py:175
  54.8 125.2 %copy-start.29 = (f32[2048]{0:T(1024)}, f32[2048]{0:T(1024)S(1)}, u32[]{:S(2)}) copy-start(f32[2048]{0:T(1024)S(1)} %convert_element_type.181) | copy-start | bytes 24580
  54.8 125.5 %copy-start.34 = (f32[2048]{0:T(1024)}, f32[2048]{0:T(1024)S(1)}, u32[]{:S(2)}) copy-start(f32[2048]{0:T(1024)S(1)} %convert_element_type.183) | copy-start | bytes 24580
  54.8 125.5 %copy-start.36 = (f32[2048]{0:T(1024)}, f32[2048]{0:T(1024)S(1)}, u32[]{:S(2)}) copy-start(f32[2048]{0:T(1024)S(1)} %convert_element_type.185) | copy-start | bytes 24580
  56.1 123.9 %copy-start.40 = (f32[128]{0:T(128)}, f32[128]{0:T(128)S(1)}, u32[]{:S(2)}) copy-start(f32[128]{0:T(128)S(1)} %add_rsqrt_fusion.3) | copy-start | bytes 1540
  57.0 125.0 %copy-start.26 = (f32[128,64]{1,0:T(8,128)}, f32[128,64]{1,0:T(8,128)S(1)}, u32[]{:S(2)}) copy-start(f32[128,64]{1,0:T(8,128)S(1)} %get-tuple-element.112) | copy-start | bytes 98308
  187.5 132.0 %all-gather.10.cloned.1.call-start = ((), (), s32[]{:S(2)}) async-start(), calls=%async_computation.16 | async-start | bytes 4718592 | tf_op jit(solution)/shard_map/all_gather | solution.py:176
  188.5 202.1 %all-gather.14.cloned.1.call-start = ((), (), s32[]{:S(2)}) async-start(), calls=%async_computation.18 | async-start | bytes 8650752 | tf_op jit(solution)/shard_map/all_gather | solution.py:43
  189.1 488.9 %all-gather.16.cloned.1.call-start = ((), (), s32[]{:S(2)}) async-start(), calls=%async_computation.19 | async-start | bytes 20971520 | tf_op jit(solution)/shard_map/all_gather | solution.py:53
  263.6 38.6 %all-to-all-start.2 = ((bf16[32,16,2048]{2,0,1:T(8,128)(2,1)}), bf16[32,16,2048]{2,0,1:T(8,128)(2,1)S(1)}, u32[]{:S(2)}, u32[]{:S(2)}) async-start(bf16[32,16,2048]{2,0,1:T(8,128)(2,1)} %copy.187), calls=%async_computation.2 | async-start | bytes 4194304 | tf_op jit(solution)/shard_map/all_to_all | solution.py:50
  267.4 559.9 %all-gather.18.cloned.1.call-start = ((), (), s32[]{:S(2)}) async-start(), calls=%async_computation.20 | async-start | bytes 10485760 | tf_op jit(solution)/shard_map/all_gather | solution.py:54
  267.7 128.5 %copy-start.32 = (f32[2048]{0:T(1024)}, f32[2048]{0:T(1024)S(1)}, u32[]{:S(2)}) copy-start(f32[2048]{0:T(1024)S(1)} %convert_element_type.191) | copy-start | bytes 24580
  319.5 71.1 %copy-start.12 = (bf16[128,2048]{1,0:T(8,128)(2,1)S(1)}, bf16[128,2048]{1,0:T(8,128)(2,1)}, u32[]{:S(2)}) copy-start(bf16[128,2048]{1,0:T(8,128)(2,1)} %param.15) | copy-start | bytes 1572868
  397.4 554.1 %copy-start = (bf16[128,2048]{1,0:T(8,128)(2,1)}, bf16[128,2048]{1,0:T(8,128)(2,1)S(1)}, u32[]{:S(2)}) copy-start(bf16[128,2048]{1,0:T(8,128)(2,1)S(1)} %multiply_convert_fusion.8) | copy-start | bytes 1572868
  699.0 139.2 %copy-start.5 = (bf16[2,640,1024]{2,1,0:T(8,128)(2,1)}, bf16[2,640,1024]{2,1,0:T(8,128)(2,1)S(1)}, u32[]{:S(2)}) copy-start(bf16[2,640,1024]{2,1,0:T(8,128)(2,1)S(1)} %multiply_convert_fusion.5) | copy-start | bytes 7864324
  848.3 95.6 %copy-start.25 = (bf16[128,2048]{1,0:T(8,128)(2,1)S(1)}, bf16[128,2048]{1,0:T(8,128)(2,1)}, u32[]{:S(2)}) copy-start(bf16[128,2048]{1,0:T(8,128)(2,1)} %param.27) | copy-start | bytes 1572868
  848.4 103.5 %all-to-all-start.3 = ((bf16[2,640,2048]{2,0,1:T(2,128)(2,1)}), bf16[2,640,2048]{2,0,1:T(2,128)(2,1)}, u32[]{:S(2)}, u32[]{:S(2)}) async-start(bf16[2,640,2048]{2,0,1:T(2,128)(2,1)} %copy.189), calls=%async_computation.3 | async-start | bytes 10485760 | tf_op jit(solution)/shard_map/all_to_all | solution.py:59
  1097.0 65.0 %all-to-all-start.5 = ((bf16[2,640,2048]{2,0,1:T(2,128)(2,1)}), bf16[2,640,2048]{2,0,1:T(2,128)(2,1)}, u32[]{:S(2)}, u32[]{:S(2)}) async-start(bf16[2,640,2048]{2,0,1:T(2,128)(2,1)} %copy.193), calls=%async_computation.5 | async-start | bytes 10485760 | tf_op jit(solution)/shard_map/all_to_all | solution.py:59
  1101.6 188.2 %reduce-scatter.22.cloned.1.call-start = ((), (), s32[]{:S(2)}) async-start(), calls=%async_computation.26 | async-start | bytes 4718592
  1225.6 102.9 %reduce-scatter.12.cloned.1.call-start = ((), (), s32[]{:S(2)}) async-start(), calls=%async_computation.21 | async-start | bytes 4718592 | tf_op jit(solution)/shard_map/reduce_scatter | solution.py:322
  1239.6 236.4 %reduce-scatter.20.cloned.1.call-start = ((), (), s32[]{:S(2)}) async-start(), calls=%async_computation.25 | async-start | bytes 10485760 | tf_op jit(solution)/shard_map/reduce_scatter | solution.py:253
  1251.2 508.1 %reduce-scatter.18.cloned.1.call-start = ((), (), s32[]{:S(2)}) async-start(), calls=%async_computation.24 | async-start | bytes 20971520 | tf_op jit(solution)/shard_map/reduce_scatter | solution.py:250
  1272.4 626.0 %reduce-scatter.24.cloned.1.call-start = ((), (), s32[]{:S(2)}) async-start(), calls=%async_computation.27 | async-start | bytes 1081344
  1274.7 806.6 %reduce-scatter.16.cloned.1.call-start = ((), (), s32[]{:S(2)}) async-start(), calls=%async_computation.23 | async-start | bytes 17301504 | tf_op jit(solution)/shard_map/reduce_scatter | solution.py:355
  1283.0 1238.5 %reduce-scatter.14.cloned.1.call-start = ((), (), s32[]{:S(2)}) async-start(), calls=%async_computation.22 | async-start | bytes 51904512 | tf_op jit(solution)/shard_map/reduce_scatter | solution.py:354
  1482.1 288.4 %all-to-all-start.7 = ((bf16[256,2,2048]{2,1,0:T(2,128)(2,1)}), bf16[256,2,2048]{2,1,0:T(2,128)(2,1)}, u32[]{:S(2)}, u32[]{:S(2)}) async-start(bf16[256,2,2048]{2,1,0:T(2,128)(2,1)} %copy.211), calls=%async_computation.12 | async-start | bytes 4194304 | tf_op jit(solution)/shard_map/all_to_all | solution.py:261
  1770.5 129.3 %copy-start.13 = (bf16[128,2048]{1,0:T(8,128)(2,1)S(1)}, bf16[128,2048]{1,0:T(8,128)(2,1)}, u32[]{:S(2)}) copy-start(bf16[128,2048]{1,0:T(8,128)(2,1)} %param.15) | copy-start | bytes 1572868
  1770.5 129.3 %copy-start.18 = (bf16[128,2048]{1,0:T(8,128)(2,1)S(1)}, bf16[128,2048]{1,0:T(8,128)(2,1)}, u32[]{:S(2)}) copy-start(bf16[128,2048]{1,0:T(8,128)(2,1)} %get-tuple-element.87) | copy-start | bytes 1572868
  1770.5 129.3 %copy-start.19 = (bf16[128,2048]{1,0:T(8,128)(2,1)S(1)}, bf16[128,2048]{1,0:T(8,128)(2,1)}, u32[]{:S(2)}) copy-start(bf16[128,2048]{1,0:T(8,128)(2,1)} %get-tuple-element.88) | copy-start | bytes 1572868
  1770.5 129.3 %copy-start.28 = (bf16[128,2048]{1,0:T(8,128)(2,1)S(1)}, bf16[128,2048]{1,0:T(8,128)(2,1)}, u32[]{:S(2)}) copy-start(bf16[128,2048]{1,0:T(8,128)(2,1)} %reduce-scatter.12.cloned.1.call-done) | copy-start | bytes 1572868
  1770.5 202.0 %all-to-all-start.6 = ((bf16[512,2,2048]{2,1,0:T(2,128)(2,1)}), bf16[512,2,2048]{2,1,0:T(2,128)(2,1)}, u32[]{:S(2)}, u32[]{:S(2)}) async-start(bf16[512,2,2048]{2,1,0:T(2,128)(2,1)} %copy.207), calls=%async_computation.10 | async-start | bytes 8388608 | tf_op jit(solution)/shard_map/all_to_all | solution.py:258
  (44 other events, 585.1 us)
Sparse Core Ops, SparseCore 0:
  10.9 158.7 all-gather.7
  187.6 68.5 all-gather.11
  258.7 52.2 all-gather.9
  313.8 76.7 all-gather.13
  392.6 285.3 all-gather.15
  679.4 147.8 all-gather.17
  1225.7 47.6 reduce-scatter.21
  1277.2 51.3 reduce-scatter.11
  1331.4 144.4 reduce-scatter.19
  1478.2 281.0 reduce-scatter.17
  1761.6 136.7 reduce-scatter.23
  1901.1 180.2 reduce-scatter.15
  2088.3 433.2 reduce-scatter.13
where the time goes:
time: 2540 us; the launch traced here: 2530 us
  waiting for transfers between devices  1680 us (66%)
  blocking collectives  368 us (14%)
  matrix products  200 us (8%)
  local copies, waits for them, and re-layouts  192 us (8%)
  other arithmetic  51.9 us (2%)
    reduce_scatter x1, waiting for transfers between devices, body(): lax.psum_scatter(qkv_term, ('dp', 'fsdp'), scatter_dimension=0, tiled=True)  440 us
    reduce_scatter x1, waiting for transfers between devices, body(): lax.psum_scatter(inner_total.astype(jnp.bfloat16), 'dp', scatter_dimensio...  273 us
    all_gather x1, waiting for transfers between devices, fetch_local(): lax.all_gather(exchanged[0], 'dp', axis=0, tiled=True)  205 us
    all_gather x1, waiting for transfers between devices, fetch_local(): lax.all_gather(exchanged[1], 'dp', axis=0, tiled=True)  128 us
    reduce_scatter x1, waiting for transfers between devices, body(): lax.psum_scatter(outer_total.astype(jnp.bfloat16), 'dp', scatter_dimensio...  126 us
    unnamed x15, waiting for transfers between devices  123 us
    all_gather x1, waiting for transfers between devices, fetch_shared(): lax.all_gather(qkv_weight, ('dp', 'fsdp'), axis=0, tiled=True)  113 us
    reduce_scatter x1, waiting for transfers between devices, body(): lax.psum_scatter(out_term, ('dp', 'fsdp'), scatter_dimension=0, tiled=True)  94.3 us
  transfers between devices with their start and end apart: 18, of which 12 were waited for; matrix products, arithmetic and copies ran while one was open for 10% of the time, Pallas kernels for 0%

commit v1 on v0

v1 whole, which is shorter than its diff:
```python
import functools

import jax
import jax.numpy as jnp
from jax import lax
from jax.experimental import pallas as pl
from jax.experimental.pallas import tpu as pltpu
from jax.sharding import PartitionSpec as P

HEADS = 16
HEAD_DIM = 128
EPS = 1e-05
BOTH = ("dp", "fsdp")
MESH_ID = pl.DeviceIdType.MESH
F32 = jnp.float32
BF16 = jnp.bfloat16


def rms_scale(values_in):
    return lax.rsqrt(jnp.mean(values_in * values_in, axis=-1, keepdims=True) + EPS)


def norm_back(grad_in, unit_rows, scaling):
    return scaling * (grad_in - unit_rows * jnp.mean(grad_in * unit_rows, axis=-1, keepdims=True))


def rotate(values_in, cosine, sine, direction):
    half_width = values_in.shape[-1] // 2
    first_half = values_in[..., :half_width]
    second_half = values_in[..., half_width:]
    return jnp.concatenate(
        [
            first_half * cosine - direction * second_half * sine,
            second_half * cosine + direction * first_half * sine,
        ],
        axis=-1,
    )


def place(axes, fsdp, index):
    if axes == BOTH:
        return {"dp": index // fsdp, "fsdp": lax.rem(index, fsdp)}
    return {axes[0]: index}


def exchange_kernel(axes, n, fsdp, spread, x, o, send, recv, own):
    if axes == BOTH:
        me = lax.axis_index("dp") * fsdp + lax.axis_index("fsdp")
    else:
        me = lax.axis_index(axes[0])
    barrier = pltpu.get_barrier_semaphore()
    for k in range(1, n):
        peer = place(axes, fsdp, lax.rem(me + k, n))
        pl.semaphore_signal(barrier, inc=1, device_id=peer, device_id_type=MESH_ID)
    pl.semaphore_wait(barrier, n - 1)
    local = pltpu.make_async_copy(x.at[me] if spread else x, o.at[me], own)
    local.start()
    copies = []
    for k in range(1, n):
        target = lax.rem(me + k, n)
        copy = pltpu.make_async_remote_copy(
            x.at[target] if spread else x,
            o.at[me],
            send.at[k],
            recv.at[k],
            device_id=place(axes, fsdp, target),
            device_id_type=MESH_ID,
        )
        copy.start()
        copies.append(copy)
    local.wait()
    for copy in copies:
        copy.wait()


def exchange(x, axes, ident, spread):
    fsdp = lax.axis_size("fsdp")
    n = lax.axis_size(axes)
    shape = x.shape if spread else (n,) + x.shape
    return pl.pallas_call(
        functools.partial(exchange_kernel, axes, n, fsdp, spread),
        out_shape=jax.ShapeDtypeStruct(shape, x.dtype),
        in_specs=[pl.BlockSpec(memory_space=pl.ANY)],
        out_specs=pl.BlockSpec(memory_space=pl.ANY),
        scratch_shapes=[
            pltpu.SemaphoreType.DMA((n,)),
            pltpu.SemaphoreType.DMA((n,)),
            pltpu.SemaphoreType.DMA,
        ],
        compiler_params=pltpu.CompilerParams(collective_id=ident, has_side_effects=True),
    )(x)


def tiles_of(x, rows):
    flat = x.reshape(-1)
    return jnp.pad(flat, (0, rows * 128 - flat.shape[0])).reshape(rows, 128)


def plane_sum(x, ident):
    rows = -(-x.size // 1024) * 8
    got = exchange(tiles_of(x, rows), ("fsdp",), ident, False)
    return jnp.sum(got, axis=0).reshape(-1)[: x.size].reshape(x.shape)


def dot(a, b, dims):
    return lax.dot_general(a, b, (dims, ((), ())), preferred_element_type=F32)


def body(
    hidden_in,
    lengths,
    routes,
    attn_gain,
    query_gain,
    key_gain,
    ffn_gain,
    qkv_weight,
    out_weight,
    router_weight,
    expert_in,
    expert_out,
    cotangent,
):
    rows, width = hidden_in.shape
    dp = lax.axis_size("dp")
    fsdp = lax.axis_size("fsdp")
    n = dp * fsdp
    experts = router_weight.shape[1]
    seq = rows * fsdp
    tokens = rows * n
    own_rows = width // n
    heads_here = HEADS // fsdp
    cols = heads_here * HEAD_DIM
    experts_here = experts // fsdp
    ff = expert_out.shape[0] * n
    ff_here = ff // dp
    inner = experts_here * ff_here
    z = lax.axis_index("dp")
    f = lax.axis_index("fsdp")
    valid = lengths[z]
    scaling = HEAD_DIM ** (-0.5)

    small = jnp.concatenate(
        [attn_gain, query_gain, key_gain, ffn_gain, router_weight.reshape(-1)]
    )
    small_rows = -(-small.size // 2048) * 16
    small = exchange(tiles_of(small, small_rows), BOTH, 0, False).reshape(n, -1)
    gains = small[:, : 4 * own_rows].reshape(n, 4, own_rows).transpose(1, 0, 2)
    gains = gains.reshape(4, width).astype(F32)
    router_full = small[:, 4 * own_rows : 4 * own_rows + own_rows * experts]
    router_full = router_full.reshape(width, experts)
    gain_attn, gain_query, gain_key, gain_ffn = gains[0], gains[1], gains[2], gains[3]

    attn_weight = jnp.concatenate(
        [
            qkv_weight.reshape(own_rows, 3, fsdp, cols),
            out_weight.reshape(own_rows, 1, fsdp, cols),
        ],
        axis=1,
    )
    attn_weight = attn_weight.transpose(2, 0, 1, 3).reshape(fsdp, own_rows, 4 * cols)
    attn_weight = lax.all_to_all(attn_weight, "fsdp", 0, 0, tiled=True)
    attn_weight = lax.all_gather(
        attn_weight.reshape(fsdp * own_rows, 4 * cols), "dp", axis=0, tiled=True
    )
    qkv_here = attn_weight[:, : 3 * cols]
    out_here = attn_weight[:, 3 * cols :]

    inner_weight = expert_in.reshape(own_rows, fsdp, experts_here, 2, dp, ff_here)
    inner_weight = inner_weight.transpose(4, 1, 0, 3, 2, 5).reshape(n, own_rows, 2 * inner)
    inner_weight = lax.all_to_all(inner_weight, BOTH, 0, 0, tiled=True).reshape(width, 2 * inner)
    outer_weight = expert_out.reshape(-1, fsdp, experts_here, width).transpose(1, 2, 0, 3)
    outer_weight = lax.all_to_all(outer_weight, "fsdp", 0, 0, tiled=True)
    outer_weight = outer_weight.transpose(1, 0, 2, 3).reshape(inner, width)

    hidden_all = lax.all_gather(hidden_in, "fsdp", axis=0, tiled=True).astype(F32)
    normed_all = (hidden_all * rms_scale(hidden_all) * gain_attn).astype(BF16)
    mixed = dot(normed_all, qkv_here, ((1,), (0,)))
    raw = mixed[:, : 2 * cols].reshape(seq, 2, cols)
    squares = plane_sum(jnp.sum(raw * raw, axis=-1), 1)
    qk_scale = lax.rsqrt(squares / width + EPS)[:, :, None]
    qk_unit = raw * qk_scale
    here = f * cols
    qk_gain = jnp.stack(
        [
            lax.dynamic_slice(gain_query, (here,), (cols,)),
            lax.dynamic_slice(gain_key, (here,), (cols,)),
        ]
    )
    pos = jnp.arange(seq, dtype=jnp.int32)
    frequency = jnp.power(10000.0, -jnp.arange(HEAD_DIM // 2, dtype=F32) * 2.0 / HEAD_DIM)
    angles = pos.astype(F32)[:, None] * frequency[None, :]
    cosine = jnp.cos(angles)[:, None, None, :]
    sine = jnp.sin(angles)[:, None, None, :]
    shape4 = (seq, 2, heads_here, HEAD_DIM)
    turned = rotate((qk_unit * qk_gain).reshape(shape4), cosine, sine, 1.0).astype(BF16)
    query = turned[:, 0]
    key = turned[:, 1]
    value = mixed[:, 2 * cols :].astype(BF16).reshape(seq, heads_here, HEAD_DIM)
    allowed = ((pos[None, :] <= pos[:, None]) & (pos[None, :] < valid))[None]
    scores = jnp.einsum("qhd,khd->hqk", query, key, preferred_element_type=F32) * scaling
    masked = jnp.where(allowed, scores, -1e30)
    weights = jnp.where(allowed, jnp.exp(masked - jnp.max(masked, axis=-1, keepdims=True)), 0.0)
    probs = weights / jnp.sum(weights, axis=-1, keepdims=True)
    probs_low = probs.astype(BF16)
    attended = jnp.einsum("hqk,khd->qhd", probs_low, value, preferred_element_type=F32)
    attended = attended.reshape(seq, cols).astype(BF16)
    attended_all = lax.all_gather(attended, "fsdp", axis=0, tiled=False)
    branch = jnp.einsum(
        "fsc,fcn->sn", attended_all, out_here.reshape(fsdp, cols, cols), preferred_element_type=F32
    )
    branch = exchange(branch.astype(BF16).reshape(fsdp, rows, cols), ("fsdp",), 2, True)
    branch = branch.transpose(1, 0, 2).reshape(rows, width).astype(F32)

    hidden = hidden_in.astype(F32)
    scale1 = rms_scale(hidden)
    unit1 = hidden * scale1
    middle = hidden + branch
    scale2 = rms_scale(middle)
    unit2 = middle * scale2
    normed2 = (unit2 * gain_ffn).astype(BF16)
    logits = dot(normed2, router_full, ((1,), (0,)))
    router_probs = jax.nn.softmax(logits, axis=-1)
    chosen = jnp.sum(
        (routes[:, :, None] == jnp.arange(experts, dtype=jnp.int32)[None, None, :]).astype(F32),
        axis=1,
    )
    live_mask = (f * rows + jnp.arange(rows, dtype=jnp.int32) < valid).astype(F32)[:, None]
    grad_total = cotangent.astype(F32) * live_mask

    grad_all = lax.all_gather(grad_total.astype(BF16), BOTH, axis=0, tiled=True)
    rows_all = lax.all_gather(normed2, BOTH, axis=0, tiled=True)
    gates = (router_probs * chosen).reshape(rows, fsdp, experts_here).transpose(1, 2, 0)
    gates = jnp.broadcast_to(gates[None], (dp, fsdp, experts_here, rows))
    gates = gates.reshape(n, experts_here, rows)
    gates = jnp.pad(gates, ((0, 0), (0, 8 - experts_here), (0, 0)))
    gates = exchange(gates, BOTH, 3, True)[:, :experts_here]
    gates = gates.transpose(0, 2, 1).reshape(tokens, experts_here, 1)
    gate_up = dot(rows_all, inner_weight, ((1,), (0,)))
    gate = gate_up[:, :inner]
    up = gate_up[:, inner:]
    sigmoid = jax.nn.sigmoid(gate)
    silu = gate * sigmoid
    activation = (silu * up).astype(BF16).astype(F32)
    grad_act = dot(grad_all, outer_weight, ((1,), (1,)))
    grad_gates = jnp.sum(
        (activation * grad_act).reshape(tokens, experts_here, ff_here), axis=-1
    )
    by_part = (tokens, experts_here, ff_here)
    activation = (activation.reshape(by_part) * gates).reshape(tokens, inner).astype(BF16)
    grad_act = (grad_act.reshape(by_part) * gates).reshape(tokens, inner)
    grad_gate_up = jnp.concatenate(
        [grad_act * up * sigmoid * (1.0 + gate * (1.0 - sigmoid)), grad_act * silu], axis=1
    ).astype(BF16)
    expert_sum = dot(activation, outer_weight, ((1,), (0,))).astype(BF16)
    expert_sum = lax.psum_scatter(expert_sum, BOTH, scatter_dimension=0, tiled=True).astype(F32)
    if tokens > 8192:
        grad_gate_up, expert_sum = lax.optimization_barrier((grad_gate_up, expert_sum))
    grad_rows = dot(grad_gate_up, inner_weight, ((1,), (1,))).astype(BF16)
    grad_rows = lax.psum_scatter(grad_rows, BOTH, scatter_dimension=0, tiled=True).astype(F32)
    inner_grad = dot(rows_all, grad_gate_up, ((0,), (0,))).astype(BF16)
    outer_grad = dot(activation, grad_all, ((0,), (0,))).astype(BF16)
    grad_gates = grad_gates.reshape(n, rows, experts_here).transpose(0, 2, 1)
    grad_gates = jnp.pad(grad_gates, ((0, 0), (0, 8 - experts_here), (0, 0)))
    grad_gates = exchange(grad_gates, BOTH, 4, True)[:, :experts_here]
    grad_gates = jnp.sum(grad_gates.reshape(dp, fsdp, experts_here, rows), axis=0)
    grad_router_probs = grad_gates.reshape(experts, rows).transpose(1, 0) * chosen

    inner_grad = lax.all_to_all(inner_grad.reshape(n, own_rows, 2 * inner), BOTH, 0, 0, tiled=True)
    inner_grad = inner_grad.reshape(dp, fsdp, own_rows, 2, experts_here, ff_here)
    inner_grad = inner_grad.transpose(2, 1, 4, 3, 0, 5).reshape(own_rows, experts, 2 * ff)
    outer_grad = outer_grad.reshape(experts_here, fsdp, -1, width).transpose(1, 0, 2, 3)
    outer_grad = lax.all_to_all(outer_grad, "fsdp", 0, 0, tiled=True)
    outer_grad = outer_grad.transpose(2, 0, 1, 3).reshape(-1, experts, width)

    block_total = middle + expert_sum
    squares = jnp.stack(
        [
            jnp.sum(live_mask * block_total * block_total),
            jnp.sum(live_mask * branch * branch),
            jnp.sum(live_mask * expert_sum * expert_sum),
        ]
    )

    grad_logits = router_probs * (
        grad_router_probs - jnp.sum(router_probs * grad_router_probs, axis=-1, keepdims=True)
    )
    grad_logits = grad_logits.astype(BF16)
    router_term = dot(normed2, grad_logits, ((0,), (0,)))
    grad_normed2 = grad_rows + dot(grad_logits, router_full, ((1,), (1,)))
    ffn_term = jnp.sum(grad_normed2 * unit2, axis=0)
    grad_middle = grad_total + norm_back(grad_normed2 * gain_ffn, unit2, scale2)

    grad_cols = grad_middle.astype(BF16).reshape(rows, fsdp, cols).transpose(1, 0, 2)
    grad_cols = exchange(grad_cols, ("fsdp",), 5, True).reshape(seq, cols)
    out_grad = jnp.einsum("fsc,sn->fcn", attended_all, grad_cols, preferred_element_type=F32)
    grad_attended = jnp.einsum(
        "sn,fcn->fsc", grad_cols, out_here.reshape(fsdp, cols, cols), preferred_element_type=F32
    )
    grad_attended = lax.psum_scatter(
        grad_attended.astype(BF16).reshape(fsdp * seq, cols), "fsdp", scatter_dimension=0, tiled=True
    )
    grad_attended = grad_attended.reshape(seq, heads_here, HEAD_DIM)
    grad_probs = jnp.einsum("qhd,khd->hqk", grad_attended, value, preferred_element_type=F32)
    grad_scores = probs * (grad_probs - jnp.sum(probs * grad_probs, axis=-1, keepdims=True))
    grad_scores = grad_scores.astype(BF16)
    grad_query = jnp.einsum("hqk,khd->qhd", grad_scores, key, preferred_element_type=F32)
    grad_key = jnp.einsum("hqk,qhd->khd", grad_scores, query, preferred_element_type=F32)
    grad_value = jnp.einsum("hqk,qhd->khd", probs_low, grad_attended, preferred_element_type=F32)
    grad_qk = rotate(jnp.stack([grad_query, grad_key], axis=1) * scaling, cosine, sine, -1.0)
    grad_qk = grad_qk.reshape(seq, 2, cols)
    qk_term = jnp.sum(grad_qk * qk_unit, axis=0)
    grad_qk = grad_qk * qk_gain
    inner_means = plane_sum(jnp.sum(grad_qk * qk_unit, axis=-1), 6)[:, :, None] / width
    grad_qk = qk_scale * (grad_qk - qk_unit * inner_means)
    grad_qkv = jnp.concatenate(
        [grad_qk.reshape(seq, 2 * cols), grad_value.reshape(seq, cols)], axis=1
    ).astype(BF16)
    qkv_grad = dot(normed_all, grad_qkv, ((0,), (0,)))
    grad_normed = dot(grad_qkv, qkv_here, ((1,), (1,))).astype(BF16)
    grad_normed = lax.psum_scatter(grad_normed, "fsdp", scatter_dimension=0, tiled=True).astype(F32)
    attn_term = jnp.sum(grad_normed * unit1, axis=0)
    hidden_grad = grad_middle + norm_back(grad_normed * gain_attn, unit1, scale1)

    attn_grad = jnp.concatenate([qkv_grad, out_grad.reshape(width, cols)], axis=1).astype(BF16)
    attn_grad = lax.psum_scatter(attn_grad, "dp", scatter_dimension=0, tiled=True)
    attn_grad = attn_grad.reshape(fsdp, own_rows, 4 * cols)
    attn_grad = lax.all_to_all(attn_grad, "fsdp", 0, 0, tiled=True)
    attn_grad = attn_grad.reshape(fsdp, own_rows, 4, cols).transpose(1, 2, 0, 3).astype(F32)
    attn_grad = attn_grad.reshape(own_rows, 4 * width)

    qk_full = jnp.zeros((2, width), F32)
    qk_full = lax.dynamic_update_slice(qk_full, qk_term, (0, here))
    terms = jnp.concatenate([attn_term[None], qk_full, ffn_term[None]])
    terms = terms.reshape(4, n, own_rows).transpose(1, 0, 2).reshape(n, 4 * own_rows)
    terms = jnp.concatenate(
        [
            terms,
            router_term.reshape(n, own_rows * experts),
            jnp.broadcast_to(squares[None], (n, 3)),
        ],
        axis=1,
    )
    term_size = terms.shape[1]
    term_rows = -(-term_size // 1024) * 8
    terms = jnp.pad(terms, ((0, 0), (0, term_rows * 128 - term_size)))
    terms = exchange(terms.reshape(n, term_rows, 128), BOTH, 7, True)
    terms = jnp.sum(terms, axis=0).reshape(-1)
    gain_grads = terms[: 4 * own_rows].reshape(4, own_rows)
    router_grad = terms[4 * own_rows : 4 * own_rows + own_rows * experts]
    valid_cells = jnp.sum(lengths).astype(F32) * width
    stats = jnp.sqrt(terms[term_size - 3 : term_size] / valid_cells)

    return (
        block_total.astype(BF16),
        hidden_grad,
        gain_grads[0],
        gain_grads[1],
        gain_grads[2],
        gain_grads[3],
        attn_grad[:, : 3 * width],
        attn_grad[:, 3 * width :],
        router_grad.reshape(own_rows, experts),
        inner_grad.astype(F32),
        outer_grad.astype(F32),
        stats,
    )


def solution(mesh):
    one = P(BOTH)
    two = P(BOTH, None)
    three = P(BOTH, None, None)
    in_specs = (two, P(), two, one, one, one, one, two, two, two, three, three, two)
    out_specs = (two, two, one, one, one, one, two, two, two, three, three, P())
    return jax.shard_map(body, mesh=mesh, in_specs=in_specs, out_specs=out_specs, check_vma=False)
```

time: 2540 us -> 1440 us (0.57)
  waiting for transfers between devices: 1680 us -> 919 us
  blocking collectives: 368 us -> 26.1 us
  Pallas kernels: 0 us -> 66 us
  local copies, waits for them, and re-layouts: 192 us -> 132 us
    reduce_scatter x5, waiting for transfers between devices: 960 us -> 401 us  [the longest x1 187 us: body(): lax.psum_scatter(expert_sum, BOTH, scatter_dimension=0, tiled=True)]
    all_gather x6 -> x5, waiting for transfers between devices: 510 us -> 196 us  [the longest x1 80.4 us: body(): grad_all = lax.all_gather(grad_total.astype(BF16), BOTH, axis=0, tiled=True)]
    all_to_all x5, waiting for transfers between devices: 85.2 us -> 321 us  [the longest x1 153 us: body(): lax.all_to_all(inner_weight, BOTH, 0, 0, tiled=True)]
    all_to_all x3 -> x1, blocking collectives: 192 us -> 26.1 us  [body(): attn_weight = lax.all_to_all(attn_weight, 'fsdp', 0, 0, tiled=True)]
    unnamed x15 -> x10, waiting for transfers between devices: 123 us -> 0.83 us
    all_gather x1 -> x0, blocking collectives: 89.9 us -> none  [fetch_shared(): lax.all_gather(router_weight, ('dp', 'fsdp'), axis=0, tiled=True)]
    unnamed x2 -> x0, blocking collectives: 85.7 us -> none
    pallas_call x0 -> x8, Pallas kernels: none -> 66 us  [exchange(): pl.pallas_call(functools.partial(exchange_kernel, axes, n, fsdp, spread),...]
  transfers between devices with their start and end apart: 18 -> 15, of which waited for: 12 -> 12; matrix products, arithmetic and copies ran while one was open for 10% -> 14% of each run, Pallas kernels for 0% -> 1%
where the time goes in v1:
time: 1440 us; the launch traced here: 1430 us
  waiting for transfers between devices  919 us (64%)
  matrix products  193 us (13%)
  local copies, waits for them, and re-layouts  132 us (9%)
  Pallas kernels  66 us (5%)
  other arithmetic  55.6 us (4%)
  blocking collectives  26.1 us (2%)
  starting transfers between devices  20.7 us (1%)
  between operations  16.2 us (1%)
    reduce_scatter x1, waiting for transfers between devices, body(): lax.psum_scatter(expert_sum, BOTH, scatter_dimension=0, tiled=True)  187 us
    reduce_scatter x1, waiting for transfers between devices, body(): lax.psum_scatter(grad_rows, BOTH, scatter_dimension=0, tiled=True)  168 us
    dot_general x12, matrix products, dot(): return lax.dot_general(a, b, (dims, ((), ())), preferred_element_type=F32)  155 us
    all_to_all x1, waiting for transfers between devices, body(): lax.all_to_all(inner_weight, BOTH, 0, 0, tiled=True)  153 us
    all_to_all x1, waiting for transfers between devices, body(): lax.all_to_all(inner_grad.reshape(n, own_rows, 2 * inner), BOTH, 0, 0, ti...  137 us
    all_gather x1, waiting for transfers between devices, body(): grad_all = lax.all_gather(grad_total.astype(BF16), BOTH, axis=0, tiled=True)  80.4 us
    all_gather x1, waiting for transfers between devices, body(): lax.all_gather(attn_weight.reshape(fsdp * own_rows, 4 * cols), 'dp', axis...  78.6 us
    pallas_call x8, Pallas kernels, exchange(): pl.pallas_call(functools.partial(exchange_kernel, axes, n, fsdp, spread),...  66 us
  transfers between devices with their start and end apart: 15, of which 12 were waited for; matrix products, arithmetic and copies ran while one was open for 14% of the time, Pallas kernels for 1%

profile of v1, /device:TPU:0, one launch (start us, length us, event | category | flops | bytes accessed | tf_op | source)
XLA Modules:
  0.0 1428.0 jit_solution(7829282233803781591)
XLA Ops:
  13.0 26.1 %all_to_all.30 = bf16[8,64,1024]{2,1,0:T(8,128)(2,1)} all-to-all(bf16[8,64,1024]{2,1,0:T(8,128)(2,1)S(1)} %reshape.405), channel_id=1, replica_groups=mesh['dp'=4,'fsdp'=8] {'fsdp'}, dimensions={0} | all-to-all | bytes 2097152 | tf_op jit(solution)/shard_map/all_to_all | solution.py:162
  40.1 9.4 shard_map.220
  63.5 78.6 %all-gather.8.cloned.1.call-done = bf16[2048,1024]{1,0:T(8,128)(2,1)} async-done(((bf16[512,1024]{1,0:T(8,128)(2,1)}), bf16[2048,1024]{1,0:T(8,128)(2,1)}) %all-gather.8.cloned.1.call-update) | async-done | bytes 4194320 | tf_op jit(solution)/shard_map/all_gather | solution.py:163
  142.0 6.6 fusion.14
  166.2 9.6 fusion.70
  182.5 33.9 %all-gather.10.cloned.1.call-done = bf16[8,1024,256]{2,1,0:T(8,128)(2,1)} async-done(((bf16[1,1024,256]{2,1,0:T(8,128)(2,1)}), bf16[8,1024,256]{2,1,0:T(8,128)(2,1)}) %all-gather.10.cloned.1.call-update) | async-done | bytes 4194320 | tf_op jit(solution)/shard_map/all_gather | solution.py:208
  220.6 9.0 shard_map.222
  242.1 7.9 reshape.412
  250.0 8.6 copy.226
  258.6 7.7 reshape.413
  278.7 153.5 %all-to-all-done.1 = bf16[32,64,1024]{2,1,0:T(8,128)(2,1)} async-done(((bf16[32,64,1024]{2,1,0:T(8,128)(2,1)}), bf16[32,64,1024]{2,1,0:T(8,128)(2,1)}, u32[]{:S(2)}, u32[]{:S(2)}) %all-to-all-start.1) | async-done | bytes 4194336 | tf_op jit(solution)/shard_map/all_to_all | solution.py:171
  432.2 31.9 %fusion.76 = f32[4096,1024]{0,1:T(8,128)} fusion(bf16[4096,2048]{1,0:T(8,128)(2,1)} %all-gather.12.cloned.1.call-done, bf16[2048,1024]{1,0:T(8,128)(2,1)} %bitcast.18), kind=kOutput, calls=%fused_computation.167 | convolution fusion | flops 17179869184 | bytes 37748736 | tf_op jit(solution)/shard_map/dot_general | solution.py:106
  464.1 80.4 %all-gather.14.cloned.1.call-done = bf16[4096,2048]{1,0:T(8,128)(2,1)} async-done(((bf16[128,2048]{1,0:T(8,128)(2,1)}), bf16[4096,2048]{1,0:T(8,128)(2,1)}) %all-gather.14.cloned.1.call-update) | async-done | bytes 16777232 | tf_op jit(solution)/shard_map/all_gather | solution.py:231
  544.5 20.8 %bitcast_reduce_fusion = (f32[4096,2]{0,1:T(2,128)S(1)}, bf16[4096,512]{0,1:T(8,128)(2,1)}, f32[4096,512]{0,1:T(8,128)}) fusion(f32[4096,1024]{0,1:T(8,128)} %fusion.76, bf16[4096,2048]{1,0:T(8,128)(2,1)} %all-gather.14.cloned.1.call-done, bf16[512,2048]{1,0:T(8,128)(2,1)S(1)} %bitcast.220), kind=kOutput, calls=%fused_computation.13 | convolution fusion | flops 8608800768 | bytes 48267264 | tf_op jit(solution)/shard_map/dot_general | solution.py:106
  566.1 8.5 shard_map.224
  576.2 8.7 shard_map.223
  585.8 17.2 %multiply_convert_fusion.2 = (bf16[4096,512]{0,1:T(8,128)(2,1)}, bf16[4096,512]{0,1:T(8,128)(2,1)}, bf16[4096,512]{0,1:T(8,128)(2,1)}) fusion(f32[4096,512]{0,1:T(8,128)} %get-tuple-element.105, f32[4096,1024]{0,1:T(8,128)} %fusion.76, f32[4096,2]{0,1:T(2,128)S(1)} %slice_bitcast_fusion, bf16[4096,512]{0,1:T(8,128)(2,1)} %get-tuple-element.76), kind=kLoop, calls=%fused_computation.18 | loop fusion | flops 35651584 | bytes 41975808 | tf_op jit(solution)/shard_map/convert.19
  603.0 25.3 %convolution_convert_fusion = bf16[4096,2048]{1,0:T(8,128)(2,1)} fusion(bf16[2048,1024]{1,0:T(8,128)(2,1)} %bitcast.18, bf16[4096,512]{0,1:T(8,128)(2,1)} %get-tuple-element.80, bf16[4096,512]{0,1:T(8,128)(2,1)} %get-tuple-element.79), kind=kOutput, calls=%fused_computation.1 | convolution fusion | flops 17205035008 | bytes 29360128 | tf_op jit(solution)/shard_map/dot_general | solution.py:106
  628.4 15.1 %convolution_convert_fusion.1 = bf16[4096,2048]{1,0:T(8,128)(2,1)} fusion(bf16[4096,512]{0,1:T(8,128)(2,1)} %get-tuple-element.90, bf16[512,2048]{1,0:T(8,128)(2,1)S(1)} %bitcast.221), kind=kOutput, calls=%fused_computation.2 | convolution fusion | flops 8598323200 | bytes 23068672 | tf_op jit(solution)/shard_map/dot_general | solution.py:106
  643.6 168.0 %reduce-scatter.8.cloned.1.call-done = bf16[128,2048]{1,0:T(8,128)(2,1)} async-done(((bf16[4096,2048]{1,0:T(8,128)(2,1)}), bf16[128,2048]{1,0:T(8,128)(2,1)}) %reduce-scatter.8.cloned.1.call-update) | async-done | bytes 524304 | tf_op jit(solution)/shard_map/reduce_scatter | solution.py:260
  811.5 186.8 %reduce-scatter.6.cloned.1.call-done = bf16[128,2048]{1,0:T(8,128)(2,1)} async-done(((bf16[4096,2048]{1,0:T(8,128)(2,1)}), bf16[128,2048]{1,0:T(8,128)(2,1)}) %reduce-scatter.6.cloned.1.call-update) | async-done | bytes 524304 | tf_op jit(solution)/shard_map/reduce_scatter | solution.py:256
  1004.2 9.4 shard_map.225
  1031.8 46.0 %reduce-scatter.10.cloned.1.call-done = bf16[1024,256]{1,0:T(8,128)(2,1)} async-done(((bf16[8192,256]{1,0:T(8,128)(2,1)}), bf16[1024,256]{1,0:T(8,128)(2,1)}) %reduce-scatter.10.cloned.1.call-update) | async-done | bytes 524304 | tf_op jit(solution)/shard_map/reduce_scatter | solution.py:300
  1122.8 13.6 convolution_convert_fusion.4
  1141.5 24.7 %fusion.12 = bf16[2048,1024]{1,0:T(8,128)(2,1)} fusion(bf16[4096,2048]{1,0:T(8,128)(2,1)} %all-gather.12.cloned.1.call-done, bf16[4096,512]{0,1:T(8,128)(2,1)} %get-tuple-element.80, bf16[4096,512]{0,1:T(8,128)(2,1)} %get-tuple-element.79), kind=kOutput, calls=%fused_computation.36 | convolution fusion | flops 17198743552 | bytes 29360128 | tf_op jit(solution)/shard_map/dot_general | solution.py:106
  1168.5 10.7 all-to-all-done.5
  1203.3 137.4 %all-to-all-done.4 = bf16[32,64,1024]{2,1,0:T(8,128)(2,1)} async-done(((bf16[32,64,1024]{2,1,0:T(8,128)(2,1)}), bf16[32,64,1024]{2,1,0:T(8,128)(2,1)}, u32[]{:S(2)}, u32[]{:S(2)}) %all-to-all-start.4) | async-done | bytes 4194336 | tf_op jit(solution)/shard_map/all_to_all | solution.py:269
  1340.7 11.7 reshape.451
  1352.4 12.0 copy.225
  1364.4 10.8 reshape.445
  1380.1 10.5 shard_map.227
  1402.0 13.5 all-to-all-done.3
  (306 shorter events, 198.0 us)
Async XLA Ops:
  7.2 53.2 %all-gather.6.cloned.1.call-start = ((), (), s32[]{:S(2)}) async-start(), calls=%async_computation.11 | async-start | bytes 4718592 | tf_op jit(solution)/shard_map/all_gather | solution.py:176
  7.9 134.1 %all-gather.8.cloned.1.call-start = ((), (), s32[]{:S(2)}) async-start(), calls=%async_computation.12 | async-start | bytes 5242880 | tf_op jit(solution)/shard_map/all_gather | solution.py:163
  11.1 28.3 %copy-start.59 = (bf16[64]{0:T(256)(128)(2,1)S(1)}, bf16[64]{0:T(256)(128)(2,1)}, u32[]{:S(2)}) copy-start(bf16[64]{0:T(256)(128)(2,1)} %param.16) | copy-start | bytes 388
  11.1 28.3 %copy-start.60 = (bf16[64]{0:T(256)(128)(2,1)S(1)}, bf16[64]{0:T(256)(128)(2,1)}, u32[]{:S(2)}) copy-start(bf16[64]{0:T(256)(128)(2,1)} %param.17) | copy-start | bytes 388
  11.2 40.5 %copy-start.63 = (s32[4]{0:T(128)S(1)}, s32[4]{0:T(128)}, u32[]{:S(2)}) copy-start(s32[4]{0:T(128)} %param.14) | copy-start | bytes 52
  39.1 177.3 %all-gather.10.cloned.1.call-start = ((), (), s32[]{:S(2)}) async-start(), calls=%async_computation.13 | async-start | bytes 4718592 | tf_op jit(solution)/shard_map/all_gather | solution.py:208
  50.8 97.9 %copy-start.41 = (f32[2048]{0:T(1024)}, f32[2048]{0:T(1024)S(1)}, u32[]{:S(2)}) copy-start(f32[2048]{0:T(1024)S(1)} %mul.450) | copy-start | bytes 24580
  51.6 110.6 %copy-start.45 = (f32[2,2,128]{2,1,0:T(2,128)}, f32[2,2,128]{2,1,0:T(2,128)S(1)}, u32[]{:S(2)}) copy-start(f32[2,2,128]{2,1,0:T(2,128)S(1)} %mul.458) | copy-start | bytes 6148
  63.5 78.6 %copy-start.54 = (f32[1024]{0:T(1024)}, f32[1024]{0:T(1024)S(1)}, u32[]{:S(2)}) copy-start(f32[1024]{0:T(1024)S(1)} %add_rsqrt_fusion.1) | copy-start | bytes 12292
  181.1 251.1 %all-gather.12.cloned.1.call-start = ((), (), s32[]{:S(2)}) async-start(), calls=%async_computation.14 | async-start | bytes 17301504 | tf_op jit(solution)/shard_map/all_gather | solution.py:232
  181.2 51.1 %copy-start.43 = (f32[2048]{0:T(1024)}, f32[2048]{0:T(1024)S(1)}, u32[]{:S(2)}) copy-start(f32[2048]{0:T(1024)S(1)} %mul.475) | copy-start | bytes 24580
  182.5 33.9 %copy-start.19 = (bf16[2048,256]{1,0:T(8,128)(2,1)}, bf16[2048,256]{1,0:T(8,128)(2,1)S(1)}, u32[]{:S(2)}) copy-start(bf16[2048,256]{1,0:T(8,128)(2,1)S(1)} %slice.140) | copy-start | bytes 3145732
  234.2 310.3 %all-gather.14.cloned.1.call-start = ((), (), s32[]{:S(2)}) async-start(), calls=%async_computation.16 | async-start | bytes 17301504 | tf_op jit(solution)/shard_map/all_gather | solution.py:231
  238.5 33.9 %all-to-all-start.2 = ((bf16[8,2,32,2048]{3,2,1,0:T(8,128)(2,1)}), bf16[8,2,32,2048]{3,2,1,0:T(8,128)(2,1)S(1)}, u32[]{:S(2)}, u32[]{:S(2)}) async-start(bf16[8,2,32,2048]{3,2,1,0:T(8,128)(2,1)} %bitcast.207), calls=%async_computation.2 | async-start | bytes 4194304 | tf_op jit(solution)/shard_map/all_to_all | solution.py:173
  272.4 159.8 %all-to-all-start.1 = ((bf16[32,64,1024]{2,1,0:T(8,128)(2,1)}), bf16[32,64,1024]{2,1,0:T(8,128)(2,1)}, u32[]{:S(2)}, u32[]{:S(2)}) async-start(bf16[32,64,1024]{2,1,0:T(8,128)(2,1)} %reshape.413), calls=%async_computation.1 | async-start | bytes 8388608 | tf_op jit(solution)/shard_map/all_to_all | solution.py:171
  276.4 535.1 %reduce-scatter.8.cloned.1.call-start = ((), (), s32[]{:S(2)}) async-start(), calls=%async_computation.17 | async-start | bytes 17301504 | tf_op jit(solution)/shard_map/reduce_scatter | solution.py:260
  276.9 187.2 %copy-start.28 = (bf16[2048,16]{1,0:T(8,128)(2,1)}, bf16[2048,16]{1,0:T(8,128)(2,1)S(1)}, u32[]{:S(2)}) copy-start(bf16[2048,16]{1,0:T(8,128)(2,1)S(1)} %reshape.415) | copy-start | bytes 196612
  432.2 112.3 %copy-start.26 = (bf16[2,8,32,2048]{3,2,1,0:T(8,128)(2,1)S(1)}, bf16[2,8,32,2048]{3,2,1,0:T(8,128)(2,1)}, u32[]{:S(2)}) copy-start(bf16[2,8,32,2048]{3,2,1,0:T(8,128)(2,1)} %copy.173) | copy-start | bytes 6291460
  628.3 370.0 %reduce-scatter.6.cloned.1.call-start = ((), (), s32[]{:S(2)}) async-start(), calls=%async_computation.15 | async-start | bytes 17301504 | tf_op jit(solution)/shard_map/reduce_scatter | solution.py:256
  643.4 354.8 %copy-start.9 = (f32[128,2048]{1,0:T(8,128)S(1)}, f32[128,2048]{1,0:T(8,128)}, u32[]{:S(2)}) copy-start(f32[128,2048]{1,0:T(8,128)} %copy-done.8) | copy-start | bytes 3145732
  643.4 354.8 %copy-start.29 = (bf16[2048,16]{1,0:T(8,128)(2,1)S(1)}, bf16[2048,16]{1,0:T(8,128)(2,1)}, u32[]{:S(2)}) copy-start(bf16[2048,16]{1,0:T(8,128)(2,1)} %copy-done.28) | copy-start | bytes 196612
  643.4 354.8 %copy-start.44 = (f32[2048]{0:T(1024)S(1)}, f32[2048]{0:T(1024)}, u32[]{:S(2)}) copy-start(f32[2048]{0:T(1024)} %copy-done.43) | copy-start | bytes 24580
  643.4 354.8 %copy-start.51 = (f32[128]{0:T(128)S(1)}, f32[128]{0:T(128)}, u32[]{:S(2)}) copy-start(f32[128]{0:T(128)} %copy-done.50) | copy-start | bytes 1540
  643.4 354.8 %copy-start.57 = (f32[128]{0:T(128)S(1)}, f32[128]{0:T(128)}, u32[]{:S(2)}) copy-start(f32[128]{0:T(128)} %copy-done.56) | copy-start | bytes 1540
  643.5 358.1 %copy-start.24 = (bf16[128,2048]{1,0:T(8,128)(2,1)S(1)}, bf16[128,2048]{1,0:T(8,128)(2,1)}, u32[]{:S(2)}) copy-start(bf16[128,2048]{1,0:T(8,128)(2,1)} %param.25) | copy-start | bytes 1572868
  643.5 434.3 %reduce-scatter.10.cloned.1.call-start = ((), (), s32[]{:S(2)}) async-start(), calls=%async_computation.18 | async-start | bytes 4718592 | tf_op jit(solution)/shard_map/reduce_scatter | solution.py:300
  1024.5 353.0 %reduce-scatter.12.cloned.1.call-start = ((), (), s32[]{:S(2)}) async-start(), calls=%async_computation.19 | async-start | bytes 4718592 | tf_op jit(solution)/shard_map/reduce_scatter | solution.py:321
  1025.2 53.9 %copy-start.48 = (f32[2,1024]{1,0:T(2,128)S(1)}, f32[2,1024]{1,0:T(2,128)}, u32[]{:S(2)}) copy-start(f32[2,1024]{1,0:T(2,128)} %copy-done.47) | copy-start | bytes 24580
  1137.9 41.4 %all-to-all-start.5 = ((bf16[8,2,32,2048]{3,2,1,0:T(8,128)(2,1)}), bf16[8,2,32,2048]{3,2,1,0:T(8,128)(2,1)S(1)}, u32[]{:S(2)}, u32[]{:S(2)}) async-start(bf16[8,2,32,2048]{3,2,1,0:T(8,128)(2,1)} %bitcast.206), calls=%async_computation.10 | async-start | bytes 4194304 | tf_op jit(solution)/shard_map/all_to_all | solution.py:273
  1179.2 161.5 %all-to-all-start.4 = ((bf16[32,64,1024]{2,1,0:T(8,128)(2,1)}), bf16[32,64,1024]{2,1,0:T(8,128)(2,1)}, u32[]{:S(2)}, u32[]{:S(2)}) async-start(bf16[32,64,1024]{2,1,0:T(8,128)(2,1)} %bitcast.213), calls=%async_computation.9 | async-start | bytes 8388608 | tf_op jit(solution)/shard_map/all_to_all | solution.py:269
  1183.1 209.9 %reduce-scatter.14.cloned.1.call-start = ((), (), s32[]{:S(2)}) async-start(), calls=%async_computation.20 | async-start | bytes 5242880 | tf_op jit(solution)/shard_map/reduce_scatter | solution.py:326
  1395.2 20.3 %all-to-all-start.3 = ((bf16[8,64,1024]{2,1,0:T(8,128)(2,1)}), bf16[8,64,1024]{2,1,0:T(8,128)(2,1)S(1)}, u32[]{:S(2)}, u32[]{:S(2)}) async-start(bf16[8,64,1024]{2,1,0:T(8,128)(2,1)} %bitcast.215), calls=%async_computation.8 | async-start | bytes 2097152 | tf_op jit(solution)/shard_map/all_to_all | solution.py:328
  (51 other events, 378.8 us)
Sparse Core Ops, SparseCore 0:
  9.9 50.4 all-gather.5
  62.0 80.0 all-gather.7
  181.2 35.1 all-gather.9
  234.3 193.8 all-gather.11
  431.5 112.9 all-gather.13
  628.4 183.0 reduce-scatter.7
  813.8 184.4 reduce-scatter.5
  1024.6 53.0 reduce-scatter.9
  1122.9 91.0 reduce-scatter.11
  1216.2 121.4 reduce-scatter.13

commit v2 on v1

--- a/solution.py
+++ b/solution.py
@@ -104,6 +104,503 @@
 
 def dot(a, b, dims):
     return lax.dot_general(a, b, (dims, ((), ())), preferred_element_type=F32)
+
+
+def expert_kernel(
+    dp,
+    x_in,
+    c_all,
+    gates,
+    inner_in,
+    outer_in,
+    sums,
+    gate_out,
+    inner_out,
+    outer_out,
+    gathered,
+    far,
+    xv,
+    cv,
+    wi,
+    wo,
+    gi,
+    go,
+    ggu,
+    act,
+    gv,
+    part,
+    held,
+    core_in,
+    half_in,
+    full_in,
+    local,
+    z_send,
+    z_recv,
+    a_send,
+    a_recv,
+    b_send,
+    b_recv,
+    k_send,
+    k_recv,
+    c_send,
+    c_recv,
+    s1_send,
+    s1_recv,
+    s2_send,
+    s2_recv,
+    o_send,
+    o_recv,
+    credit,
+):
+    rows, width = x_in.shape
+    half = rows // 2
+    z = lax.axis_index("dp")
+    f = lax.axis_index("fsdp")
+    core = lax.rem(f, 2)
+    chip = f // 2
+    xbit = lax.rem(chip, 2)
+    ybit = chip // 2
+    chip_x = ybit * 2 + (1 - xbit)
+    chip_y = (1 - ybit) * 2 + xbit
+    chip_d = (1 - ybit) * 2 + (1 - xbit)
+    fx = chip_x * 2 + core
+    fy = chip_y * 2 + core
+    fd = chip_d * 2 + core
+    fc = chip * 2 + (1 - core)
+    to_x = {"fsdp": fx}
+    to_y = {"fsdp": fy}
+    to_c = {"fsdp": fc}
+    upper = pl.ds(0, half)
+    lower = pl.ds(half, half)
+
+    def remote(src, dst, send, recv, device):
+        return pltpu.make_async_remote_copy(
+            src, dst, send, recv, device_id=device, device_id_type=MESH_ID
+        )
+
+    def plane_at(s):
+        return lax.rem(z + 1 + s, dp)
+
+    def far_copy(i):
+        return remote(
+            x_in,
+            gathered.at[z, f],
+            z_send.at[i],
+            z_recv.at[i],
+            {"dp": lax.rem(z + dp - i, dp)},
+        )
+
+    def gather_one(s):
+        block = gathered.at[plane_at(s), f]
+        return (
+            remote(block.at[upper], block.at[upper], a_send.at[s, 0], a_recv.at[s, 0], to_x),
+            remote(block.at[lower], block.at[lower], a_send.at[s, 1], a_recv.at[s, 1], to_y),
+        )
+
+    def gather_two(s):
+        p = plane_at(s)
+        copies = []
+        for i, (owner, piece, device) in enumerate(
+            ((f, upper, to_y), (fx, upper, to_y), (f, lower, to_x), (fy, lower, to_x))
+        ):
+            ref = gathered.at[p, owner, piece]
+            copies.append(remote(ref, ref, b_send.at[s, i], b_recv.at[s, i], device))
+        return copies
+
+    def gather_core(s):
+        p = plane_at(s)
+        copies = []
+        for i, owner in enumerate((f, fx, fy, fd)):
+            ref = gathered.at[p, owner]
+            copies.append(remote(ref, ref, k_send.at[s, i], k_recv.at[s, i], to_c))
+        return copies
+
+    def block_rows(owner):
+        return pl.ds(pl.multiple_of(owner * rows, rows), rows)
+
+    def core_copy(k, j):
+        return remote(
+            part.at[k, block_rows(j * 2 + 1 - core)],
+            core_in.at[k, j],
+            c_send.at[k, j],
+            c_recv.at[k, j],
+            to_c,
+        )
+
+    def half_copies(k):
+        return (
+            remote(
+                held.at[k, chip_d, upper], half_in.at[k, 0], s1_send.at[k, 0], s1_recv.at[k, 0], to_x
+            ),
+            remote(
+                held.at[k, chip_d, lower], half_in.at[k, 1], s1_send.at[k, 1], s1_recv.at[k, 1], to_y
+            ),
+        )
+
+    def full_copies(k):
+        return (
+            remote(held.at[k, chip_x], full_in.at[k, 0], s2_send.at[k, 0], s2_recv.at[k, 0], to_x),
+            remote(held.at[k, chip_y], full_in.at[k, 1], s2_send.at[k, 1], s2_recv.at[k, 1], to_y),
+        )
+
+    def out_copy(s, k):
+        return remote(
+            held.at[k, chip], far.at[k, z], o_send.at[s, k], o_recv.at[s, k], {"dp": plane_at(s)}
+        )
+
+    def add_core():
+        for k in range(2):
+            for j in range(4):
+                core_copy(k, j).wait()
+            def one(j, carry):
+                held[k, j] = (
+                    part[k, block_rows(j * 2 + core)].astype(F32) + core_in[k, j].astype(F32)
+                ).astype(BF16)
+                return carry
+            lax.fori_loop(0, 4, one, 0)
+        pl.semaphore_signal(credit, inc=1, device_id=to_c, device_id_type=MESH_ID)
+
+    def start_half():
+        for k in range(2):
+            for copy in half_copies(k):
+                copy.start()
+
+    def pass_full():
+        for k in range(2):
+            for copy in half_copies(k):
+                copy.wait()
+            held[k, chip_y, upper] = (
+                held[k, chip_y, upper].astype(F32) + half_in[k, 0].astype(F32)
+            ).astype(BF16)
+            held[k, chip_x, lower] = (
+                held[k, chip_x, lower].astype(F32) + half_in[k, 1].astype(F32)
+            ).astype(BF16)
+            for copy in full_copies(k):
+                copy.start()
+
+    def total_here(k):
+        for copy in full_copies(k):
+            copy.wait()
+        return held[k, chip].astype(F32) + full_in[k, 0].astype(F32) + full_in[k, 1].astype(F32)
+
+    barrier = pltpu.get_barrier_semaphore()
+    for device in (to_x, to_y, to_c):
+        pl.semaphore_signal(barrier, inc=1, device_id=device, device_id_type=MESH_ID)
+    for i in range(1, dp):
+        pl.semaphore_signal(
+            barrier, inc=1, device_id={"dp": lax.rem(z + i, dp)}, device_id_type=MESH_ID
+        )
+    pl.semaphore_wait(barrier, 3 + dp - 1)
+
+    for i in range(1, dp):
+        far_copy(i).start()
+    loads = [pltpu.make_async_copy(x_in, gathered.at[z, f], local.at[0])]
+    for q in range(4):
+        loads.append(pltpu.make_async_copy(inner_in.at[:, q], wi.at[q], local.at[1 + q]))
+    for e in range(2):
+        loads.append(pltpu.make_async_copy(outer_in.at[:, e], wo.at[e], local.at[5 + e]))
+    for load in loads:
+        load.start()
+    gi[...] = jnp.zeros_like(gi)
+    go[...] = jnp.zeros_like(go)
+    for load in loads:
+        load.wait()
+
+    def begin_gather(s):
+        @pl.when(s < dp - 1)
+        def _():
+            far_copy(s + 1).wait_recv()
+
+        for copy in gather_one(s):
+            copy.start()
+
+    def middle_gather(s):
+        for copy in gather_one(s):
+            copy.wait_recv()
+        for copy in gather_two(s):
+            copy.start()
+
+    def end_gather(s):
+        for copy in gather_two(s):
+            copy.wait_recv()
+        for copy in gather_core(s):
+            copy.start()
+
+    begin_gather(0)
+    middle_gather(0)
+    begin_gather(1)
+    end_gather(0)
+
+    inner_rows = wi.shape[1] * wi.shape[2]
+    ff_here = wo.shape[1] * wo.shape[2]
+    tile = xv.shape[0] // 2
+
+    def tile_step(t):
+        r = pl.ds(pl.multiple_of(t * tile, tile), tile)
+        x = xv[r, :]
+        c = cv[r, :]
+        for e in range(2):
+            gate = dot(x, wi[e].reshape(inner_rows, ff_here), ((1,), (0,)))
+            up = dot(x, wi[2 + e].reshape(inner_rows, ff_here), ((1,), (0,)))
+            back = dot(c, wo[e].reshape(ff_here, width), ((1,), (1,)))
+            sigmoid = 1.0 / (1.0 + jnp.exp(-gate))
+            silu = gate * sigmoid
+            active = (silu * up).astype(BF16).astype(F32)
+            weight = gv[r, e : e + 1]
+            gv[r, 8 + e : 9 + e] = jnp.sum(active * back, axis=-1, keepdims=True)
+            act[e, r, :] = (weight * active).astype(BF16)
+            back = weight * back
+            ggu[e, r, :] = (back * up * sigmoid * (1.0 + gate * (1.0 - sigmoid))).astype(BF16)
+            ggu[2 + e, r, :] = (back * silu).astype(BF16)
+        step = 512
+        for i in range(width // step):
+            col = pl.ds(i * step, step)
+            blocks = pl.ds(i * step // wi.shape[2], step // wi.shape[2])
+            total = dot(act[0, r, :], wo[0, :, :, col].reshape(ff_here, step), ((1,), (0,)))
+            total += dot(act[1, r, :], wo[1, :, :, col].reshape(ff_here, step), ((1,), (0,)))
+            part[0, r, col] = total.astype(BF16)
+            total = dot(ggu[0, r, :], wi[0, blocks].reshape(step, ff_here), ((1,), (1,)))
+            for q in range(1, 4):
+                total += dot(ggu[q, r, :], wi[q, blocks].reshape(step, ff_here), ((1,), (1,)))
+            part[1, r, col] = total.astype(BF16)
+
+    def weight_step():
+        def inner_part(i, carry):
+            col = pl.ds(pl.multiple_of(i * 256, 256), 256)
+            xt = xv[:, col]
+            for q in range(4):
+                gi[q, col, :] += dot(xt, ggu[q], ((0,), (0,)))
+            return carry
+
+        lax.fori_loop(0, width // 256, inner_part, 0)
+
+        def outer_part(i, carry):
+            col = pl.ds(pl.multiple_of(i * 512, 512), 512)
+            ct = cv[:, col]
+            for e in range(2):
+                go[e, :, col] += dot(act[e], ct, ((0,), (0,)))
+            return carry
+
+        lax.fori_loop(0, width // 512, outer_part, 0)
+
+    def chunk(s, carry):
+        p = plane_at(s)
+        c_load = pltpu.make_async_copy(c_all.at[p], cv, local.at[1])
+        g_load = pltpu.make_async_copy(gates.at[p], gv, local.at[2])
+        c_load.start()
+        g_load.start()
+        for copy in gather_core(s):
+            copy.wait_recv()
+        for j in range(8):
+            pltpu.make_async_copy(
+                gathered.at[p, j], xv.at[pl.ds(j * rows, rows)], local.at[3 + j]
+            ).start()
+        c_load.wait()
+        g_load.wait()
+        for j in range(8):
+            pltpu.make_async_copy(
+                gathered.at[p, j], xv.at[pl.ds(j * rows, rows)], local.at[3 + j]
+            ).wait()
+        tile_step(0)
+
+        @pl.when(s > 0)
+        def _():
+            pass_full()
+
+        @pl.when(s < dp - 1)
+        def _():
+            middle_gather(s + 1)
+
+        @pl.when(s < dp - 2)
+        def _():
+            begin_gather(s + 2)
+
+        tile_step(1)
+        g_store = pltpu.make_async_copy(gv, gate_out.at[p], local.at[2])
+        g_store.start()
+
+        @pl.when(s > 0)
+        def _():
+            pl.semaphore_wait(credit, 1)
+
+        for k in range(2):
+            for j in range(4):
+                core_copy(k, j).start()
+        weight_step()
+
+        @pl.when(s > 0)
+        def _():
+            for k in range(2):
+                held[k, chip] = total_here(k).astype(BF16)
+                out_copy(s - 1, k).start()
+            for k in range(2):
+                out_copy(s - 1, k).wait_send()
+
+        add_core()
+        start_half()
+
+        @pl.when(s < dp - 1)
+        def _():
+            end_gather(s + 1)
+
+        g_store.wait()
+        return carry
+
+    lax.fori_loop(0, dp, chunk, 0)
+
+    pass_full()
+    for q in range(4):
+        wi[q] = gi[q].astype(BF16).reshape(wi.shape[1:])
+    for e in range(2):
+        wo[e] = go[e].astype(BF16).reshape(wo.shape[1:])
+    stores = []
+    for q in range(4):
+        stores.append(pltpu.make_async_copy(wi.at[q], inner_out.at[:, q], local.at[q]))
+    for e in range(2):
+        stores.append(pltpu.make_async_copy(wo.at[e], outer_out.at[:, e], local.at[4 + e]))
+    for store in stores:
+        store.start()
+    pl.semaphore_wait(credit, 1)
+    for i in range(1, dp):
+        for k in range(2):
+            remote(
+                held.at[k, chip],
+                far.at[k, lax.rem(z + dp - i, dp)],
+                o_send.at[i - 1, k],
+                o_recv.at[i - 1, k],
+                to_x,
+            ).wait_recv()
+    fetch = []
+    for i in range(1, dp):
+        for k in range(2):
+            fetch.append(
+                pltpu.make_async_copy(
+                    far.at[k, lax.rem(z + i, dp)], core_in.at[k, i], local.at[6 + (i - 1) * 2 + k]
+                )
+            )
+    for copy in fetch:
+        copy.start()
+    for copy in fetch:
+        copy.wait()
+    for k in range(2):
+        total = total_here(k)
+        for i in range(1, dp):
+            total += core_in[k, i].astype(F32)
+        sums[k] = total
+    for store in stores:
+        store.wait()
+    for i in range(1, dp):
+        far_copy(i).wait_send()
+
+    def settle(s, carry):
+        for copy in (*gather_one(s), *gather_two(s), *gather_core(s)):
+            copy.wait_send()
+        return carry
+
+    lax.fori_loop(0, dp, settle, 0)
+
+
+def expert_pass(x_in, c_all, gates, inner_in, outer_in, ident):
+    dp = lax.axis_size("dp")
+    fsdp = lax.axis_size("fsdp")
+    rows, width = x_in.shape
+    n, four, own_rows, ff_here = inner_in.shape
+    _, two, out_rows, _ = outer_in.shape
+    chunk = fsdp * rows
+    shape = jax.ShapeDtypeStruct
+    dma = pltpu.SemaphoreType.DMA
+    anywhere = pl.BlockSpec(memory_space=pl.ANY)
+    got = pl.pallas_call(
+        functools.partial(expert_kernel, dp),
+        out_shape=(
+            shape((2, rows, width), F32),
+            shape((dp, chunk, 128), F32),
+            shape(inner_in.shape, BF16),
+            shape(outer_in.shape, BF16),
+            shape((dp, fsdp, rows, width), BF16),
+            shape((2, dp, rows, width), BF16),
+        ),
+        in_specs=[anywhere] * 5,
+        out_specs=(pl.BlockSpec(memory_space=pltpu.VMEM),) + (anywhere,) * 5,
+        scratch_shapes=[
+            pltpu.VMEM((chunk, width), BF16),
+            pltpu.VMEM((chunk, width), BF16),
+            pltpu.VMEM((four, n, own_rows, ff_here), BF16),
+            pltpu.VMEM((two, fsdp, out_rows, width), BF16),
+            pltpu.VMEM((four, width, ff_here), F32),
+            pltpu.VMEM((two, ff_here, width), F32),
+            pltpu.VMEM((four, chunk, ff_here), BF16),
+            pltpu.VMEM((two, chunk, ff_here), BF16),
+            pltpu.VMEM((chunk, 128), F32),
+            pltpu.VMEM((2, chunk, width), BF16),
+            pltpu.VMEM((2, 4, rows, width), BF16),
+            pltpu.VMEM((2, 4, rows, width), BF16),
+            pltpu.VMEM((2, 2, rows // 2, width), BF16),
+            pltpu.VMEM((2, 2, rows, width), BF16),
+            dma((12 + 2 * dp,)),
+            dma((dp,)),
+            dma((dp,)),
+            dma((dp, 2)),
+            dma((dp, 2)),
+            dma((dp, 4)),
+            dma((dp, 4)),
+            dma((dp, 4)),
+            dma((dp, 4)),
+            dma((2, 4)),
+            dma((2, 4)),
+            dma((2, 2)),
+            dma((2, 2)),
+            dma((2, 2)),
+            dma((2, 2)),
+            dma((dp, 2)),
+            dma((dp, 2)),
+            pltpu.SemaphoreType.REGULAR,
+        ],
+        compiler_params=pltpu.CompilerParams(
+            collective_id=ident, has_side_effects=True, vmem_limit_bytes=63 * 1024 * 1024
+        ),
+    )(x_in, c_all, gates, inner_in, outer_in)
+    return got[:4]
+
+
+def expert_pass_dense(normed2, grad_all, gates, inner_weight, outer_weight):
+    n, parts, own_rows, ff_here = inner_weight.shape
+    experts_here = parts // 2
+    inner = experts_here * ff_here
+    width = n * own_rows
+    tokens = grad_all.shape[0]
+    gates = gates[:, :, None]
+    rows_all = lax.all_gather(normed2, BOTH, axis=0, tiled=True)
+    inner_block = inner_weight.transpose(0, 2, 1, 3).reshape(width, 2 * inner)
+    outer_shape = outer_weight.shape
+    outer_block = outer_weight.transpose(1, 0, 2, 3).reshape(inner, width)
+    gate_up = dot(rows_all, inner_block, ((1,), (0,)))
+    gate = gate_up[:, :inner]
+    up = gate_up[:, inner:]
+    sigmoid = jax.nn.sigmoid(gate)
+    silu = gate * sigmoid
+    activation = (silu * up).astype(BF16).astype(F32)
+    grad_act = dot(grad_all, outer_block, ((1,), (1,)))
+    grad_gates = jnp.sum(
+        (activation * grad_act).reshape(tokens, experts_here, ff_here), axis=-1
+    )
+    by_part = (tokens, experts_here, ff_here)
+    activation = (activation.reshape(by_part) * gates).reshape(tokens, inner).astype(BF16)
+    grad_act = (grad_act.reshape(by_part) * gates).reshape(tokens, inner)
+    grad_gate_up = jnp.concatenate(
+        [grad_act * up * sigmoid * (1.0 + gate * (1.0 - sigmoid)), grad_act * silu], axis=1
+    ).astype(BF16)
+    expert_sum = dot(activation, outer_block, ((1,), (0,))).astype(BF16)
+    expert_sum = lax.psum_scatter(expert_sum, BOTH, scatter_dimension=0, tiled=True).astype(F32)
+    if tokens > 8192:
+        grad_gate_up, expert_sum = lax.optimization_barrier((grad_gate_up, expert_sum))
+    grad_rows = dot(grad_gate_up, inner_block, ((1,), (1,))).astype(BF16)
+    grad_rows = lax.psum_scatter(grad_rows, BOTH, scatter_dimension=0, tiled=True).astype(F32)
+    inner_grad = dot(rows_all, grad_gate_up, ((0,), (0,))).astype(BF16)
+    outer_grad = dot(activation, grad_all, ((0,), (0,))).astype(BF16)
+    inner_grad = inner_grad.reshape(n, own_rows, parts, ff_here).transpose(0, 2, 1, 3)
+    outer_grad = outer_grad.reshape(experts_here, outer_shape[0], outer_shape[2], width)
+    return expert_sum, grad_rows, grad_gates, inner_grad, outer_grad.transpose(1, 0, 2, 3)
 
 
 def body(
@@ -134,7 +631,6 @@
     experts_here = experts // fsdp
     ff = expert_out.shape[0] * n
     ff_here = ff // dp
-    inner = experts_here * ff_here
     z = lax.axis_index("dp")
     f = lax.axis_index("fsdp")
     valid = lengths[z]
@@ -166,12 +662,13 @@
     qkv_here = attn_weight[:, : 3 * cols]
     out_here = attn_weight[:, 3 * cols :]
 
+    fused = fsdp == 8
     inner_weight = expert_in.reshape(own_rows, fsdp, experts_here, 2, dp, ff_here)
-    inner_weight = inner_weight.transpose(4, 1, 0, 3, 2, 5).reshape(n, own_rows, 2 * inner)
-    inner_weight = lax.all_to_all(inner_weight, BOTH, 0, 0, tiled=True).reshape(width, 2 * inner)
+    inner_weight = inner_weight.transpose(4, 1, 3, 2, 0, 5)
+    inner_weight = inner_weight.reshape(n, 2 * experts_here, own_rows, ff_here)
+    inner_weight = lax.all_to_all(inner_weight, BOTH, 0, 0, tiled=True)
     outer_weight = expert_out.reshape(-1, fsdp, experts_here, width).transpose(1, 2, 0, 3)
     outer_weight = lax.all_to_all(outer_weight, "fsdp", 0, 0, tiled=True)
-    outer_weight = outer_weight.transpose(1, 0, 2, 3).reshape(inner, width)
 
     hidden_all = lax.all_gather(hidden_in, "fsdp", axis=0, tiled=True).astype(F32)
     normed_all = (hidden_all * rms_scale(hidden_all) * gain_attn).astype(BF16)
@@ -229,47 +726,33 @@
     grad_total = cotangent.astype(F32) * live_mask
 
     grad_all = lax.all_gather(grad_total.astype(BF16), BOTH, axis=0, tiled=True)
-    rows_all = lax.all_gather(normed2, BOTH, axis=0, tiled=True)
     gates = (router_probs * chosen).reshape(rows, fsdp, experts_here).transpose(1, 2, 0)
     gates = jnp.broadcast_to(gates[None], (dp, fsdp, experts_here, rows))
     gates = gates.reshape(n, experts_here, rows)
     gates = jnp.pad(gates, ((0, 0), (0, 8 - experts_here), (0, 0)))
     gates = exchange(gates, BOTH, 3, True)[:, :experts_here]
-    gates = gates.transpose(0, 2, 1).reshape(tokens, experts_here, 1)
-    gate_up = dot(rows_all, inner_weight, ((1,), (0,)))
-    gate = gate_up[:, :inner]
-    up = gate_up[:, inner:]
-    sigmoid = jax.nn.sigmoid(gate)
-    silu = gate * sigmoid
-    activation = (silu * up).astype(BF16).astype(F32)
-    grad_act = dot(grad_all, outer_weight, ((1,), (1,)))
-    grad_gates = jnp.sum(
-        (activation * grad_act).reshape(tokens, experts_here, ff_here), axis=-1
-    )
-    by_part = (tokens, experts_here, ff_here)
-    activation = (activation.reshape(by_part) * gates).reshape(tokens, inner).astype(BF16)
-    grad_act = (grad_act.reshape(by_part) * gates).reshape(tokens, inner)
-    grad_gate_up = jnp.concatenate(
-        [grad_act * up * sigmoid * (1.0 + gate * (1.0 - sigmoid)), grad_act * silu], axis=1
-    ).astype(BF16)
-    expert_sum = dot(activation, outer_weight, ((1,), (0,))).astype(BF16)
-    expert_sum = lax.psum_scatter(expert_sum, BOTH, scatter_dimension=0, tiled=True).astype(F32)
-    if tokens > 8192:
-        grad_gate_up, expert_sum = lax.optimization_barrier((grad_gate_up, expert_sum))
-    grad_rows = dot(grad_gate_up, inner_weight, ((1,), (1,))).astype(BF16)
-    grad_rows = lax.psum_scatter(grad_rows, BOTH, scatter_dimension=0, tiled=True).astype(F32)
-    inner_grad = dot(rows_all, grad_gate_up, ((0,), (0,))).astype(BF16)
-    outer_grad = dot(activation, grad_all, ((0,), (0,))).astype(BF16)
+    gates = gates.transpose(0, 2, 1).reshape(tokens, experts_here)
+    if fused:
+        gates = jnp.pad(gates, ((0, 0), (0, 128 - experts_here))).reshape(dp, seq, 128)
+        sums, grad_gates, inner_grad, outer_grad = expert_pass(
+            normed2, grad_all.reshape(dp, seq, width), gates, inner_weight, outer_weight, 8
+        )
+        expert_sum = sums[0]
+        grad_rows = sums[1]
+        grad_gates = grad_gates.reshape(tokens, 128)[:, 8 : 8 + experts_here]
+    else:
+        expert_sum, grad_rows, grad_gates, inner_grad, outer_grad = expert_pass_dense(
+            normed2, grad_all, gates, inner_weight, outer_weight
+        )
     grad_gates = grad_gates.reshape(n, rows, experts_here).transpose(0, 2, 1)
     grad_gates = jnp.pad(grad_gates, ((0, 0), (0, 8 - experts_here), (0, 0)))
     grad_gates = exchange(grad_gates, BOTH, 4, True)[:, :experts_here]
     grad_gates = jnp.sum(grad_gates.reshape(dp, fsdp, experts_here, rows), axis=0)
     grad_router_probs = grad_gates.reshape(experts, rows).transpose(1, 0) * chosen
 
-    inner_grad = lax.all_to_all(inner_grad.reshape(n, own_rows, 2 * inner), BOTH, 0, 0, tiled=True)
-    inner_grad = inner_grad.reshape(dp, fsdp, own_rows, 2, experts_here, ff_here)
-    inner_grad = inner_grad.transpose(2, 1, 4, 3, 0, 5).reshape(own_rows, experts, 2 * ff)
-    outer_grad = outer_grad.reshape(experts_here, fsdp, -1, width).transpose(1, 0, 2, 3)
+    inner_grad = lax.all_to_all(inner_grad, BOTH, 0, 0, tiled=True)
+    inner_grad = inner_grad.reshape(dp, fsdp, 2, experts_here, own_rows, ff_here)
+    inner_grad = inner_grad.transpose(4, 1, 3, 2, 0, 5).reshape(own_rows, experts, 2 * ff)
     outer_grad = lax.all_to_all(outer_grad, "fsdp", 0, 0, tiled=True)
     outer_grad = outer_grad.transpose(2, 0, 1, 3).reshape(-1, experts, width)
 

time: 1440 us -> 1120 us (0.78)
  waiting for transfers between devices: 919 us -> 388 us
  Pallas kernels: 66 us -> 441 us
  matrix products: 193 us -> 61 us
  local copies, waits for them, and re-layouts: 132 us -> 112 us
    reduce_scatter x2 -> x0, waiting for transfers between devices: 355 us -> none  [the longest x1 187 us: body(): lax.psum_scatter(expert_sum, BOTH, scatter_dimension=0, tiled=True)]
    pallas_call x0 -> x1, Pallas kernels: none -> 278 us  [expert_pass(): pl.pallas_call(functools.partial(expert_kernel, dp), out_shape=(shape((2,...]
    all_to_all x2, waiting for transfers between devices: 291 us -> 132 us  [the longest x1 132 us: body(): inner_grad = lax.all_to_all(inner_grad, BOTH, 0, 0, tiled=True)]
    dot_general x12 -> x6, matrix products: 155 us -> 21.1 us  [dot(): return lax.dot_general(a, b, (dims, ((), ())), preferred_element_type=F32)]
    pallas_call x8, Pallas kernels: 66 us -> 163 us  [exchange(): pl.pallas_call(functools.partial(exchange_kernel, axes, n, fsdp, spread),...]
    all_gather x1, waiting for transfers between devices: 80.4 us -> 47.3 us  [body(): grad_all = lax.all_gather(grad_total.astype(BF16), BOTH, axis=0, tiled=True)]
    another operation x2 -> x1, other arithmetic: 17.9 us -> 0.74 us
    all_to_all x1, waiting for transfers between devices: 10.7 us -> 25.2 us  [body(): outer_grad = lax.all_to_all(outer_grad, 'fsdp', 0, 0, tiled=True)]
  transfers between devices with their start and end apart: 15 -> 12, of which waited for: 12 -> 9; matrix products, arithmetic and copies ran while one was open for 14% -> 10% of each run, Pallas kernels for 1% -> 11%
where the time goes in v2:
time: 1120 us; the launch traced here: 1110 us
  Pallas kernels  441 us (39%)
  waiting for transfers between devices  388 us (35%)
  local copies, waits for them, and re-layouts  112 us (10%)
  matrix products  61 us (5%)
  other arithmetic  43.5 us (4%)
  blocking collectives  26.1 us (2%)
  starting transfers between devices  19.8 us (2%)
  between operations  16.1 us (1%)
    pallas_call x1, Pallas kernels, expert_pass(): pl.pallas_call(functools.partial(expert_kernel, dp), out_shape=(shape((2,...  278 us
    pallas_call x8, Pallas kernels, exchange(): pl.pallas_call(functools.partial(exchange_kernel, axes, n, fsdp, spread),...  163 us
    all_to_all x1, waiting for transfers between devices, body(): inner_grad = lax.all_to_all(inner_grad, BOTH, 0, 0, tiled=True)  132 us
    all_gather x1, waiting for transfers between devices, body(): lax.all_gather(attn_weight.reshape(fsdp * own_rows, 4 * cols), 'dp', axis...  78.6 us
    reduce_scatter x1, waiting for transfers between devices, body(): lax.psum_scatter(grad_attended.astype(BF16).reshape(fsdp * seq, cols), 'f...  52.3 us
    all_gather x1, waiting for transfers between devices, body(): grad_all = lax.all_gather(grad_total.astype(BF16), BOTH, axis=0, tiled=True)  47.3 us
    all_to_all x1, blocking collectives, body(): attn_weight = lax.all_to_all(attn_weight, 'fsdp', 0, 0, tiled=True)  26.1 us
    all_to_all x1, waiting for transfers between devices, body(): outer_grad = lax.all_to_all(outer_grad, 'fsdp', 0, 0, tiled=True)  25.2 us
  transfers between devices with their start and end apart: 12, of which 9 were waited for; matrix products, arithmetic and copies ran while one was open for 10% of the time, Pallas kernels for 11%

profile of v2, /device:TPU:0, one launch (start us, length us, event | category | flops | bytes accessed | tf_op | source)
XLA Modules:
  0.0 1108.0 jit_solution(2336204718599389179)
XLA Ops:
  13.0 26.1 %all_to_all.30 = bf16[8,64,1024]{2,1,0:T(8,128)(2,1)} all-to-all(bf16[8,64,1024]{2,1,0:T(8,128)(2,1)S(1)} %reshape.394), channel_id=1, replica_groups=mesh['dp'=4,'fsdp'=8] {'fsdp'}, dimensions={0} | all-to-all | bytes 2097152 | tf_op jit(solution)/shard_map/all_to_all | solution.py:658
  40.1 9.4 shard_map.220
  63.5 78.6 %all-gather.7.cloned.1.call-done = bf16[2048,1024]{1,0:T(8,128)(2,1)} async-done(((bf16[512,1024]{1,0:T(8,128)(2,1)}), bf16[2048,1024]{1,0:T(8,128)(2,1)}) %all-gather.7.cloned.1.call-update) | async-done | bytes 4194320 | tf_op jit(solution)/shard_map/all_gather | solution.py:659
  142.0 6.7 fusion.10
  153.2 5.3 shard_map.221
  166.4 9.6 fusion.64
  189.1 7.8 reshape.407
  196.9 6.5 copy.175
  203.4 15.7 %all-to-all-done.2.outer_in = bf16[8,2,32,2048]{3,2,1,0:T(8,128)(2,1)S(1)} async-done(((bf16[8,2,32,2048]{3,2,1,0:T(8,128)(2,1)}), bf16[8,2,32,2048]{3,2,1,0:T(8,128)(2,1)S(1)}, u32[]{:S(2)}, u32[]{:S(2)}) %all-to-all-start.2) | async-done | bytes 2097184 | tf_op jit(solution)/shard_map/all_to_all | solution.py:671
  226.1 19.4 %all-gather.9.cloned.1.call-done = bf16[8,1024,256]{2,1,0:T(8,128)(2,1)} async-done(((bf16[1,1024,256]{2,1,0:T(8,128)(2,1)}), bf16[8,1024,256]{2,1,0:T(8,128)(2,1)}) %all-gather.9.cloned.1.call-update) | async-done | bytes 4194320 | tf_op jit(solution)/shard_map/all_gather | solution.py:705
  249.8 34.9 %shard_map.222 = bf16[8,128,256]{2,1,0:T(8,128)(2,1)} custom-call(bf16[8,128,256]{2,1,0:T(8,128)(2,1)} %bitcast.219), custom_call_target="tpu_custom_call" | custom-call | tf_op jit(solution)/shard_map/pallas_call | solution.py:80
  288.4 67.4 %shard_map.223 = f32[32,8,128]{2,1,0:T(8,128)} custom-call(f32[32,8,128]{2,1,0:T(8,128)} %pad.20.x), custom_call_target="tpu_custom_call" | custom-call | tf_op jit(solution)/shard_map/pallas_call | solution.py:80
  358.9 47.3 %all-gather.11.cloned.1.call-done = bf16[4096,2048]{1,0:T(8,128)(2,1)} async-done(((bf16[128,2048]{1,0:T(8,128)(2,1)}), bf16[4096,2048]{1,0:T(8,128)(2,1)}) %all-gather.11.cloned.1.call-update) | async-done | bytes 16777232 | tf_op jit(solution)/shard_map/all_gather | solution.py:728
  406.2 278.4 %shard_map.224 = (f32[2,128,2048]{2,1,0:T(8,128)}, f32[4,1024,128]{2,1,0:T(8,128)}, bf16[32,4,64,256]{3,2,1,0:T(8,128)(2,1)}, bf16[8,2,32,2048]{3,2,1,0:T(8,128)...) custom-call(bf16[128,2048]{1,0:T(8,128)(2,1)} %copy-done.11, ...), custom_call_target="tpu_custom_call" | custom-call | tf_op jit(solution)/shard_map/pallas_call | solution.py:513
  688.1 19.6 %shard_map.225 = f32[32,8,128]{2,1,0:T(8,128)} custom-call(f32[32,8,128]{2,1,0:T(8,128)} %pad.22.x), custom_call_target="tpu_custom_call" | custom-call | tf_op jit(solution)/shard_map/pallas_call | solution.py:80
  715.2 8.9 shard_map.226
  728.5 6.5 copy.182
  735.0 52.3 %reduce-scatter.4.cloned.1.call-done = bf16[1024,256]{1,0:T(8,128)(2,1)} async-done(((bf16[8192,256]{1,0:T(8,128)(2,1)}), bf16[1024,256]{1,0:T(8,128)(2,1)}) %reduce-scatter.4.cloned.1.call-update) | async-done | bytes 524304 | tf_op jit(solution)/shard_map/reduce_scatter | solution.py:783
  788.6 5.9 fusion.27
  794.4 4.9 multiply_reduce_fusion
  812.5 5.2 shard_map.227
  827.3 5.1 convolution_convert_fusion
  836.1 6.5 copy.199
  842.5 25.2 %all-to-all-done.5 = bf16[8,2,32,2048]{3,2,1,0:T(8,128)(2,1)S(1)} async-done(((bf16[8,2,32,2048]{3,2,1,0:T(8,128)(2,1)}), bf16[8,2,32,2048]{3,2,1,0:T(8,128)(2,1)S(1)}, u32[]{:S(2)}, u32[]{:S(2)}) %all-to-all-start.5) | async-done | bytes 2097184 | tf_op jit(solution)/shard_map/all_to_all | solution.py:756
  890.1 4.4 copy.204
  894.7 131.8 %all-to-all-done.4 = bf16[32,4,64,256]{3,2,1,0:T(8,128)(2,1)} async-done(((bf16[32,4,64,256]{3,2,1,0:T(8,128)(2,1)}), bf16[32,4,64,256]{3,2,1,0:T(8,128)(2,1)}, u32[]{:S(2)}, u32[]{:S(2)}) %all-to-all-start.4) | async-done | bytes 4194336 | tf_op jit(solution)/shard_map/all_to_all | solution.py:753
  1026.5 6.7 convert_bitcast_fusion
  1033.2 12.0 %copy.202 = f32[64,8,2,2,4,256]{5,4,3,2,1,0:T(4,128)} copy(f32[64,8,2,2,4,256]{5,0,2,3,1,4:T(8,128)} %convert_bitcast_fusion) | data formatting | bytes 16777216 | tf_op jit(solution)/shard_map/convert_element_type | solution.py:847
  1045.2 11.0 reshape.433
  1058.8 11.7 %shard_map.228 = f32[32,16,128]{2,1,0:T(8,128)} custom-call(f32[32,16,128]{2,1,0:T(8,128)} %bitcast.212), custom_call_target="tpu_custom_call" | custom-call | tf_op jit(solution)/shard_map/pallas_call | solution.py:80
  1075.2 4.9 all-to-all-start.3
  1082.0 13.5 %all-to-all-done.3 = bf16[8,64,1024]{2,1,0:T(8,128)(2,1)S(1)} async-done(((bf16[8,64,1024]{2,1,0:T(8,128)(2,1)}), bf16[8,64,1024]{2,1,0:T(8,128)(2,1)S(1)}, u32[]{:S(2)}, u32[]{:S(2)}) %all-to-all-start.3) | async-done | bytes 1048608 | tf_op jit(solution)/shard_map/all_to_all | solution.py:811
  (252 shorter events, 142.8 us)
Async XLA Ops:
  7.2 53.2 %all-gather.5.cloned.1.call-start = ((), (), s32[]{:S(2)}) async-start(), calls=%async_computation.9 | async-start | bytes 4718592 | tf_op jit(solution)/shard_map/all_gather | solution.py:673
  7.9 134.1 %all-gather.7.cloned.1.call-start = ((), (), s32[]{:S(2)}) async-start(), calls=%async_computation.10 | async-start | bytes 5242880 | tf_op jit(solution)/shard_map/all_gather | solution.py:659
  11.1 28.1 %copy-start.37 = (bf16[64,16]{0,1:T(8,128)(2,1)S(1)}, bf16[64,16]{0,1:T(8,128)(2,1)}, u32[]{:S(2)}) copy-start(bf16[64,16]{0,1:T(8,128)(2,1)} %param.22) | copy-start | bytes 6148
  11.1 28.3 %copy-start.39 = (bf16[64]{0:T(256)(128)(2,1)S(1)}, bf16[64]{0:T(256)(128)(2,1)}, u32[]{:S(2)}) copy-start(bf16[64]{0:T(256)(128)(2,1)} %param.16) | copy-start | bytes 388
  11.1 28.3 %copy-start.40 = (bf16[64]{0:T(256)(128)(2,1)S(1)}, bf16[64]{0:T(256)(128)(2,1)}, u32[]{:S(2)}) copy-start(bf16[64]{0:T(256)(128)(2,1)} %param.17) | copy-start | bytes 388
  11.1 28.3 %copy-start.41 = (bf16[64]{0:T(256)(128)(2,1)S(1)}, bf16[64]{0:T(256)(128)(2,1)}, u32[]{:S(2)}) copy-start(bf16[64]{0:T(256)(128)(2,1)} %param.18) | copy-start | bytes 388
  11.1 28.3 %copy-start.42 = (bf16[64]{0:T(256)(128)(2,1)S(1)}, bf16[64]{0:T(256)(128)(2,1)}, u32[]{:S(2)}) copy-start(bf16[64]{0:T(256)(128)(2,1)} %param.19) | copy-start | bytes 388
  11.2 39.9 %copy-start.43 = (s32[4]{0:T(128)S(1)}, s32[4]{0:T(128)}, u32[]{:S(2)}) copy-start(s32[4]{0:T(128)} %param.14) | copy-start | bytes 52
  39.1 206.5 %all-gather.9.cloned.1.call-start = ((), (), s32[]{:S(2)}) async-start(), calls=%async_computation.11 | async-start | bytes 4718592 | tf_op jit(solution)/shard_map/all_gather | solution.py:705
  165.1 10.9 copy-start.4
  166.4 9.7 copy-start.29
  181.3 224.9 %all-gather.11.cloned.1.call-start = ((), (), s32[]{:S(2)}) async-start(), calls=%async_computation.12 | async-start | bytes 17301504 | tf_op jit(solution)/shard_map/all_gather | solution.py:728
  185.5 33.7 %all-to-all-start.2 = ((bf16[8,2,32,2048]{3,2,1,0:T(8,128)(2,1)}), bf16[8,2,32,2048]{3,2,1,0:T(8,128)(2,1)S(1)}, u32[]{:S(2)}, u32[]{:S(2)}) async-start(bf16[8,2,32,2048]{3,2,1,0:T(8,128)(2,1)} %bitcast.194), calls=%async_computation.2 | async-start | bytes 4194304 | tf_op jit(solution)/shard_map/all_to_all | solution.py:671
  220.5 138.4 %all-to-all-start.1 = ((bf16[32,4,64,256]{3,2,1,0:T(8,128)(2,1)}), bf16[32,4,64,256]{3,2,1,0:T(8,128)(2,1)}, u32[]{:S(2)}, u32[]{:S(2)}) async-start(bf16[32,4,64,256]{3,2,1,0:T(8,128)(2,1)} %bitcast.187), calls=%async_computation.1 | async-start | bytes 8388608 | tf_op jit(solution)/shard_map/all_to_all | solution.py:669
  224.0 563.3 %reduce-scatter.4.cloned.1.call-start = ((), (), s32[]{:S(2)}) async-start(), calls=%async_computation.13 | async-start | bytes 4718592 | tf_op jit(solution)/shard_map/reduce_scatter | solution.py:783
  224.6 62.8 %copy-start.28 = (bf16[2048,16]{1,0:T(8,128)(2,1)}, bf16[2048,16]{1,0:T(8,128)(2,1)S(1)}, u32[]{:S(2)}) copy-start(bf16[2048,16]{1,0:T(8,128)(2,1)S(1)} %reshape.402) | copy-start | bytes 196612
  226.1 19.5 %copy-start.20 = (bf16[2048,256]{1,0:T(8,128)(2,1)}, bf16[2048,256]{1,0:T(8,128)(2,1)S(1)}, u32[]{:S(2)}) copy-start(bf16[2048,256]{1,0:T(8,128)(2,1)S(1)} %slice.144) | copy-start | bytes 3145732
  249.8 36.1 %copy-start.13 = (bf16[128,2048]{1,0:T(8,128)(2,1)S(1)}, bf16[128,2048]{1,0:T(8,128)(2,1)}, u32[]{:S(2)}) copy-start(bf16[128,2048]{1,0:T(8,128)(2,1)} %param.13) | copy-start | bytes 1572868
  287.4 118.8 %copy-start.11 = (bf16[128,2048]{1,0:T(8,128)(2,1)}, bf16[128,2048]{1,0:T(8,128)(2,1)S(1)}, u32[]{:S(2)}) copy-start(bf16[128,2048]{1,0:T(8,128)(2,1)S(1)} %multiply_convert_fusion.1.x_in) | copy-start | bytes 1572868
  684.5 24.2 %copy-start.9 = (f32[128,2048]{1,0:T(8,128)S(1)}, f32[128,2048]{1,0:T(8,128)}, u32[]{:S(2)}) copy-start(f32[128,2048]{1,0:T(8,128)} %copy-done.8) | copy-start | bytes 3145732
  687.4 25.1 %copy-start.25 = (bf16[128,2048]{1,0:T(8,128)(2,1)S(1)}, bf16[128,2048]{1,0:T(8,128)(2,1)}, u32[]{:S(2)}) copy-start(bf16[128,2048]{1,0:T(8,128)(2,1)} %param.25) | copy-start | bytes 1572868
  712.5 11.6 %copy-start.21 = (bf16[2048,256]{1,0:T(8,128)(2,1)S(1)}, bf16[2048,256]{1,0:T(8,128)(2,1)}, u32[]{:S(2)}) copy-start(bf16[2048,256]{1,0:T(8,128)(2,1)} %copy-done.20) | copy-start | bytes 3145732
  735.0 321.2 %reduce-scatter.6.cloned.1.call-start = ((), (), s32[]{:S(2)}) async-start(), calls=%async_computation.14 | async-start | bytes 4718592 | tf_op jit(solution)/shard_map/reduce_scatter | solution.py:804
  788.6 10.7 slice-start
  809.4 14.5 %copy-start.3 = (f32[1024,768]{0,1:T(8,128)S(1)}, f32[1024,768]{0,1:T(8,128)}, u32[]{:S(2)}) copy-start(f32[1024,768]{0,1:T(8,128)} %copy-done.2) | copy-start | bytes 9437188
  832.4 35.3 %all-to-all-start.5 = ((bf16[8,2,32,2048]{3,2,1,0:T(8,128)(2,1)}), bf16[8,2,32,2048]{3,2,1,0:T(8,128)(2,1)S(1)}, u32[]{:S(2)}, u32[]{:S(2)}) async-start(bf16[8,2,32,2048]{3,2,1,0:T(8,128)(2,1)} %get-tuple-element.19), calls=%async_computation.8 | async-start | bytes 4194304 | tf_op jit(solution)/shard_map/all_to_all | solution.py:756
  867.8 158.7 %all-to-all-start.4 = ((bf16[32,4,64,256]{3,2,1,0:T(8,128)(2,1)}), bf16[32,4,64,256]{3,2,1,0:T(8,128)(2,1)}, u32[]{:S(2)}, u32[]{:S(2)}) async-start(bf16[32,4,64,256]{3,2,1,0:T(8,128)(2,1)} %get-tuple-element.18), calls=%async_computation.7 | async-start | bytes 8388608 | tf_op jit(solution)/shard_map/all_to_all | solution.py:753
  871.7 201.3 %reduce-scatter.8.cloned.1.call-start = ((), (), s32[]{:S(2)}) async-start(), calls=%async_computation.15 | async-start | bytes 5242880 | tf_op jit(solution)/shard_map/reduce_scatter | solution.py:809
  1045.2 11.0 copy-start.14
  1056.1 24.4 %copy-start.18 = (f32[128,2048]{1,0:T(8,128)S(1)}, f32[128,2048]{1,0:T(8,128)}, u32[]{:S(2)}) copy-start(f32[128,2048]{1,0:T(8,128)} %get-tuple-element.95) | copy-start | bytes 3145732
  1056.2 24.4 %copy-start.27 = (bf16[128,2048]{1,0:T(8,128)(2,1)S(1)}, bf16[128,2048]{1,0:T(8,128)(2,1)}, u32[]{:S(2)}) copy-start(bf16[128,2048]{1,0:T(8,128)(2,1)} %reduce-scatter.6.cloned.1.call-done) | copy-start | bytes 1572868
  1075.2 20.3 %all-to-all-start.3 = ((bf16[8,64,1024]{2,1,0:T(8,128)(2,1)}), bf16[8,64,1024]{2,1,0:T(8,128)(2,1)S(1)}, u32[]{:S(2)}, u32[]{:S(2)}) async-start(bf16[8,64,1024]{2,1,0:T(8,128)(2,1)} %bitcast.202), calls=%async_computation.6 | async-start | bytes 2097152 | tf_op jit(solution)/shard_map/all_to_all | solution.py:811
  (28 other events, 85.3 us)
Sparse Core Ops, SparseCore 0:
  9.9 50.4 all-gather.4
  62.0 80.0 all-gather.6
  181.4 64.1 all-gather.8
  248.3 157.8 all-gather.10
  735.1 52.1 reduce-scatter.3
  832.6 75.2 reduce-scatter.5
  910.2 116.2 reduce-scatter.7

commit v3 on v2

--- a/solution.py
+++ b/solution.py
@@ -104,6 +104,977 @@
 
 def dot(a, b, dims):
     return lax.dot_general(a, b, (dims, ((), ())), preferred_element_type=F32)
+
+
+HIGH = lax.Precision.HIGHEST
+
+
+def remote(src, dst, send, recv, device):
+    return pltpu.make_async_remote_copy(
+        src, dst, send, recv, device_id=device, device_id_type=MESH_ID
+    )
+
+
+def greet_all(n, fsdp, me):
+    barrier = pltpu.get_barrier_semaphore()
+    for k in range(1, n):
+        peer = place(BOTH, fsdp, lax.rem(me + k, n))
+        pl.semaphore_signal(barrier, inc=1, device_id=peer, device_id_type=MESH_ID)
+    pl.semaphore_wait(barrier, n - 1)
+
+
+class Plane:
+    def __init__(self, f):
+        self.f = f
+        self.core = lax.rem(f, 2)
+        self.chip = f // 2
+        xbit = lax.rem(self.chip, 2)
+        ybit = self.chip // 2
+        self.chip_x = ybit * 2 + (1 - xbit)
+        self.chip_y = (1 - ybit) * 2 + xbit
+        self.chip_d = (1 - ybit) * 2 + (1 - xbit)
+        self.fx = self.chip_x * 2 + self.core
+        self.fy = self.chip_y * 2 + self.core
+        self.fd = self.chip_d * 2 + self.core
+        self.to_x = {"fsdp": self.fx}
+        self.to_y = {"fsdp": self.fy}
+        self.to_c = {"fsdp": self.chip * 2 + 1 - self.core}
+
+
+class PlaneSum:
+    def __init__(self, plane, part, held, core_in, half_in, full_in, send, recv):
+        self.plane = plane
+        self.part = part
+        self.held = held
+        self.core_in = core_in
+        self.half_in = half_in
+        self.full_in = full_in
+        self.send = send
+        self.recv = recv
+        half = held.shape[1] // 2
+        self.upper = pl.ds(0, half)
+        self.lower = pl.ds(half, half)
+
+    def core_copy(self, j):
+        owner = j * 2 + 1 - self.plane.core
+        return remote(
+            self.part.at[owner],
+            self.core_in.at[j],
+            self.send.at[j],
+            self.recv.at[j],
+            self.plane.to_c,
+        )
+
+    def half_copies(self):
+        block = self.held.at[self.plane.chip_d]
+        send, recv, half_in = self.send, self.recv, self.half_in
+        return (
+            remote(block.at[self.upper], half_in.at[0], send.at[4], recv.at[4], self.plane.to_x),
+            remote(block.at[self.lower], half_in.at[1], send.at[5], recv.at[5], self.plane.to_y),
+        )
+
+    def full_copies(self):
+        held, full_in, send, recv = self.held, self.full_in, self.send, self.recv
+        plane = self.plane
+        return (
+            remote(held.at[plane.chip_x], full_in.at[0], send.at[6], recv.at[6], plane.to_x),
+            remote(held.at[plane.chip_y], full_in.at[1], send.at[7], recv.at[7], plane.to_y),
+        )
+
+    def start(self):
+        for j in range(4):
+            self.core_copy(j).start()
+
+    def add_core(self):
+        for j in range(4):
+            self.core_copy(j).wait()
+
+        def one(j, carry):
+            own = self.part[j * 2 + self.plane.core].astype(F32)
+            self.held[j] = (own + self.core_in[j].astype(F32)).astype(BF16)
+            return carry
+
+        lax.fori_loop(0, 4, one, 0)
+        for copy in self.half_copies():
+            copy.start()
+
+    def pass_on(self):
+        for copy in self.half_copies():
+            copy.wait()
+        held, half_in = self.held, self.half_in
+        for chip, piece, i in (
+            (self.plane.chip_y, self.upper, 0),
+            (self.plane.chip_x, self.lower, 1),
+        ):
+            total = held[chip, piece].astype(F32) + half_in[i].astype(F32)
+            held[chip, piece] = total.astype(BF16)
+        for copy in self.full_copies():
+            copy.start()
+
+    def total(self):
+        for copy in self.full_copies():
+            copy.wait()
+        total = self.held[self.plane.chip].astype(F32)
+        return total + self.full_in[0].astype(F32) + self.full_in[1].astype(F32)
+
+
+class PlaneGather:
+    def __init__(self, plane, block, rows, send, recv):
+        self.plane = plane
+        self.block = block
+        self.send = send
+        self.recv = recv
+        self.upper = pl.ds(0, rows // 2)
+        self.lower = pl.ds(rows // 2, rows // 2)
+
+    def same(self, ref, i, device):
+        return remote(ref, ref, self.send(i), self.recv(i), device)
+
+    def first(self):
+        own = self.block(self.plane.f)
+        return (
+            self.same(own.at[self.upper], 0, self.plane.to_x),
+            self.same(own.at[self.lower], 1, self.plane.to_y),
+        )
+
+    def second(self):
+        plane = self.plane
+        return (
+            self.same(self.block(plane.f).at[self.upper], 2, plane.to_y),
+            self.same(self.block(plane.fx).at[self.upper], 3, plane.to_y),
+            self.same(self.block(plane.f).at[self.lower], 4, plane.to_x),
+            self.same(self.block(plane.fy).at[self.lower], 5, plane.to_x),
+        )
+
+    def third(self):
+        plane = self.plane
+        owners = (plane.f, plane.fx, plane.fy, plane.fd)
+        return [self.same(self.block(o), 6 + i, plane.to_c) for i, o in enumerate(owners)]
+
+    def start(self):
+        for copy in self.first():
+            copy.start()
+
+    def middle(self):
+        for copy in self.first():
+            copy.wait_recv()
+        for copy in self.second():
+            copy.start()
+
+    def finish(self):
+        for copy in self.second():
+            copy.wait_recv()
+        for copy in self.third():
+            copy.start()
+
+    def wait(self):
+        for copy in self.third():
+            copy.wait_recv()
+
+    def settle(self):
+        for copy in (*self.first(), *self.second(), *self.third()):
+            copy.wait_send()
+
+
+def attention_kernel(
+    dp,
+    fsdp,
+    hidden,
+    cot,
+    weight_in,
+    inner_in,
+    outer_in,
+    gain_attn,
+    gain,
+    turn,
+    live,
+    branch,
+    qkv,
+    unit,
+    scale,
+    normed,
+    weight,
+    attended,
+    c_all,
+    inner_out,
+    outer_out,
+    hid_v,
+    normed_v,
+    w_v,
+    raw,
+    stat,
+    stat_in,
+    att_v,
+    cols_v,
+    rows_v,
+    local,
+    w_send,
+    w_recv,
+    right_send,
+    right_recv,
+    left_send,
+    left_recv,
+    h_send,
+    h_recv,
+    t_send,
+    t_recv,
+    a_send,
+    a_recv,
+    b_send,
+    b_recv,
+    c_send,
+    c_recv,
+    z_send,
+    z_recv,
+    in_send,
+    in_recv,
+    out_send,
+    out_recv,
+):
+    n = dp * fsdp
+    z = lax.axis_index("dp")
+    f = lax.axis_index("fsdp")
+    me = z * fsdp + f
+    plane = Plane(f)
+    rows, width = hidden.shape
+    seq, cols = cols_v.shape
+    own_rows = weight_in.shape[1]
+    slab = fsdp * own_rows
+    scaling = HEAD_DIM ** (-0.5)
+    greet_all(n, fsdp, me)
+
+    def weight_rows(index):
+        return pl.ds(pl.multiple_of(index * own_rows, own_rows), own_rows)
+
+    def weight_copy(k):
+        target = lax.rem(f + k, fsdp)
+        return remote(
+            weight_in.at[target],
+            w_v.at[weight_rows(me)],
+            w_send.at[k],
+            w_recv.at[k],
+            {"fsdp": target},
+        )
+
+    def slab_copy(p, near, far, send, recv):
+        ref = w_v.at[pl.ds(pl.multiple_of(p * slab, slab), slab)]
+        return remote(ref, ref, send.at[near], recv.at[near], {"dp": far})
+
+    def inner_copy(k):
+        target = lax.rem(me + k, n)
+        return remote(
+            inner_in.at[target],
+            inner_out.at[me],
+            in_send.at[k],
+            in_recv.at[k],
+            place(BOTH, fsdp, target),
+        )
+
+    def outer_copy(k):
+        target = lax.rem(f + k, fsdp)
+        return remote(
+            outer_in.at[target], outer_out.at[f], out_send.at[k], out_recv.at[k], {"fsdp": target}
+        )
+
+    def cot_copy(i):
+        return remote(
+            cot,
+            c_all.at[z, f],
+            z_send.at[i],
+            z_recv.at[i],
+            {"dp": lax.rem(z + dp - i, dp)},
+        )
+
+    hidden_gather = PlaneGather(
+        plane, lambda o: hid_v.at[o], rows, lambda i: h_send.at[i], lambda i: h_recv.at[i]
+    )
+    attended_gather = PlaneGather(
+        plane, lambda o: att_v.at[o], seq, lambda i: a_send.at[i], lambda i: a_recv.at[i]
+    )
+    cot_gather = [
+        PlaneGather(
+            plane,
+            lambda o, s=s: c_all.at[lax.rem(z + 1 + s, dp), o],
+            rows,
+            lambda i, s=s: c_send.at[s, i],
+            lambda i, s=s: c_recv.at[s, i],
+        )
+        for s in range(dp)
+    ]
+
+    keeps = [
+        pltpu.make_async_copy(hidden, hid_v.at[f], local.at[0]),
+        pltpu.make_async_copy(weight_in.at[f], w_v.at[weight_rows(me)], local.at[1]),
+        pltpu.make_async_copy(cot, c_all.at[z, f], local.at[2]),
+        pltpu.make_async_copy(inner_in.at[me], inner_out.at[me], local.at[3]),
+        pltpu.make_async_copy(outer_in.at[f], outer_out.at[f], local.at[4]),
+    ]
+    for copy in keeps:
+        copy.start()
+    for k in range(1, fsdp):
+        weight_copy(k).start()
+    keeps[0].wait()
+    hidden_gather.start()
+    keeps[1].wait()
+    for k in range(1, fsdp):
+        weight_copy(k).wait_recv()
+
+    @pl.when(z < dp - 1)
+    def _():
+        slab_copy(z, 1, z + 1, right_send, right_recv).start()
+
+    @pl.when(z > 0)
+    def _():
+        slab_copy(z, 1, z - 1, left_send, left_recv).start()
+
+    hidden_gather.middle()
+    keeps[2].wait()
+    cot_gather[dp - 1].start()
+    hidden_gather.finish()
+    for k in range(1, fsdp):
+        outer_copy(k).start()
+    hidden_gather.wait()
+
+    def norm_rows(i, carry):
+        values = hid_v[i].astype(F32)
+        values = values * lax.rsqrt(jnp.mean(values * values, axis=-1, keepdims=True) + EPS)
+        r = pl.ds(pl.multiple_of(i * rows, rows), rows)
+        normed_v[r, :] = (values * gain_attn[0:1, :]).astype(BF16)
+        return carry
+
+    lax.fori_loop(0, fsdp, norm_rows, 0)
+    normed_store = pltpu.make_async_copy(normed_v, normed, local.at[0])
+    normed_store.start()
+
+    for d in range(1, dp):
+
+        @pl.when(z >= d)
+        def _(d=d):
+            slab_copy(z - d, d, 0, right_send, right_recv).wait_recv()
+
+            @pl.when(z < dp - 1)
+            def _():
+                slab_copy(z - d, d + 1, z + 1, right_send, right_recv).start()
+
+        @pl.when(z + d < dp)
+        def _(d=d):
+            slab_copy(z + d, d, 0, left_send, left_recv).wait_recv()
+
+            @pl.when(z > 0)
+            def _():
+                slab_copy(z + d, d + 1, z - 1, left_send, left_recv).start()
+
+        if d == 1:
+            cot_gather[dp - 1].middle()
+        if d == 2:
+            cot_gather[dp - 1].finish()
+
+    for i in range(1, dp):
+        cot_copy(i).start()
+    for k in range(1, n):
+        inner_copy(k).start()
+    weight_store = pltpu.make_async_copy(w_v, weight, local.at[1])
+    weight_store.start()
+
+    tile = 256
+
+    def project(i, carry):
+        r = pl.ds(pl.multiple_of(i * tile, tile), tile)
+        for j in range(3):
+            col = pl.ds(j * cols, cols)
+            value = dot(normed_v[r, :], w_v[:, col], ((1,), (0,)))
+            if j < 2:
+                raw[r, col] = value
+            else:
+                qkv[2, r, :] = value.astype(BF16)
+        return carry
+
+    lax.fori_loop(0, seq // tile, project, 0)
+    row = lax.broadcasted_iota(jnp.int32, (8, 2 * cols), 0)
+    lane_of = lax.broadcasted_iota(jnp.int32, (8, 2 * cols), 1)
+    chooser = jnp.where(lane_of // cols == row, 1.0, 0.0).astype(F32)
+    stat[...] = lax.dot_general(
+        chooser,
+        raw[...] * raw[...],
+        (((1,), (1,)), ((), ())),
+        precision=HIGH,
+        preferred_element_type=F32,
+    )
+
+    def stat_copy(k):
+        return remote(
+            stat, stat_in.at[f], t_send.at[k], t_recv.at[k], {"fsdp": lax.rem(f + k, fsdp)}
+        )
+
+    for k in range(1, fsdp):
+        stat_copy(k).start()
+    stat_in[f] = stat[...]
+    for k in range(1, fsdp):
+        stat_copy(k).wait_recv()
+    sums = stat_in[0]
+    for i in range(1, fsdp):
+        sums = sums + stat_in[i]
+    corner = jnp.where(
+        lax.broadcasted_iota(jnp.int32, (8, 128), 0) == lax.broadcasted_iota(jnp.int32, (8, 128), 1),
+        1.0 / width,
+        0.0,
+    ).astype(F32)
+    means = lax.dot_general(
+        sums, corner, (((0,), (0,)), ((), ())), precision=HIGH, preferred_element_type=F32
+    )
+    scale[...] = lax.rsqrt(means + EPS)
+    for i in range(2):
+        wide = pl.ds(i * cols, cols)
+        unit[:, wide] = raw[:, wide] * scale[:, i : i + 1]
+        for h in range(cols // HEAD_DIM):
+            lane = pl.ds(i * cols + h * HEAD_DIM, HEAD_DIM)
+            values = unit[:, lane] * gain[0:1, lane]
+            values = values * turn[0] - pltpu.roll(values, HEAD_DIM // 2, 1) * turn[1]
+            qkv[i, :, pl.ds(h * HEAD_DIM, HEAD_DIM)] = values.astype(BF16)
+
+    def head(h, carry):
+        lane = pl.ds(pl.multiple_of(h * HEAD_DIM, HEAD_DIM), HEAD_DIM)
+        for t in range(seq // tile):
+            r = pl.ds(t * tile, tile)
+            extent = (t + 1) * tile
+            upto = pl.ds(0, extent)
+            scores = dot(qkv[0, r, lane], qkv[1, upto, lane], ((1,), (1,))) * scaling
+            q_pos = t * tile + lax.broadcasted_iota(jnp.int32, (tile, extent), 0)
+            k_pos = lax.broadcasted_iota(jnp.int32, (tile, extent), 1)
+            allowed = (k_pos <= q_pos) & (live[0:1, 0:extent] > 0.0)
+            masked = jnp.where(allowed, scores, -1e30)
+            weights = jnp.exp(masked - jnp.max(masked, axis=-1, keepdims=True))
+            weights = jnp.where(allowed, weights, 0.0)
+            probs = weights / jnp.sum(weights, axis=-1, keepdims=True)
+            att_v[f, r, lane] = dot(
+                probs.astype(BF16), qkv[2, upto, lane], ((1,), (0,))
+            ).astype(BF16)
+        return carry
+
+    lax.fori_loop(0, cols // HEAD_DIM, head, 0)
+    attended_gather.start()
+    for s in range(dp - 1):
+        cot_copy(s + 1).wait_recv()
+        cot_gather[s].start()
+        if s == 0:
+            attended_gather.middle()
+    cot_gather[0].middle()
+    attended_gather.finish()
+    for s in range(1, dp - 1):
+        cot_gather[s].middle()
+    attended_gather.wait()
+    attended_store = pltpu.make_async_copy(att_v, attended, local.at[2])
+    attended_store.start()
+
+    out_cols = pl.ds(3 * cols, cols)
+
+    def project_out(i, carry):
+        r = pl.ds(pl.multiple_of(i * tile, tile), tile)
+        total = dot(att_v[0, r, :], w_v[pl.ds(0, cols), out_cols], ((1,), (0,)))
+        for j in range(1, fsdp):
+            total += dot(att_v[j, r, :], w_v[pl.ds(j * cols, cols), out_cols], ((1,), (0,)))
+        cols_v[r, :] = total.astype(BF16)
+        return carry
+
+    lax.fori_loop(0, seq // tile, project_out, 0)
+
+    def branch_copy(k):
+        target = lax.rem(f + k, fsdp)
+        return remote(
+            cols_v.at[pl.ds(pl.multiple_of(target * rows, rows), rows)],
+            rows_v.at[f],
+            b_send.at[k],
+            b_recv.at[k],
+            {"fsdp": target},
+        )
+
+    for k in range(1, fsdp):
+        branch_copy(k).start()
+    rows_v[f] = cols_v[pl.ds(pl.multiple_of(f * rows, rows), rows), :]
+    for s in range(dp - 1):
+        cot_gather[s].finish()
+    for k in range(1, fsdp):
+        branch_copy(k).wait()
+    for i in range(fsdp):
+        branch[:, pl.ds(i * cols, cols)] = rows_v[i]
+
+    for s in range(dp):
+        cot_gather[s].wait()
+        cot_gather[s].settle()
+    hidden_gather.settle()
+    attended_gather.settle()
+    for i in range(1, dp):
+        cot_copy(i).wait_send()
+
+    @pl.when(z < dp - 1)
+    def _():
+        slab_copy(z, 1, z + 1, right_send, right_recv).wait_send()
+
+    @pl.when(z > 0)
+    def _():
+        slab_copy(z, 1, z - 1, left_send, left_recv).wait_send()
+
+    for d in range(1, dp):
+
+        @pl.when((z >= d) & (z < dp - 1))
+        def _(d=d):
+            slab_copy(z - d, d + 1, z + 1, right_send, right_recv).wait_send()
+
+        @pl.when((z + d < dp) & (z > 0))
+        def _(d=d):
+            slab_copy(z + d, d + 1, z - 1, left_send, left_recv).wait_send()
+
+    for k in range(1, fsdp):
+        weight_copy(k).wait_send()
+        stat_copy(k).wait_send()
+        outer_copy(k).wait()
+    for k in range(1, n):
+        inner_copy(k).wait()
+    for copy in keeps[3:]:
+        copy.wait()
+    normed_store.wait()
+    weight_store.wait()
+    attended_store.wait()
+
+
+def attention_forward(
+    hidden, cot, weight_in, inner_in, outer_in, gain_attn, gain, turn, live, ident
+):
+    dp = lax.axis_size("dp")
+    fsdp = lax.axis_size("fsdp")
+    n = dp * fsdp
+    rows, width = hidden.shape
+    seq = rows * fsdp
+    cols = width // fsdp
+    shape = jax.ShapeDtypeStruct
+    dma = pltpu.SemaphoreType.DMA
+    vmem = pltpu.VMEM
+    anywhere = pl.BlockSpec(memory_space=pl.ANY)
+    inside = pl.BlockSpec(memory_space=pltpu.VMEM)
+    pairs = [fsdp, dp + 1, dp + 1, 10, fsdp, 10, fsdp]
+    sems = []
+    for size in pairs:
+        sems += [dma((size,)), dma((size,))]
+    sems += [dma((dp, 10)), dma((dp, 10))]
+    for size in (dp, n, fsdp):
+        sems += [dma((size,)), dma((size,))]
+    return pl.pallas_call(
+        functools.partial(attention_kernel, dp, fsdp),
+        out_shape=(
+            shape((rows, width), BF16),
+            shape((3, seq, cols), BF16),
+            shape((seq, 2 * cols), F32),
+            shape((seq, 128), F32),
+            shape((seq, width), BF16),
+            shape((width, 4 * cols), BF16),
+            shape((fsdp, seq, cols), BF16),
+            shape((dp, fsdp, rows, width), BF16),
+            shape(inner_in.shape, BF16),
+            shape(outer_in.shape, BF16),
+        ),
+        in_specs=[anywhere] * 5 + [inside] * 4,
+        out_specs=(inside,) * 4 + (anywhere,) * 6,
+        scratch_shapes=[
+            vmem((fsdp, rows, width), BF16),
+            vmem((seq, width), BF16),
+            vmem((width, 4 * cols), BF16),
+            vmem((seq, 2 * cols), F32),
+            vmem((8, seq), F32),
+            vmem((fsdp, 8, seq), F32),
+            vmem((fsdp, seq, cols), BF16),
+            vmem((seq, cols), BF16),
+            vmem((fsdp, rows, cols), BF16),
+            dma((5,)),
+            *sems,
+        ],
+        compiler_params=pltpu.CompilerParams(
+            collective_id=ident, has_side_effects=True, vmem_limit_bytes=63 * 1024 * 1024
+        ),
+    )(hidden, cot, weight_in, inner_in, outer_in, gain_attn, gain, turn, live)
+
+
+def attention_back_kernel(
+    dp,
+    fsdp,
+    grad_rows,
+    attended,
+    weight,
+    normed,
+    qkv,
+    unit,
+    scale,
+    gain,
+    turn,
+    live,
+    inner_in,
+    outer_in,
+    grad_normed,
+    terms,
+    owned,
+    inner_out,
+    outer_out,
+    att_v,
+    w_v,
+    normed_v,
+    gcols,
+    part1,
+    held1,
+    core1,
+    half1,
+    full1,
+    part2,
+    held2,
+    core2,
+    half2,
+    full2,
+    gatt,
+    gq,
+    gk,
+    gval,
+    gqk,
+    gqkv,
+    stat,
+    stat_in,
+    wgrad,
+    z_in,
+    wsum,
+    local,
+    in_send,
+    in_recv,
+    out_send,
+    out_recv,
+    g_send,
+    g_recv,
+    s1_send,
+    s1_recv,
+    s2_send,
+    s2_recv,
+    t_send,
+    t_recv,
+    zo_send,
+    zo_recv,
+    zq_send,
+    zq_recv,
+    w_send,
+    w_recv,
+):
+    n = dp * fsdp
+    z = lax.axis_index("dp")
+    f = lax.axis_index("fsdp")
+    me = z * fsdp + f
+    plane = Plane(f)
+    rows, width = grad_rows.shape
+    seq, cols = gcols.shape
+    own_rows = inner_in.shape[2]
+    slab = fsdp * own_rows
+    scaling = HEAD_DIM ** (-0.5)
+    greet_all(n, fsdp, me)
+
+    loads = [
+        pltpu.make_async_copy(attended, att_v, local.at[0]),
+        pltpu.make_async_copy(weight, w_v, local.at[1]),
+        pltpu.make_async_copy(normed, normed_v, local.at[2]),
+        pltpu.make_async_copy(
+            grad_rows.at[:, pl.ds(pl.multiple_of(f * cols, cols), cols)],
+            gcols.at[pl.ds(pl.multiple_of(f * rows, rows), rows)],
+            local.at[3],
+        ),
+    ]
+    keeps = [
+        pltpu.make_async_copy(inner_in.at[me], inner_out.at[me], local.at[4]),
+        pltpu.make_async_copy(outer_in.at[f], outer_out.at[f], local.at[5]),
+    ]
+    for copy in loads:
+        copy.start()
+
+    def cols_copy(k):
+        target = lax.rem(f + k, fsdp)
+        return remote(
+            grad_rows.at[:, pl.ds(pl.multiple_of(target * cols, cols), cols)],
+            gcols.at[pl.ds(pl.multiple_of(f * rows, rows), rows)],
+            g_send.at[k],
+            g_recv.at[k],
+            {"fsdp": target},
+        )
+
+    def inner_copy(k):
+        target = lax.rem(me + k, n)
+        return remote(
+            inner_in.at[target],
+            inner_out.at[me],
+            in_send.at[k],
+            in_recv.at[k],
+            place(BOTH, fsdp, target),
+        )
+
+    def outer_copy(k):
+        target = lax.rem(f + k, fsdp)
+        return remote(
+            outer_in.at[target], outer_out.at[f], out_send.at[k], out_recv.at[k], {"fsdp": target}
+        )
+
+    def slab_rows(p):
+        return pl.ds(pl.multiple_of(p * slab, slab), slab)
+
+    def far_copy(i, col, send, recv):
+        p = lax.rem(z + i, dp)
+        return remote(
+            wgrad.at[slab_rows(p), col], z_in.at[i, :, col], send.at[i], recv.at[i], {"dp": p}
+        )
+
+    qkv_cols = pl.ds(0, 3 * cols)
+    out_cols = pl.ds(3 * cols, cols)
+
+    for k in range(1, fsdp):
+        cols_copy(k).start()
+    for k in range(1, n):
+        inner_copy(k).start()
+    for k in range(1, fsdp):
+        outer_copy(k).start()
+    for copy in keeps:
+        copy.start()
+    for copy in loads:
+        copy.wait()
+    for k in range(1, fsdp):
+        cols_copy(k).wait_recv()
+
+    def attended_back(i, carry):
+        block = pl.ds(pl.multiple_of(i * cols, cols), cols)
+        part1[i] = dot(gcols[...], w_v[block, out_cols], ((1,), (1,))).astype(BF16)
+        return carry
+
+    lax.fori_loop(0, fsdp, attended_back, 0)
+    sum1 = PlaneSum(plane, part1, held1, core1, half1, full1, s1_send, s1_recv)
+    sum1.start()
+
+    def out_grads(i, carry):
+        block = pl.ds(pl.multiple_of(i * cols, cols), cols)
+        wgrad[block, out_cols] = dot(att_v[i], gcols[...], ((0,), (0,))).astype(BF16)
+        return carry
+
+    lax.fori_loop(0, fsdp // 2, out_grads, 0)
+    sum1.add_core()
+    lax.fori_loop(fsdp // 2, fsdp, out_grads, 0)
+    for i in range(1, dp):
+        far_copy(i, out_cols, zo_send, zo_recv).start()
+    sum1.pass_on()
+    gk[...] = jnp.zeros_like(gk)
+    gval[...] = jnp.zeros_like(gval)
+    gatt[...] = sum1.total().astype(BF16)
+
+    tile = 256
+
+    def head(h, carry):
+        lane = pl.ds(pl.multiple_of(h * HEAD_DIM, HEAD_DIM), HEAD_DIM)
+        for t in range(seq // tile):
+            r = pl.ds(t * tile, tile)
+            extent = (t + 1) * tile
+            upto = pl.ds(0, extent)
+            query = qkv[0, r, lane]
+            key = qkv[1, upto, lane]
+            value = qkv[2, upto, lane]
+            grad = gatt[r, lane]
+            scores = dot(query, key, ((1,), (1,))) * scaling
+            q_pos = t * tile + lax.broadcasted_iota(jnp.int32, (tile, extent), 0)
+            k_pos = lax.broadcasted_iota(jnp.int32, (tile, extent), 1)
+            allowed = (k_pos <= q_pos) & (live[0:1, 0:extent] > 0.0)
+            masked = jnp.where(allowed, scores, -1e30)
+            weights = jnp.exp(masked - jnp.max(masked, axis=-1, keepdims=True))
+            weights = jnp.where(allowed, weights, 0.0)
+            probs = weights / jnp.sum(weights, axis=-1, keepdims=True)
+            grad_probs = dot(grad, value, ((1,), (1,)))
+            mean = jnp.sum(probs * grad_probs, axis=-1, keepdims=True)
+            grad_scores = (probs * (grad_probs - mean)).astype(BF16)
+            gq[r, lane] = dot(grad_scores, key, ((1,), (0,)))
+            gk[upto, lane] += dot(grad_scores, query, ((0,), (0,)))
+            gval[upto, lane] += dot(probs.astype(BF16), grad, ((0,), (0,)))
+        return carry
+
+    lax.fori_loop(0, cols // HEAD_DIM, head, 0)
+
+    heads_here = cols // HEAD_DIM
+    for i, source in enumerate((gq, gk)):
+        for h in range(heads_here):
+            lane = pl.ds(h * HEAD_DIM, HEAD_DIM)
+            wide = pl.ds(i * cols + h * HEAD_DIM, HEAD_DIM)
+            grad = source[:, lane] * scaling
+            grad = grad * turn[0] + pltpu.roll(grad, HEAD_DIM // 2, 1) * turn[1]
+            terms[:, wide] = jnp.broadcast_to(
+                jnp.sum(grad * unit[:, wide], axis=0, keepdims=True), (8, HEAD_DIM)
+            )
+            gqk[:, wide] = grad * gain[0:1, wide]
+    row = lax.broadcasted_iota(jnp.int32, (8, 2 * cols), 0)
+    lane_of = lax.broadcasted_iota(jnp.int32, (8, 2 * cols), 1)
+    chooser = jnp.where(lane_of // cols == row, 1.0, 0.0).astype(F32)
+    stat[...] = lax.dot_general(
+        chooser,
+        gqk[...] * unit[...],
+        (((1,), (1,)), ((), ())),
+        precision=HIGH,
+        preferred_element_type=F32,
+    )
+
+    def stat_copy(k):
+        return remote(
+            stat, stat_in.at[f], t_send.at[k], t_recv.at[k], {"fsdp": lax.rem(f + k, fsdp)}
+        )
+
+    for k in range(1, fsdp):
+        stat_copy(k).start()
+    stat_in[f] = stat[...]
+    gqkv[:, pl.ds(2 * cols, cols)] = gval[...].astype(BF16)
+    for k in range(1, fsdp):
+        stat_copy(k).wait_recv()
+    sums = stat_in[0]
+    for i in range(1, fsdp):
+        sums = sums + stat_in[i]
+    corner = jnp.where(
+        lax.broadcasted_iota(jnp.int32, (8, 128), 0) == lax.broadcasted_iota(jnp.int32, (8, 128), 1),
+        1.0 / width,
+        0.0,
+    ).astype(F32)
+    means = lax.dot_general(
+        sums, corner, (((0,), (0,)), ((), ())), precision=HIGH, preferred_element_type=F32
+    )
+    for i in range(2):
+        wide = pl.ds(i * cols, cols)
+        grad = scale[:, i : i + 1] * (gqk[:, wide] - unit[:, wide] * means[:, i : i + 1])
+        gqkv[:, wide] = grad.astype(BF16)
+
+    step = 512
+
+    def normed_back(i, carry):
+        r = pl.ds(pl.multiple_of(i * rows, rows), rows)
+        for c in range(width // step):
+            col = pl.ds(c * step, step)
+            part2[i, :, col] = dot(gqkv[r, :], w_v[col, qkv_cols], ((1,), (1,))).astype(BF16)
+        return carry
+
+    lax.fori_loop(0, fsdp, normed_back, 0)
+    sum2 = PlaneSum(plane, part2, held2, core2, half2, full2, s2_send, s2_recv)
+    sum2.start()
+
+    def qkv_grads(p):
+        for i in range(2):
+            block = pl.ds(pl.multiple_of(p * slab + i * (slab // 2), slab // 2), slab // 2)
+            wgrad[block, qkv_cols] = dot(normed_v[:, block], gqkv[...], ((0,), (0,))).astype(BF16)
+
+    for i in range(1, dp):
+        qkv_grads(lax.rem(z + i, dp))
+        far_copy(i, qkv_cols, zq_send, zq_recv).start()
+        if i == 1:
+            sum2.add_core()
+        if i == 2:
+            sum2.pass_on()
+    qkv_grads(z)
+    grad_normed[...] = sum2.total()
+
+    for i in range(1, dp):
+        far_copy(i, out_cols, zo_send, zo_recv).wait()
+    for i in range(1, dp):
+        far_copy(i, qkv_cols, zq_send, zq_recv).wait()
+    total = wgrad[slab_rows(z), :].astype(F32)
+    for i in range(1, dp):
+        total += z_in[i].astype(F32)
+    wsum[...] = total.astype(BF16).reshape(wsum.shape)
+
+    def owner_copy(k):
+        target = lax.rem(f + k, fsdp)
+        return remote(
+            wsum.at[target], owned.at[f], w_send.at[k], w_recv.at[k], {"fsdp": target}
+        )
+
+    for k in range(1, fsdp):
+        owner_copy(k).start()
+    owned[f] = wsum[f]
+    for k in range(1, fsdp):
+        owner_copy(k).wait()
+    for k in range(1, fsdp):
+        cols_copy(k).wait_send()
+        stat_copy(k).wait_send()
+        outer_copy(k).wait()
+    for k in range(1, n):
+        inner_copy(k).wait()
+    for copy in keeps:
+        copy.wait()
+
+
+def attention_back(
+    grad_rows, attended, weight, normed, qkv, unit, scale, gain, turn, live, inner_in, outer_in, ident
+):
+    dp = lax.axis_size("dp")
+    fsdp = lax.axis_size("fsdp")
+    n = dp * fsdp
+    rows, width = grad_rows.shape
+    seq = rows * fsdp
+    cols = width // fsdp
+    own_rows = width // n
+    shape = jax.ShapeDtypeStruct
+    dma = pltpu.SemaphoreType.DMA
+    vmem = pltpu.VMEM
+    anywhere = pl.BlockSpec(memory_space=pl.ANY)
+    inside = pl.BlockSpec(memory_space=pltpu.VMEM)
+    return pl.pallas_call(
+        functools.partial(attention_back_kernel, dp, fsdp),
+        out_shape=(
+            shape((rows, width), F32),
+            shape((8, 2 * cols), F32),
+            shape((fsdp, own_rows, 4 * cols), BF16),
+            shape(inner_in.shape, BF16),
+            shape(outer_in.shape, BF16),
+        ),
+        in_specs=[anywhere] * 4 + [inside] * 6 + [anywhere] * 2,
+        out_specs=(inside, inside, inside, anywhere, anywhere),
+        scratch_shapes=[
+            vmem((fsdp, seq, cols), BF16),
+            vmem((width, 4 * cols), BF16),
+            vmem((seq, width), BF16),
+            vmem((seq, cols), BF16),
+            vmem((fsdp, seq, cols), BF16),
+            vmem((4, seq, cols), BF16),
+            vmem((4, seq, cols), BF16),
+            vmem((2, seq // 2, cols), BF16),
+            vmem((2, seq, cols), BF16),
+            vmem((fsdp, rows, width), BF16),
+            vmem((4, rows, width), BF16),
+            vmem((4, rows, width), BF16),
+            vmem((2, rows // 2, width), BF16),
+            vmem((2, rows, width), BF16),
+            vmem((seq, cols), BF16),
+            vmem((seq, cols), F32),
+            vmem((seq, cols), F32),
+            vmem((seq, cols), F32),
+            vmem((seq, 2 * cols), F32),
+            vmem((seq, 3 * cols), BF16),
+            vmem((8, seq), F32),
+            vmem((fsdp, 8, seq), F32),
+            vmem((width, 4 * cols), BF16),
+            vmem((dp, fsdp * own_rows, 4 * cols), BF16),
+            vmem((fsdp, own_rows, 4 * cols), BF16),
+            dma((6,)),
+            dma((n,)),
+            dma((n,)),
+            dma((fsdp,)),
+            dma((fsdp,)),
+            dma((fsdp,)),
+            dma((fsdp,)),
+            dma((8,)),
+            dma((8,)),
+            dma((8,)),
+            dma((8,)),
+            dma((fsdp,)),
+            dma((fsdp,)),
+            dma((dp,)),
+            dma((dp,)),
+            dma((dp,)),
+            dma((dp,)),
+            dma((fsdp,)),
+            dma((fsdp,)),
+        ],
+        compiler_params=pltpu.CompilerParams(
+            collective_id=ident, has_side_effects=True, vmem_limit_bytes=63 * 1024 * 1024
+        ),
+    )(grad_rows, attended, weight, normed, qkv, unit, scale, gain, turn, live, inner_in, outer_in)
 
 
 def expert_kernel(
@@ -621,6 +1592,7 @@
     rows, width = hidden_in.shape
     dp = lax.axis_size("dp")
     fsdp = lax.axis_size("fsdp")
+    fused = fsdp == 8
     n = dp * fsdp
     experts = router_weight.shape[1]
     seq = rows * fsdp
@@ -655,28 +1627,13 @@
         axis=1,
     )
     attn_weight = attn_weight.transpose(2, 0, 1, 3).reshape(fsdp, own_rows, 4 * cols)
-    attn_weight = lax.all_to_all(attn_weight, "fsdp", 0, 0, tiled=True)
-    attn_weight = lax.all_gather(
-        attn_weight.reshape(fsdp * own_rows, 4 * cols), "dp", axis=0, tiled=True
-    )
-    qkv_here = attn_weight[:, : 3 * cols]
-    out_here = attn_weight[:, 3 * cols :]
-
-    fused = fsdp == 8
     inner_weight = expert_in.reshape(own_rows, fsdp, experts_here, 2, dp, ff_here)
     inner_weight = inner_weight.transpose(4, 1, 3, 2, 0, 5)
     inner_weight = inner_weight.reshape(n, 2 * experts_here, own_rows, ff_here)
-    inner_weight = lax.all_to_all(inner_weight, BOTH, 0, 0, tiled=True)
     outer_weight = expert_out.reshape(-1, fsdp, experts_here, width).transpose(1, 2, 0, 3)
-    outer_weight = lax.all_to_all(outer_weight, "fsdp", 0, 0, tiled=True)
-
-    hidden_all = lax.all_gather(hidden_in, "fsdp", axis=0, tiled=True).astype(F32)
-    normed_all = (hidden_all * rms_scale(hidden_all) * gain_attn).astype(BF16)
-    mixed = dot(normed_all, qkv_here, ((1,), (0,)))
-    raw = mixed[:, : 2 * cols].reshape(seq, 2, cols)
-    squares = plane_sum(jnp.sum(raw * raw, axis=-1), 1)
-    qk_scale = lax.rsqrt(squares / width + EPS)[:, :, None]
-    qk_unit = raw * qk_scale
+    live_mask = (f * rows + jnp.arange(rows, dtype=jnp.int32) < valid).astype(F32)[:, None]
+    grad_total = cotangent.astype(F32) * live_mask
+
     here = f * cols
     qk_gain = jnp.stack(
         [
@@ -689,25 +1646,80 @@
     angles = pos.astype(F32)[:, None] * frequency[None, :]
     cosine = jnp.cos(angles)[:, None, None, :]
     sine = jnp.sin(angles)[:, None, None, :]
-    shape4 = (seq, 2, heads_here, HEAD_DIM)
-    turned = rotate((qk_unit * qk_gain).reshape(shape4), cosine, sine, 1.0).astype(BF16)
-    query = turned[:, 0]
-    key = turned[:, 1]
-    value = mixed[:, 2 * cols :].astype(BF16).reshape(seq, heads_here, HEAD_DIM)
-    allowed = ((pos[None, :] <= pos[:, None]) & (pos[None, :] < valid))[None]
-    scores = jnp.einsum("qhd,khd->hqk", query, key, preferred_element_type=F32) * scaling
-    masked = jnp.where(allowed, scores, -1e30)
-    weights = jnp.where(allowed, jnp.exp(masked - jnp.max(masked, axis=-1, keepdims=True)), 0.0)
-    probs = weights / jnp.sum(weights, axis=-1, keepdims=True)
-    probs_low = probs.astype(BF16)
-    attended = jnp.einsum("hqk,khd->qhd", probs_low, value, preferred_element_type=F32)
-    attended = attended.reshape(seq, cols).astype(BF16)
-    attended_all = lax.all_gather(attended, "fsdp", axis=0, tiled=False)
-    branch = jnp.einsum(
-        "fsc,fcn->sn", attended_all, out_here.reshape(fsdp, cols, cols), preferred_element_type=F32
-    )
-    branch = exchange(branch.astype(BF16).reshape(fsdp, rows, cols), ("fsdp",), 2, True)
-    branch = branch.transpose(1, 0, 2).reshape(rows, width).astype(F32)
+
+    if fused:
+        gain_wide = jnp.broadcast_to(qk_gain.reshape(1, 2 * cols), (8, 2 * cols))
+        turn = jnp.stack(
+            [
+                jnp.concatenate([cosine, cosine], axis=-1).reshape(seq, HEAD_DIM),
+                jnp.concatenate([sine, -sine], axis=-1).reshape(seq, HEAD_DIM),
+            ]
+        )
+        live_keys = jnp.broadcast_to((pos < valid).astype(F32)[None], (8, seq))
+        (
+            branch,
+            qkv,
+            qk_unit,
+            qk_scale,
+            normed_all,
+            attn_weight,
+            attended_all,
+            grad_all,
+            inner_weight,
+            outer_weight,
+        ) = attention_forward(
+            hidden_in,
+            grad_total.astype(BF16),
+            attn_weight,
+            inner_weight,
+            outer_weight,
+            jnp.broadcast_to(gain_attn[None], (8, width)),
+            gain_wide,
+            turn,
+            live_keys,
+            10,
+        )
+        branch = branch.astype(F32)
+    else:
+        attn_weight = lax.all_to_all(attn_weight, "fsdp", 0, 0, tiled=True)
+        attn_weight = lax.all_gather(
+            attn_weight.reshape(fsdp * own_rows, 4 * cols), "dp", axis=0, tiled=True
+        )
+        qkv_here = attn_weight[:, : 3 * cols]
+        out_here = attn_weight[:, 3 * cols :]
+        inner_weight = lax.all_to_all(inner_weight, BOTH, 0, 0, tiled=True)
+        outer_weight = lax.all_to_all(outer_weight, "fsdp", 0, 0, tiled=True)
+        hidden_all = lax.all_gather(hidden_in, "fsdp", axis=0, tiled=True).astype(F32)
+        normed_all = (hidden_all * rms_scale(hidden_all) * gain_attn).astype(BF16)
+        mixed = dot(normed_all, qkv_here, ((1,), (0,)))
+        raw = mixed[:, : 2 * cols].reshape(seq, 2, cols)
+        squares = plane_sum(jnp.sum(raw * raw, axis=-1), 1)
+        qk_scale = lax.rsqrt(squares / width + EPS)[:, :, None]
+        qk_unit = raw * qk_scale
+        shape4 = (seq, 2, heads_here, HEAD_DIM)
+        turned = rotate((qk_unit * qk_gain).reshape(shape4), cosine, sine, 1.0).astype(BF16)
+        query = turned[:, 0]
+        key = turned[:, 1]
+        value = mixed[:, 2 * cols :].astype(BF16).reshape(seq, heads_here, HEAD_DIM)
+        allowed = ((pos[None, :] <= pos[:, None]) & (pos[None, :] < valid))[None]
+        scores = jnp.einsum("qhd,khd->hqk", query, key, preferred_element_type=F32) * scaling
+        masked = jnp.where(allowed, scores, -1e30)
+        weights = jnp.exp(masked - jnp.max(masked, axis=-1, keepdims=True))
+        weights = jnp.where(allowed, weights, 0.0)
+        probs = weights / jnp.sum(weights, axis=-1, keepdims=True)
+        probs_low = probs.astype(BF16)
+        attended = jnp.einsum("hqk,khd->qhd", probs_low, value, preferred_element_type=F32)
+        attended = attended.reshape(seq, cols).astype(BF16)
+        attended_all = lax.all_gather(attended, "fsdp", axis=0, tiled=False)
+        branch = jnp.einsum(
+            "fsc,fcn->sn",
+            attended_all,
+            out_here.reshape(fsdp, cols, cols),
+            preferred_element_type=F32,
+        )
+        branch = exchange(branch.astype(BF16).reshape(fsdp, rows, cols), ("fsdp",), 2, True)
+        branch = branch.transpose(1, 0, 2).reshape(rows, width).astype(F32)
+        grad_all = lax.all_gather(grad_total.astype(BF16), BOTH, axis=0, tiled=True)
 
     hidden = hidden_in.astype(F32)
     scale1 = rms_scale(hidden)
@@ -722,10 +1734,7 @@
         (routes[:, :, None] == jnp.arange(experts, dtype=jnp.int32)[None, None, :]).astype(F32),
         axis=1,
     )
-    live_mask = (f * rows + jnp.arange(rows, dtype=jnp.int32) < valid).astype(F32)[:, None]
-    grad_total = cotangent.astype(F32) * live_mask
-
-    grad_all = lax.all_gather(grad_total.astype(BF16), BOTH, axis=0, tiled=True)
+
     gates = (router_probs * chosen).reshape(rows, fsdp, experts_here).transpose(1, 2, 0)
     gates = jnp.broadcast_to(gates[None], (dp, fsdp, experts_here, rows))
     gates = gates.reshape(n, experts_here, rows)
@@ -750,12 +1759,6 @@
     grad_gates = jnp.sum(grad_gates.reshape(dp, fsdp, experts_here, rows), axis=0)
     grad_router_probs = grad_gates.reshape(experts, rows).transpose(1, 0) * chosen
 
-    inner_grad = lax.all_to_all(inner_grad, BOTH, 0, 0, tiled=True)
-    inner_grad = inner_grad.reshape(dp, fsdp, 2, experts_here, own_rows, ff_here)
-    inner_grad = inner_grad.transpose(4, 1, 3, 2, 0, 5).reshape(own_rows, experts, 2 * ff)
-    outer_grad = lax.all_to_all(outer_grad, "fsdp", 0, 0, tiled=True)
-    outer_grad = outer_grad.transpose(2, 0, 1, 3).reshape(-1, experts, width)
-
     block_total = middle + expert_sum
     squares = jnp.stack(
         [
@@ -774,43 +1777,65 @@
     ffn_term = jnp.sum(grad_normed2 * unit2, axis=0)
     grad_middle = grad_total + norm_back(grad_normed2 * gain_ffn, unit2, scale2)
 
-    grad_cols = grad_middle.astype(BF16).reshape(rows, fsdp, cols).transpose(1, 0, 2)
-    grad_cols = exchange(grad_cols, ("fsdp",), 5, True).reshape(seq, cols)
-    out_grad = jnp.einsum("fsc,sn->fcn", attended_all, grad_cols, preferred_element_type=F32)
-    grad_attended = jnp.einsum(
-        "sn,fcn->fsc", grad_cols, out_here.reshape(fsdp, cols, cols), preferred_element_type=F32
-    )
-    grad_attended = lax.psum_scatter(
-        grad_attended.astype(BF16).reshape(fsdp * seq, cols), "fsdp", scatter_dimension=0, tiled=True
-    )
-    grad_attended = grad_attended.reshape(seq, heads_here, HEAD_DIM)
-    grad_probs = jnp.einsum("qhd,khd->hqk", grad_attended, value, preferred_element_type=F32)
-    grad_scores = probs * (grad_probs - jnp.sum(probs * grad_probs, axis=-1, keepdims=True))
-    grad_scores = grad_scores.astype(BF16)
-    grad_query = jnp.einsum("hqk,khd->qhd", grad_scores, key, preferred_element_type=F32)
-    grad_key = jnp.einsum("hqk,qhd->khd", grad_scores, query, preferred_element_type=F32)
-    grad_value = jnp.einsum("hqk,qhd->khd", probs_low, grad_attended, preferred_element_type=F32)
-    grad_qk = rotate(jnp.stack([grad_query, grad_key], axis=1) * scaling, cosine, sine, -1.0)
-    grad_qk = grad_qk.reshape(seq, 2, cols)
-    qk_term = jnp.sum(grad_qk * qk_unit, axis=0)
-    grad_qk = grad_qk * qk_gain
-    inner_means = plane_sum(jnp.sum(grad_qk * qk_unit, axis=-1), 6)[:, :, None] / width
-    grad_qk = qk_scale * (grad_qk - qk_unit * inner_means)
-    grad_qkv = jnp.concatenate(
-        [grad_qk.reshape(seq, 2 * cols), grad_value.reshape(seq, cols)], axis=1
-    ).astype(BF16)
-    qkv_grad = dot(normed_all, grad_qkv, ((0,), (0,)))
-    grad_normed = dot(grad_qkv, qkv_here, ((1,), (1,))).astype(BF16)
-    grad_normed = lax.psum_scatter(grad_normed, "fsdp", scatter_dimension=0, tiled=True).astype(F32)
+    if fused:
+        grad_normed, qk_term, attn_grad, inner_grad, outer_grad = attention_back(
+            grad_middle.astype(BF16),
+            attended_all,
+            attn_weight,
+            normed_all,
+            qkv,
+            qk_unit,
+            qk_scale,
+            gain_wide,
+            turn,
+            live_keys,
+            inner_grad,
+            outer_grad,
+            9,
+        )
+        qk_term = qk_term[0].reshape(2, cols)
+    else:
+        grad_cols = grad_middle.astype(BF16).reshape(rows, fsdp, cols).transpose(1, 0, 2)
+        grad_cols = exchange(grad_cols, ("fsdp",), 5, True).reshape(seq, cols)
+        out_grad = jnp.einsum("fsc,sn->fcn", attended_all, grad_cols, preferred_element_type=F32)
+        grad_attended = jnp.einsum(
+            "sn,fcn->fsc", grad_cols, out_here.reshape(fsdp, cols, cols), preferred_element_type=F32
+        )
+        grad_attended = lax.psum_scatter(
+            grad_attended.astype(BF16).reshape(fsdp * seq, cols), "fsdp", scatter_dimension=0, tiled=True
+        )
+        grad_attended = grad_attended.reshape(seq, heads_here, HEAD_DIM)
+        grad_probs = jnp.einsum("qhd,khd->hqk", grad_attended, value, preferred_element_type=F32)
+        grad_scores = probs * (grad_probs - jnp.sum(probs * grad_probs, axis=-1, keepdims=True))
+        grad_scores = grad_scores.astype(BF16)
+        grad_query = jnp.einsum("hqk,khd->qhd", grad_scores, key, preferred_element_type=F32)
+        grad_key = jnp.einsum("hqk,qhd->khd", grad_scores, query, preferred_element_type=F32)
+        grad_value = jnp.einsum("hqk,qhd->khd", probs_low, grad_attended, preferred_element_type=F32)
+        grad_qk = rotate(jnp.stack([grad_query, grad_key], axis=1) * scaling, cosine, sine, -1.0)
+        grad_qk = grad_qk.reshape(seq, 2, cols)
+        qk_term = jnp.sum(grad_qk * qk_unit, axis=0)
+        grad_qk = grad_qk * qk_gain
+        inner_means = plane_sum(jnp.sum(grad_qk * qk_unit, axis=-1), 6)[:, :, None] / width
+        grad_qk = qk_scale * (grad_qk - qk_unit * inner_means)
+        grad_qkv = jnp.concatenate(
+            [grad_qk.reshape(seq, 2 * cols), grad_value.reshape(seq, cols)], axis=1
+        ).astype(BF16)
+        qkv_grad = dot(normed_all, grad_qkv, ((0,), (0,)))
+        grad_normed = dot(grad_qkv, qkv_here, ((1,), (1,))).astype(BF16)
+        grad_normed = lax.psum_scatter(grad_normed, "fsdp", scatter_dimension=0, tiled=True).astype(F32)
+        attn_grad = jnp.concatenate([qkv_grad, out_grad.reshape(width, cols)], axis=1).astype(BF16)
+        attn_grad = lax.psum_scatter(attn_grad, "dp", scatter_dimension=0, tiled=True)
+        attn_grad = attn_grad.reshape(fsdp, own_rows, 4 * cols)
+        attn_grad = lax.all_to_all(attn_grad, "fsdp", 0, 0, tiled=True)
+        inner_grad = lax.all_to_all(inner_grad, BOTH, 0, 0, tiled=True)
+        outer_grad = lax.all_to_all(outer_grad, "fsdp", 0, 0, tiled=True)
+    inner_grad = inner_grad.reshape(dp, fsdp, 2, experts_here, own_rows, ff_here)
+    inner_grad = inner_grad.transpose(4, 1, 3, 2, 0, 5).reshape(own_rows, experts, 2 * ff)
+    outer_grad = outer_grad.transpose(2, 0, 1, 3).reshape(-1, experts, width)
+    attn_grad = attn_grad.reshape(fsdp, own_rows, 4, cols).transpose(1, 2, 0, 3).astype(F32)
+    attn_grad = attn_grad.reshape(own_rows, 4 * width)
     attn_term = jnp.sum(grad_normed * unit1, axis=0)
     hidden_grad = grad_middle + norm_back(grad_normed * gain_attn, unit1, scale1)
-
-    attn_grad = jnp.concatenate([qkv_grad, out_grad.reshape(width, cols)], axis=1).astype(BF16)
-    attn_grad = lax.psum_scatter(attn_grad, "dp", scatter_dimension=0, tiled=True)
-    attn_grad = attn_grad.reshape(fsdp, own_rows, 4 * cols)
-    attn_grad = lax.all_to_all(attn_grad, "fsdp", 0, 0, tiled=True)
-    attn_grad = attn_grad.reshape(fsdp, own_rows, 4, cols).transpose(1, 2, 0, 3).astype(F32)
-    attn_grad = attn_grad.reshape(own_rows, 4 * width)
 
     qk_full = jnp.zeros((2, width), F32)
     qk_full = lax.dynamic_update_slice(qk_full, qk_term, (0, here))

time: 1120 us -> 944 us (0.84)
  Pallas kernels: 441 us -> 829 us
  waiting for transfers between devices: 388 us -> 0 us
  matrix products: 61 us -> 4.65 us
  local copies, waits for them, and re-layouts: 112 us -> 76.3 us
  blocking collectives: 26.1 us -> 0 us
  starting transfers between devices: 19.8 us -> 0 us
  other arithmetic: 43.5 us -> 25.3 us
  between operations: 16.1 us -> 2.22 us
    pallas_call x0 -> x2, Pallas kernels: none -> 457 us  [the longest x1 252 us: attention_forward(): pl.pallas_call(functools.partial(attention_kernel, dp, fsdp), out_shape=(...]
    all_to_all x5 -> x0, waiting for transfers between devices: 186 us -> none  [the longest x1 132 us: body(): inner_grad = lax.all_to_all(inner_grad, BOTH, 0, 0, tiled=True)]
    all_gather x4 -> x0, waiting for transfers between devices: 149 us -> none  [the longest x1 78.6 us: body(): lax.all_gather(attn_weight.reshape(fsdp * own_rows, 4 * cols), 'dp', axis...]
    pallas_call x8 -> x4, Pallas kernels: 163 us -> 94.8 us  [exchange(): pl.pallas_call(functools.partial(exchange_kernel, axes, n, fsdp, spread),...]
    reduce_scatter x3 -> x0, waiting for transfers between devices: 52.3 us -> none  [the longest x1 52.3 us: body(): lax.psum_scatter(grad_attended.astype(BF16).reshape(fsdp * seq, cols), 'f...]
    dot_general x8 -> x0, matrix products: 30.2 us -> none  [the longest x1 5.85 us: body(): jnp.einsum('hqk,qhd->khd', probs_low, grad_attended, preferred_element_ty...]
    all_to_all x1 -> x0, blocking collectives: 26.1 us -> none  [body(): attn_weight = lax.all_to_all(attn_weight, 'fsdp', 0, 0, tiled=True)]
    all_to_all x5 -> x0, starting transfers between devices: 19.6 us -> none  [the longest x1 4.86 us: body(): attn_grad = lax.all_to_all(attn_grad, 'fsdp', 0, 0, tiled=True)]
  transfers between devices with their start and end apart: 12 -> 0, of which waited for: 9 -> 0; matrix products, arithmetic and copies ran while one was open for 10% -> 0% of each run, Pallas kernels for 11% -> 0%
where the time goes in v3:
time: 944 us; the launch traced here: 938 us
  Pallas kernels  829 us (88%)
  local copies, waits for them, and re-layouts  76.3 us (8%)
  other arithmetic  25.3 us (3%)
    pallas_call x1, Pallas kernels, expert_pass(): pl.pallas_call(functools.partial(expert_kernel, dp), out_shape=(shape((2,...  278 us
    pallas_call x1, Pallas kernels, attention_forward(): pl.pallas_call(functools.partial(attention_kernel, dp, fsdp), out_shape=(...  252 us
    pallas_call x1, Pallas kernels, attention_back(): pl.pallas_call(functools.partial(attention_back_kernel, dp, fsdp), out_sh...  205 us
    pallas_call x4, Pallas kernels, exchange(): pl.pallas_call(functools.partial(exchange_kernel, axes, n, fsdp, spread),...  94.8 us
    convert_element_type x2, local copies, waits for them, and re-layouts, body(): inner_grad.astype(F32)  23.1 us

profile of v3, /device:TPU:0, one launch (start us, length us, event | category | flops | bytes accessed | tf_op | source)
XLA Modules:
  0.0 938.0 jit_solution(1766083354074475679)
XLA Ops:
  1.5 2.8 concatenate.26
  4.9 11.1 %shard_map.220 = bf16[32,16,128]{2,1,0:T(8,128)(2,1)} custom-call(bf16[16,128]{1,0:T(8,128)(2,1)} %pad_bitcast_fusion.1.x), custom_call_target="tpu_custom_call" | custom-call | tf_op jit(solution)/shard_map/pallas_call | solution.py:80
  18.1 1.9 multiply_cosine_fusion
  20.4 1.0 pad_maximum_fusion.turn
  25.6 8.0 reshape.319
  33.6 6.6 copy.64
  41.6 1.1 maximum_bitcast_fusion
  42.7 1.5 reshape.318.weight_in
  44.3 4.1 copy.65
  48.3 251.8 %shard_map.221 = (bf16[128,2048]{1,0:T(8,128)(2,1)}, bf16[3,1024,256]{2,1,0:T(8,128)(2,1)}, f32[1024,512]{1,0:T(8,128)}, f32[1024,128]{1,0:T(8,128)}, bf16[1024,...) custom-call(bf16[128,2048]{1,0:T(8,128)(2,1)} %hidden.1, ...), custom_call_target="tpu_custom_call" | custom-call | tf_op jit(solution)/shard_map/pallas_call | solution.py:661
  300.2 1.3 multiply_reduce_fusion.2
  301.6 1.3 multiply_convert_fusion.x_in
  304.4 21.9 %shard_map.222 = f32[32,8,128]{2,1,0:T(8,128)} custom-call(f32[32,8,128]{2,1,0:T(8,128)} %pad.20.x), custom_call_target="tpu_custom_call" | custom-call | tf_op jit(solution)/shard_map/pallas_call | solution.py:80
  327.9 1.5 pad.21.clone
  329.4 278.0 %shard_map.223 = (f32[2,128,2048]{2,1,0:T(8,128)}, f32[4,1024,128]{2,1,0:T(8,128)}, bf16[32,4,64,256]{3,2,1,0:T(8,128)(2,1)}, bf16[8,2,32,2048]{3,2,1,0:T(8,128)...) custom-call(bf16[128,2048]{1,0:T(8,128)(2,1)} %copy-done.1, bf16[4,1024,2048]{2,1,0:T(8,128)(2,1)} %bitcast.92, ...), custom_call_target="tpu_custom_call" | custom-call | tf_op jit(solution)/shard_map/pallas_call | solution.py:1484
  607.4 2.2 slice.102
  610.9 31.9 %shard_map.224 = f32[32,8,128]{2,1,0:T(8,128)} custom-call(f32[32,8,128]{2,1,0:T(8,128)} %pad.22.x), custom_call_target="tpu_custom_call" | custom-call | tf_op jit(solution)/shard_map/pallas_call | solution.py:80
  643.7 4.0 fusion.9
  647.8 1.3 fusion.21.grad_rows
  649.0 204.9 %shard_map.225 = (f32[128,2048]{1,0:T(8,128)}, f32[8,512]{1,0:T(8,128)}, bf16[8,64,1024]{2,1,0:T(8,128)(2,1)}, bf16[32,4,64,256]{3,2,1,0:T(8,128)(2,1)}, bf16[8,2,32,2048]{3,2,1,0:T(8,128)(2,1)}) custom-call(bf16[128,2048]{1,0:T(8,128)(2,1)} %fusion.21.grad_rows, bf16[8,1024,256]{2,1,0:T(8,128)(2,1)} %get-tuple-element.37.attended, ...), custom_call_target="tpu_custom_call" | custom-call | tf_op jit(solution)/shard_map/pallas_call | solution.py:1017
  853.9 6.7 convert_bitcast_fusion
  860.6 12.0 %copy.73 = f32[64,8,2,2,4,256]{5,4,3,2,1,0:T(4,128)} copy(f32[64,8,2,2,4,256]{5,0,2,3,1,4:T(8,128)} %convert_bitcast_fusion) | data formatting | bytes 16777216 | tf_op jit(solution)/shard_map/convert_element_type | solution.py:1872
  872.6 11.1 %reshape.345 = f32[64,16,2048]{2,1,0:T(8,128)} reshape(f32[64,8,2,2,4,256]{5,4,3,2,1,0:T(4,128)} %copy.73) | data formatting | bytes 16777216 | tf_op jit(solution)/shard_map/convert_element_type | solution.py:1872
  884.3 4.4 copy.75
  888.7 2.0 reshape.350
  890.7 1.2 copy.72
  891.9 1.2 copy.84
  893.1 1.2 slice.104
  895.2 2.0 pad_maximum_fusion.1
  900.6 29.8 %shard_map.226 = f32[32,16,128]{2,1,0:T(8,128)} custom-call(f32[32,16,128]{2,1,0:T(8,128)} %bitcast.104), custom_call_target="tpu_custom_call" | custom-call | tf_op jit(solution)/shard_map/pallas_call | solution.py:80
  930.4 1.0 reduce_sum.148
  934.6 2.9 fusion.6
  (108 shorter events, 21.9 us)
Async XLA Ops:
  20.0 1.4 copy-start.16
  20.0 2.6 copy-start.5
  33.6 6.6 copy-start.13
  40.2 0.9 copy-start.14
  48.3 251.8 %copy-start = (bf16[128,2048]{1,0:T(8,128)(2,1)S(1)}, bf16[128,2048]{1,0:T(8,128)(2,1)}, u32[]{:S(2)}) copy-start(bf16[128,2048]{1,0:T(8,128)(2,1)} %hidden.1) | copy-start | bytes 1572868
  300.2 3.4 copy-start.15
  302.9 25.0 %copy-start.1 = (bf16[128,2048]{1,0:T(8,128)(2,1)}, bf16[128,2048]{1,0:T(8,128)(2,1)S(1)}, u32[]{:S(2)}) copy-start(bf16[128,2048]{1,0:T(8,128)(2,1)S(1)} %multiply_convert_fusion.x_in) | copy-start | bytes 1572868
  303.3 23.0 %copy-start.12 = (bf16[2048,16]{1,0:T(8,128)(2,1)}, bf16[2048,16]{1,0:T(8,128)(2,1)S(1)}, u32[]{:S(2)}) copy-start(bf16[2048,16]{1,0:T(8,128)(2,1)S(1)} %reshape.326) | copy-start | bytes 196612
  609.6 34.2 %copy-start.3 = (bf16[128,2048]{1,0:T(8,128)(2,1)S(1)}, bf16[128,2048]{1,0:T(8,128)(2,1)}, u32[]{:S(2)}) copy-start(bf16[128,2048]{1,0:T(8,128)(2,1)} %get-tuple-element.31) | copy-start | bytes 1572868
  643.7 4.0 copy-start.6
  647.8 1.3 copy-start.8
  872.6 11.1 %copy-start.11 = (bf16[8,2,32,2048]{3,2,1,0:T(8,128)(2,1)S(1)}, bf16[8,2,32,2048]{3,2,1,0:T(8,128)(2,1)}, u32[]{:S(2)}) copy-start(bf16[8,2,32,2048]{3,2,1,0:T(8,128)(2,1)} %get-tuple-element.49) | copy-start | bytes 6291460
  893.1 5.0 copy-start.10
  894.4 4.4 copy-start.2
  899.2 35.5 %copy-start.4 = (bf16[128,2048]{1,0:T(8,128)(2,1)S(1)}, bf16[128,2048]{1,0:T(8,128)(2,1)}, u32[]{:S(2)}) copy-start(bf16[128,2048]{1,0:T(8,128)(2,1)} %get-tuple-element.31) | copy-start | bytes 1572868
  899.2 35.4 %copy-start.7 = (bf16[128,2048]{1,0:T(8,128)(2,1)S(1)}, bf16[128,2048]{1,0:T(8,128)(2,1)}, u32[]{:S(2)}) copy-start(bf16[128,2048]{1,0:T(8,128)(2,1)} %param.25) | copy-start | bytes 1572868
  899.8 34.8 %copy-start.9 = (f32[128,2048]{1,0:T(8,128)S(1)}, f32[128,2048]{1,0:T(8,128)}, u32[]{:S(2)}) copy-start(f32[128,2048]{1,0:T(8,128)} %copy-done.8) | copy-start | bytes 3145732

commit v4 on v3

--- a/solution.py
+++ b/solution.py
@@ -121,6 +121,35 @@
         peer = place(BOTH, fsdp, lax.rem(me + k, n))
         pl.semaphore_signal(barrier, inc=1, device_id=peer, device_id_type=MESH_ID)
     pl.semaphore_wait(barrier, n - 1)
+
+
+def reorder(get, put, outer, inner):
+    total = outer * inner
+    tile = 256
+    step = 512
+
+    def one(i, carry):
+        row = i * tile + lax.broadcasted_iota(jnp.int32, (tile, total), 0)
+        col = lax.broadcasted_iota(jnp.int32, (tile, total), 1)
+        pick = jnp.where(lax.rem(row, outer) * inner + row // outer == col, 1.0, 0.0).astype(BF16)
+        for c in range(2048 // step):
+            lanes = pl.ds(c * step, step)
+            put(i, tile, lanes, dot(pick, get(lanes), ((1,), (0,))).astype(BF16))
+        return carry
+
+    lax.fori_loop(0, total // tile, one, 0)
+
+
+def corner_of(rows, shift, value):
+    row = lax.broadcasted_iota(jnp.int32, (rows, 128), 0)
+    lane = lax.broadcasted_iota(jnp.int32, (rows, 128), 1)
+    return jnp.where(lane == row + shift, value, 0.0).astype(F32)
+
+
+def exact_dot(a, b, dims):
+    return lax.dot_general(
+        a, b, (dims, ((), ())), precision=HIGH, preferred_element_type=F32
+    )
 
 
 class Plane:
@@ -307,6 +336,10 @@
     att_v,
     cols_v,
     rows_v,
+    inner_raw,
+    inner_v,
+    outer_raw,
+    outer_v,
     local,
     w_send,
     w_recv,
@@ -360,20 +393,35 @@
         ref = w_v.at[pl.ds(pl.multiple_of(p * slab, slab), slab)]
         return remote(ref, ref, send.at[near], recv.at[near], {"dp": far})
 
-    def inner_copy(k):
+    experts = inner_v.shape[0]
+    here = experts // fsdp
+    ff = width // 2
+    part = ff // dp
+
+    def inner_block(target, half):
+        lanes = pl.ds(pl.multiple_of(half * ff + target // fsdp * part, part), part)
+        owned = pl.ds(lax.rem(target, fsdp) * here, here)
+        return inner_v.at[owned, :, lanes], inner_out.at[me, pl.ds(half * here, here)]
+
+    def inner_copies(k):
         target = lax.rem(me + k, n)
-        return remote(
-            inner_in.at[target],
-            inner_out.at[me],
-            in_send.at[k],
-            in_recv.at[k],
-            place(BOTH, fsdp, target),
-        )
+        return [
+            remote(
+                *inner_block(target, half),
+                in_send.at[k, half],
+                in_recv.at[k, half],
+                place(BOTH, fsdp, target),
+            )
+            for half in range(2)
+        ]
+
+    def outer_block(target):
+        return outer_v.at[pl.ds(target * here, here)]
 
     def outer_copy(k):
         target = lax.rem(f + k, fsdp)
         return remote(
-            outer_in.at[target], outer_out.at[f], out_send.at[k], out_recv.at[k], {"fsdp": target}
+            outer_block(target), outer_out.at[f], out_send.at[k], out_recv.at[k], {"fsdp": target}
         )
 
     def cot_copy(i):
@@ -406,8 +454,8 @@
         pltpu.make_async_copy(hidden, hid_v.at[f], local.at[0]),
         pltpu.make_async_copy(weight_in.at[f], w_v.at[weight_rows(me)], local.at[1]),
         pltpu.make_async_copy(cot, c_all.at[z, f], local.at[2]),
-        pltpu.make_async_copy(inner_in.at[me], inner_out.at[me], local.at[3]),
-        pltpu.make_async_copy(outer_in.at[f], outer_out.at[f], local.at[4]),
+        pltpu.make_async_copy(outer_in, outer_raw, local.at[3]),
+        pltpu.make_async_copy(inner_in, inner_raw, local.at[4]),
     ]
     for copy in keeps:
         copy.start()
@@ -430,9 +478,32 @@
     hidden_gather.middle()
     keeps[2].wait()
     cot_gather[dp - 1].start()
+
+    keeps[3].wait()
+    outer_rows = outer_v.shape[1]
+
+    def put_outer(i, tile, lanes, value):
+        block = tile // outer_rows
+        outer_v[pl.ds(i * block, block), :, lanes] = value.reshape(block, outer_rows, -1)
+
+    reorder(lambda lanes: outer_raw[:, lanes], put_outer, outer_rows, experts)
     hidden_gather.finish()
     for k in range(1, fsdp):
         outer_copy(k).start()
+    keeps[4].wait()
+
+    def put_inner(i, tile, lanes, value):
+        block = tile // own_rows
+        inner_v[pl.ds(i * block, block), :, lanes] = value.reshape(block, own_rows, -1)
+
+    reorder(lambda lanes: inner_raw[:, lanes], put_inner, own_rows, experts)
+    owns = [
+        pltpu.make_async_copy(outer_block(f), outer_out.at[f], local.at[3]),
+        pltpu.make_async_copy(*inner_block(me, 0), local.at[4]),
+        pltpu.make_async_copy(*inner_block(me, 1), local.at[5]),
+    ]
+    for copy in owns:
+        copy.start()
     hidden_gather.wait()
 
     def norm_rows(i, carry):
@@ -472,7 +543,8 @@
     for i in range(1, dp):
         cot_copy(i).start()
     for k in range(1, n):
-        inner_copy(k).start()
+        for copy in inner_copies(k):
+            copy.start()
     weight_store = pltpu.make_async_copy(w_v, weight, local.at[1])
     weight_store.start()
 
@@ -629,8 +701,9 @@
         stat_copy(k).wait_send()
         outer_copy(k).wait()
     for k in range(1, n):
-        inner_copy(k).wait()
-    for copy in keeps[3:]:
+        for copy in inner_copies(k):
+            copy.wait()
+    for copy in owns:
         copy.wait()
     normed_store.wait()
     weight_store.wait()
@@ -655,9 +728,11 @@
     sems = []
     for size in pairs:
         sems += [dma((size,)), dma((size,))]
-    sems += [dma((dp, 10)), dma((dp, 10))]
-    for size in (dp, n, fsdp):
-        sems += [dma((size,)), dma((size,))]
+    sems += [dma((dp, 10)), dma((dp, 10)), dma((dp,)), dma((dp,))]
+    sems += [dma((n, 2)), dma((n, 2)), dma((fsdp,)), dma((fsdp,))]
+    experts = inner_in.shape[1]
+    out_rows = outer_in.shape[0]
+    here = experts // fsdp
     return pl.pallas_call(
         functools.partial(attention_kernel, dp, fsdp),
         out_shape=(
@@ -669,8 +744,8 @@
             shape((width, 4 * cols), BF16),
             shape((fsdp, seq, cols), BF16),
             shape((dp, fsdp, rows, width), BF16),
-            shape(inner_in.shape, BF16),
-            shape(outer_in.shape, BF16),
+            shape((n, 2 * here, width // n, width // 2 // dp), BF16),
+            shape((fsdp, here, out_rows, width), BF16),
         ),
         in_specs=[anywhere] * 5 + [inside] * 4,
         out_specs=(inside,) * 4 + (anywhere,) * 6,
@@ -684,13 +759,27 @@
             vmem((fsdp, seq, cols), BF16),
             vmem((seq, cols), BF16),
             vmem((fsdp, rows, cols), BF16),
-            dma((5,)),
+            vmem((width // n * experts, width), BF16),
+            vmem((experts, width // n, width), BF16),
+            vmem((out_rows * experts, width), BF16),
+            vmem((experts, out_rows, width), BF16),
+            dma((6,)),
             *sems,
         ],
         compiler_params=pltpu.CompilerParams(
             collective_id=ident, has_side_effects=True, vmem_limit_bytes=63 * 1024 * 1024
         ),
-    )(hidden, cot, weight_in, inner_in, outer_in, gain_attn, gain, turn, live)
+    )(
+        hidden,
+        cot,
+        weight_in,
+        inner_in.reshape(-1, width),
+        outer_in.reshape(-1, width),
+        gain_attn,
+        gain,
+        turn,
+        live,
+    )
 
 
 def attention_back_kernel(
@@ -706,11 +795,17 @@
     gain,
     turn,
     live,
+    grad_middle,
+    hidden,
+    gain_attn,
+    terms,
     inner_in,
     outer_in,
-    grad_normed,
-    terms,
+    hidden_grad,
+    terms_out,
     owned,
+    inner_owned,
+    outer_owned,
     inner_out,
     outer_out,
     att_v,
@@ -738,7 +833,11 @@
     wgrad,
     z_in,
     wsum,
+    term_v,
+    term_in,
     local,
+    v_send,
+    v_recv,
     in_send,
     in_recv,
     out_send,
@@ -765,10 +864,19 @@
     plane = Plane(f)
     rows, width = grad_rows.shape
     seq, cols = gcols.shape
-    own_rows = inner_in.shape[2]
+    own_rows = width // n
     slab = fsdp * own_rows
     scaling = HEAD_DIM ** (-0.5)
     greet_all(n, fsdp, me)
+    ff = width // 2
+    ff_here = ff // dp
+
+    def inner_place(half):
+        lanes = pl.ds(pl.multiple_of(half * ff + z * ff_here, ff_here), ff_here)
+        return inner_out.at[f, :, lanes]
+
+    pair = outer_in.shape[1]
+    outer_place = outer_out.at[f // 2, pl.ds(pl.multiple_of(lax.rem(f, 2) * pair, pair), pair)]
 
     loads = [
         pltpu.make_async_copy(attended, att_v, local.at[0]),
@@ -781,8 +889,9 @@
         ),
     ]
     keeps = [
-        pltpu.make_async_copy(inner_in.at[me], inner_out.at[me], local.at[4]),
-        pltpu.make_async_copy(outer_in.at[f], outer_out.at[f], local.at[5]),
+        pltpu.make_async_copy(inner_in.at[me, 0], inner_place(0), local.at[4]),
+        pltpu.make_async_copy(inner_in.at[me, 1], inner_place(1), local.at[5]),
+        pltpu.make_async_copy(outer_in.at[f], outer_place, local.at[6]),
     ]
     for copy in loads:
         copy.start()
@@ -797,20 +906,23 @@
             {"fsdp": target},
         )
 
-    def inner_copy(k):
+    def inner_copies(k):
         target = lax.rem(me + k, n)
-        return remote(
-            inner_in.at[target],
-            inner_out.at[me],
-            in_send.at[k],
-            in_recv.at[k],
-            place(BOTH, fsdp, target),
-        )
+        return [
+            remote(
+                inner_in.at[target, half],
+                inner_place(half),
+                in_send.at[k, half],
+                in_recv.at[k, half],
+                place(BOTH, fsdp, target),
+            )
+            for half in range(2)
+        ]
 
     def outer_copy(k):
         target = lax.rem(f + k, fsdp)
         return remote(
-            outer_in.at[target], outer_out.at[f], out_send.at[k], out_recv.at[k], {"fsdp": target}
+            outer_in.at[target], outer_place, out_send.at[k], out_recv.at[k], {"fsdp": target}
         )
 
     def slab_rows(p):
@@ -828,11 +940,13 @@
     for k in range(1, fsdp):
         cols_copy(k).start()
     for k in range(1, n):
-        inner_copy(k).start()
+        for copy in inner_copies(k):
+            copy.start()
     for k in range(1, fsdp):
         outer_copy(k).start()
     for copy in keeps:
         copy.start()
+    term_v[...] = terms[...]
     for copy in loads:
         copy.wait()
     for k in range(1, fsdp):
@@ -899,8 +1013,9 @@
             wide = pl.ds(i * cols + h * HEAD_DIM, HEAD_DIM)
             grad = source[:, lane] * scaling
             grad = grad * turn[0] + pltpu.roll(grad, HEAD_DIM // 2, 1) * turn[1]
-            terms[:, wide] = jnp.broadcast_to(
-                jnp.sum(grad * unit[:, wide], axis=0, keepdims=True), (8, HEAD_DIM)
+            place_lanes = pl.ds(pl.multiple_of(f * cols + h * HEAD_DIM, HEAD_DIM), HEAD_DIM)
+            term_v[1 + i : 2 + i, place_lanes] = jnp.sum(
+                grad * unit[:, wide], axis=0, keepdims=True
             )
             gqk[:, wide] = grad * gain[0:1, wide]
     row = lax.broadcasted_iota(jnp.int32, (8, 2 * cols), 0)
@@ -967,7 +1082,74 @@
         if i == 2:
             sum2.pass_on()
     qkv_grads(z)
-    grad_normed[...] = sum2.total()
+
+    grad = sum2.total()
+    values = hidden[...].astype(F32)
+    scale1 = lax.rsqrt(jnp.mean(values * values, axis=-1, keepdims=True) + EPS)
+    values = values * scale1
+    term_v[0:1, :] = jnp.sum(grad * values, axis=0, keepdims=True)
+    grad = grad * gain_attn[0:1, :]
+    grad = scale1 * (grad - values * jnp.mean(grad * values, axis=-1, keepdims=True))
+    hidden_grad[...] = grad_middle[...] + grad
+
+    def term_copy(k):
+        target = lax.rem(me + k, n)
+        lanes = pl.ds(pl.multiple_of(target // 2 * 128, 128), 128)
+        return remote(
+            term_v.at[:, lanes],
+            term_in.at[me],
+            v_send.at[k],
+            v_recv.at[k],
+            place(BOTH, fsdp, target),
+        )
+
+    for k in range(1, n):
+        term_copy(k).start()
+    term_in[me] = term_v[:, pl.ds(pl.multiple_of(me // 2 * 128, 128), 128)]
+
+    for copy in keeps:
+        copy.wait()
+    for k in range(1, fsdp):
+        outer_copy(k).wait()
+    outer_load = pltpu.make_async_copy(outer_out, core2, local.at[0])
+    outer_load.start()
+    for k in range(1, n):
+        for copy in inner_copies(k):
+            copy.wait()
+    inner_load = pltpu.make_async_copy(inner_out, part2, local.at[1])
+    inner_load.start()
+    experts = fsdp * (inner_in.shape[2] // own_rows)
+    outer_load.wait()
+    outer_rows = core2.shape[0] * core2.shape[1]
+    inner_rows = part2.shape[0] * part2.shape[1]
+
+    def put_outer(i, tile, lanes, value):
+        block = tile // rows
+        held2[pl.ds(i * block, block), :, lanes] = value.reshape(block, rows, -1)
+
+    reorder(
+        lambda lanes: core2[:, :, lanes].reshape(outer_rows, -1),
+        put_outer,
+        experts,
+        outer_rows // experts,
+    )
+    inner_load.wait()
+
+    def put_inner(i, tile, lanes, value):
+        normed_v[pl.ds(pl.multiple_of(i * tile, tile), tile), lanes] = value
+
+    reorder(
+        lambda lanes: part2[:, :, lanes].reshape(inner_rows, -1),
+        put_inner,
+        experts,
+        inner_rows // experts,
+    )
+    stores = [
+        pltpu.make_async_copy(held2, outer_owned, local.at[0]),
+        pltpu.make_async_copy(normed_v, inner_owned, local.at[1]),
+    ]
+    for store in stores:
+        store.start()
 
     for i in range(1, dp):
         far_copy(i, out_cols, zo_send, zo_recv).wait()
@@ -992,15 +1174,34 @@
     for k in range(1, fsdp):
         cols_copy(k).wait_send()
         stat_copy(k).wait_send()
-        outer_copy(k).wait()
     for k in range(1, n):
-        inner_copy(k).wait()
-    for copy in keeps:
-        copy.wait()
+        term_copy(k).wait()
+    total = term_in[0]
+    for i in range(1, n):
+        total += term_in[i]
+    terms_out[...] = total
+    for store in stores:
+        store.wait()
 
 
 def attention_back(
-    grad_rows, attended, weight, normed, qkv, unit, scale, gain, turn, live, inner_in, outer_in, ident
+    grad_rows,
+    attended,
+    weight,
+    normed,
+    qkv,
+    unit,
+    scale,
+    gain,
+    turn,
+    live,
+    grad_middle,
+    hidden,
+    gain_attn,
+    terms,
+    inner_in,
+    outer_in,
+    ident,
 ):
     dp = lax.axis_size("dp")
     fsdp = lax.axis_size("fsdp")
@@ -1018,13 +1219,15 @@
         functools.partial(attention_back_kernel, dp, fsdp),
         out_shape=(
             shape((rows, width), F32),
-            shape((8, 2 * cols), F32),
+            shape((terms.shape[0], 128), F32),
             shape((fsdp, own_rows, 4 * cols), BF16),
-            shape(inner_in.shape, BF16),
-            shape(outer_in.shape, BF16),
+            shape((seq, width), BF16),
+            shape((4, rows, width), BF16),
+            shape((fsdp, rows, width), BF16),
+            shape((4, rows, width), BF16),
         ),
-        in_specs=[anywhere] * 4 + [inside] * 6 + [anywhere] * 2,
-        out_specs=(inside, inside, inside, anywhere, anywhere),
+        in_specs=[anywhere] * 4 + [inside] * 10 + [anywhere] * 2,
+        out_specs=(inside,) * 3 + (anywhere,) * 4,
         scratch_shapes=[
             vmem((fsdp, seq, cols), BF16),
             vmem((width, 4 * cols), BF16),
@@ -1051,9 +1254,13 @@
             vmem((width, 4 * cols), BF16),
             vmem((dp, fsdp * own_rows, 4 * cols), BF16),
             vmem((fsdp, own_rows, 4 * cols), BF16),
-            dma((6,)),
+            vmem(terms.shape, F32),
+            vmem((n, terms.shape[0], 128), F32),
+            dma((7,)),
             dma((n,)),
             dma((n,)),
+            dma((n, 2)),
+            dma((n, 2)),
             dma((fsdp,)),
             dma((fsdp,)),
             dma((fsdp,)),
@@ -1074,18 +1281,36 @@
         compiler_params=pltpu.CompilerParams(
             collective_id=ident, has_side_effects=True, vmem_limit_bytes=63 * 1024 * 1024
         ),
-    )(grad_rows, attended, weight, normed, qkv, unit, scale, gain, turn, live, inner_in, outer_in)
+    )(
+        grad_rows,
+        attended,
+        weight,
+        normed,
+        qkv,
+        unit,
+        scale,
+        gain,
+        turn,
+        live,
+        grad_middle,
+        hidden,
+        gain_attn,
+        terms,
+        inner_in,
+        outer_in,
+    )
 
 
 def expert_kernel(
     dp,
+    fsdp,
     x_in,
     c_all,
     gates,
     inner_in,
     outer_in,
     sums,
-    gate_out,
+    gate_sum,
     inner_out,
     outer_out,
     gathered,
@@ -1104,7 +1329,14 @@
     core_in,
     half_in,
     full_in,
+    gates_in,
+    grads_out,
+    grads_in,
     local,
+    g_send,
+    g_recv,
+    gg_send,
+    gg_recv,
     z_send,
     z_recv,
     a_send,
@@ -1254,22 +1486,39 @@
             copy.wait()
         return held[k, chip].astype(F32) + full_in[k, 0].astype(F32) + full_in[k, 1].astype(F32)
 
-    barrier = pltpu.get_barrier_semaphore()
-    for device in (to_x, to_y, to_c):
-        pl.semaphore_signal(barrier, inc=1, device_id=device, device_id_type=MESH_ID)
-    for i in range(1, dp):
-        pl.semaphore_signal(
-            barrier, inc=1, device_id={"dp": lax.rem(z + i, dp)}, device_id_type=MESH_ID
-        )
-    pl.semaphore_wait(barrier, 3 + dp - 1)
-
-    for i in range(1, dp):
-        far_copy(i).start()
+    n = dp * fsdp
+    me = z * fsdp + f
+    greet_all(n, fsdp, me)
+
+    def gate_copy(k):
+        target = lax.rem(me + k, n)
+        return remote(
+            gates.at[target],
+            gates_in.at[me],
+            g_send.at[k],
+            g_recv.at[k],
+            place(BOTH, fsdp, target),
+        )
+
+    def gate_grad_copy(k):
+        target = lax.rem(me + k, n)
+        return remote(
+            grads_out.at[target],
+            grads_in.at[me],
+            gg_send.at[k],
+            gg_recv.at[k],
+            place(BOTH, fsdp, target),
+        )
+
+    far_copy(1).start()
+    for k in range(1, n):
+        gate_copy(k).start()
     loads = [pltpu.make_async_copy(x_in, gathered.at[z, f], local.at[0])]
     for q in range(4):
         loads.append(pltpu.make_async_copy(inner_in.at[:, q], wi.at[q], local.at[1 + q]))
     for e in range(2):
         loads.append(pltpu.make_async_copy(outer_in.at[:, e], wo.at[e], local.at[5 + e]))
+    loads.append(pltpu.make_async_copy(gates.at[me], gates_in.at[me], local.at[7]))
     for load in loads:
         load.start()
     gi[...] = jnp.zeros_like(gi)
@@ -1298,9 +1547,12 @@
             copy.start()
 
     begin_gather(0)
+    for i in range(2, dp):
+        far_copy(i).start()
     middle_gather(0)
-    begin_gather(1)
     end_gather(0)
+    for k in range(1, n):
+        gate_copy(k).wait()
 
     inner_rows = wi.shape[1] * wi.shape[2]
     ff_here = wo.shape[1] * wo.shape[2]
@@ -1357,9 +1609,14 @@
     def chunk(s, carry):
         p = plane_at(s)
         c_load = pltpu.make_async_copy(c_all.at[p], cv, local.at[1])
-        g_load = pltpu.make_async_copy(gates.at[p], gv, local.at[2])
         c_load.start()
-        g_load.start()
+
+        def to_columns(j, carry):
+            r = pl.ds(pl.multiple_of(j * rows, rows), rows)
+            gv[r, :] = exact_dot(gates_in[p * fsdp + j], corner_of(8, 0, 1.0), ((0,), (0,)))
+            return carry
+
+        lax.fori_loop(0, fsdp, to_columns, 0)
         for copy in gather_core(s):
             copy.wait_recv()
         for j in range(8):
@@ -1367,11 +1624,14 @@
                 gathered.at[p, j], xv.at[pl.ds(j * rows, rows)], local.at[3 + j]
             ).start()
         c_load.wait()
-        g_load.wait()
         for j in range(8):
             pltpu.make_async_copy(
                 gathered.at[p, j], xv.at[pl.ds(j * rows, rows)], local.at[3 + j]
             ).wait()
+        @pl.when(s < dp - 1)
+        def _():
+            begin_gather(s + 1)
+
         tile_step(0)
 
         @pl.when(s > 0)
@@ -1382,13 +1642,7 @@
         def _():
             middle_gather(s + 1)
 
-        @pl.when(s < dp - 2)
-        def _():
-            begin_gather(s + 2)
-
         tile_step(1)
-        g_store = pltpu.make_async_copy(gv, gate_out.at[p], local.at[2])
-        g_store.start()
 
         @pl.when(s > 0)
         def _():
@@ -1397,6 +1651,12 @@
         for k in range(2):
             for j in range(4):
                 core_copy(k, j).start()
+        def to_rows(j, carry):
+            r = pl.ds(pl.multiple_of(j * rows, rows), rows)
+            grads_out[p * fsdp + j] = exact_dot(corner_of(8, 8, 1.0), gv[r, :], ((1,), (1,)))
+            return carry
+
+        lax.fori_loop(0, fsdp, to_rows, 0)
         weight_step()
 
         @pl.when(s > 0)
@@ -1414,12 +1674,14 @@
         def _():
             end_gather(s + 1)
 
-        g_store.wait()
         return carry
 
     lax.fori_loop(0, dp, chunk, 0)
 
     pass_full()
+    for k in range(1, n):
+        gate_grad_copy(k).start()
+    grads_in[me] = grads_out[me]
     for q in range(4):
         wi[q] = gi[q].astype(BF16).reshape(wi.shape[1:])
     for e in range(2):
@@ -1458,6 +1720,13 @@
         for i in range(1, dp):
             total += core_in[k, i].astype(F32)
         sums[k] = total
+    for k in range(1, n):
+        gate_grad_copy(k).wait()
+    for j in range(fsdp):
+        total = grads_in[j]
+        for i in range(1, dp):
+            total += grads_in[i * fsdp + j]
+        gate_sum[j] = total
     for store in stores:
         store.wait()
     for i in range(1, dp):
@@ -1482,17 +1751,17 @@
     dma = pltpu.SemaphoreType.DMA
     anywhere = pl.BlockSpec(memory_space=pl.ANY)
     got = pl.pallas_call(
-        functools.partial(expert_kernel, dp),
+        functools.partial(expert_kernel, dp, fsdp),
         out_shape=(
             shape((2, rows, width), F32),
-            shape((dp, chunk, 128), F32),
+            shape((fsdp, 8, 128), F32),
             shape(inner_in.shape, BF16),
             shape(outer_in.shape, BF16),
             shape((dp, fsdp, rows, width), BF16),
             shape((2, dp, rows, width), BF16),
         ),
         in_specs=[anywhere] * 5,
-        out_specs=(pl.BlockSpec(memory_space=pltpu.VMEM),) + (anywhere,) * 5,
+        out_specs=(pl.BlockSpec(memory_space=pltpu.VMEM),) * 2 + (anywhere,) * 4,
         scratch_shapes=[
             pltpu.VMEM((chunk, width), BF16),
             pltpu.VMEM((chunk, width), BF16),
@@ -1508,7 +1777,14 @@
             pltpu.VMEM((2, 4, rows, width), BF16),
             pltpu.VMEM((2, 2, rows // 2, width), BF16),
             pltpu.VMEM((2, 2, rows, width), BF16),
+            pltpu.VMEM((n, 8, 128), F32),
+            pltpu.VMEM((n, 8, 128), F32),
+            pltpu.VMEM((n, 8, 128), F32),
             dma((12 + 2 * dp,)),
+            dma((n,)),
+            dma((n,)),
+            dma((n,)),
+            dma((n,)),
             dma((dp,)),
             dma((dp,)),
             dma((dp, 2)),
@@ -1627,10 +1903,6 @@
         axis=1,
     )
     attn_weight = attn_weight.transpose(2, 0, 1, 3).reshape(fsdp, own_rows, 4 * cols)
-    inner_weight = expert_in.reshape(own_rows, fsdp, experts_here, 2, dp, ff_here)
-    inner_weight = inner_weight.transpose(4, 1, 3, 2, 0, 5)
-    inner_weight = inner_weight.reshape(n, 2 * experts_here, own_rows, ff_here)
-    outer_weight = expert_out.reshape(-1, fsdp, experts_here, width).transpose(1, 2, 0, 3)
     live_mask = (f * rows + jnp.arange(rows, dtype=jnp.int32) < valid).astype(F32)[:, None]
     grad_total = cotangent.astype(F32) * live_mask
 
@@ -1671,8 +1943,8 @@
             hidden_in,
             grad_total.astype(BF16),
             attn_weight,
-            inner_weight,
-            outer_weight,
+            expert_in,
+            expert_out,
             jnp.broadcast_to(gain_attn[None], (8, width)),
             gain_wide,
             turn,
@@ -1687,6 +1959,10 @@
         )
         qkv_here = attn_weight[:, : 3 * cols]
         out_here = attn_weight[:, 3 * cols :]
+        inner_weight = expert_in.reshape(own_rows, fsdp, experts_here, 2, dp, ff_here)
+        inner_weight = inner_weight.transpose(4, 1, 3, 2, 0, 5)
+        inner_weight = inner_weight.reshape(n, 2 * experts_here, own_rows, ff_here)
+        outer_weight = expert_out.reshape(-1, fsdp, experts_here, width).transpose(1, 2, 0, 3)
         inner_weight = lax.all_to_all(inner_weight, BOTH, 0, 0, tiled=True)
         outer_weight = lax.all_to_all(outer_weight, "fsdp", 0, 0, tiled=True)
         hidden_all = lax.all_gather(hidden_in, "fsdp", axis=0, tiled=True).astype(F32)
@@ -1739,24 +2015,23 @@
     gates = jnp.broadcast_to(gates[None], (dp, fsdp, experts_here, rows))
     gates = gates.reshape(n, experts_here, rows)
     gates = jnp.pad(gates, ((0, 0), (0, 8 - experts_here), (0, 0)))
-    gates = exchange(gates, BOTH, 3, True)[:, :experts_here]
-    gates = gates.transpose(0, 2, 1).reshape(tokens, experts_here)
     if fused:
-        gates = jnp.pad(gates, ((0, 0), (0, 128 - experts_here))).reshape(dp, seq, 128)
         sums, grad_gates, inner_grad, outer_grad = expert_pass(
             normed2, grad_all.reshape(dp, seq, width), gates, inner_weight, outer_weight, 8
         )
         expert_sum = sums[0]
         grad_rows = sums[1]
-        grad_gates = grad_gates.reshape(tokens, 128)[:, 8 : 8 + experts_here]
+        grad_gates = grad_gates[:, :experts_here]
     else:
+        gates = exchange(gates, BOTH, 3, True)[:, :experts_here]
+        gates = gates.transpose(0, 2, 1).reshape(tokens, experts_here)
         expert_sum, grad_rows, grad_gates, inner_grad, outer_grad = expert_pass_dense(
             normed2, grad_all, gates, inner_weight, outer_weight
         )
-    grad_gates = grad_gates.reshape(n, rows, experts_here).transpose(0, 2, 1)
-    grad_gates = jnp.pad(grad_gates, ((0, 0), (0, 8 - experts_here), (0, 0)))
-    grad_gates = exchange(grad_gates, BOTH, 4, True)[:, :experts_here]
-    grad_gates = jnp.sum(grad_gates.reshape(dp, fsdp, experts_here, rows), axis=0)
+        grad_gates = grad_gates.reshape(n, rows, experts_here).transpose(0, 2, 1)
+        grad_gates = jnp.pad(grad_gates, ((0, 0), (0, 8 - experts_here), (0, 0)))
+        grad_gates = exchange(grad_gates, BOTH, 4, True)[:, :experts_here]
+        grad_gates = jnp.sum(grad_gates.reshape(dp, fsdp, experts_here, rows), axis=0)
     grad_router_probs = grad_gates.reshape(experts, rows).transpose(1, 0) * chosen
 
     block_total = middle + expert_sum
@@ -1772,13 +2047,21 @@
         grad_router_probs - jnp.sum(router_probs * grad_router_probs, axis=-1, keepdims=True)
     )
     grad_logits = grad_logits.astype(BF16)
-    router_term = dot(normed2, grad_logits, ((0,), (0,)))
     grad_normed2 = grad_rows + dot(grad_logits, router_full, ((1,), (1,)))
     ffn_term = jnp.sum(grad_normed2 * unit2, axis=0)
     grad_middle = grad_total + norm_back(grad_normed2 * gain_ffn, unit2, scale2)
 
     if fused:
-        grad_normed, qk_term, attn_grad, inner_grad, outer_grad = attention_back(
+        terms = jnp.concatenate(
+            [
+                jnp.zeros((3, width), F32),
+                ffn_term[None],
+                jnp.broadcast_to(squares[:, None], (3, width)),
+                jnp.zeros((1, width), F32),
+                dot(grad_logits, normed2, ((0,), (0,))),
+            ]
+        )
+        hidden_grad, terms, attn_grad, inner_grad, outer_grad, _, _ = attention_back(
             grad_middle.astype(BF16),
             attended_all,
             attn_weight,
@@ -1789,11 +2072,20 @@
             gain_wide,
             turn,
             live_keys,
-            inner_grad,
-            outer_grad,
+            grad_middle,
+            hidden_in,
+            jnp.broadcast_to(gain_attn[None], (8, width)),
+            terms,
+            inner_grad.reshape(n, 2, experts_here * own_rows, ff_here),
+            outer_grad.reshape(fsdp, -1, width),
             9,
         )
-        qk_term = qk_term[0].reshape(2, cols)
+        inner_grad = inner_grad.reshape(own_rows, experts, 2 * ff)
+        outer_grad = outer_grad.reshape(-1, experts, width)
+        terms = lax.dynamic_slice(terms, (0, lax.rem(f, 2) * own_rows), (terms.shape[0], own_rows))
+        gain_grads = terms[:4]
+        router_grad = terms[8:].transpose(1, 0)
+        square_sums = terms[4:7, 0]
     else:
         grad_cols = grad_middle.astype(BF16).reshape(rows, fsdp, cols).transpose(1, 0, 2)
         grad_cols = exchange(grad_cols, ("fsdp",), 5, True).reshape(seq, cols)
@@ -1829,35 +2121,38 @@
         attn_grad = lax.all_to_all(attn_grad, "fsdp", 0, 0, tiled=True)
         inner_grad = lax.all_to_all(inner_grad, BOTH, 0, 0, tiled=True)
         outer_grad = lax.all_to_all(outer_grad, "fsdp", 0, 0, tiled=True)
-    inner_grad = inner_grad.reshape(dp, fsdp, 2, experts_here, own_rows, ff_here)
-    inner_grad = inner_grad.transpose(4, 1, 3, 2, 0, 5).reshape(own_rows, experts, 2 * ff)
-    outer_grad = outer_grad.transpose(2, 0, 1, 3).reshape(-1, experts, width)
+        inner_grad = inner_grad.reshape(dp, fsdp, 2, experts_here, own_rows, ff_here)
+        inner_grad = inner_grad.transpose(4, 1, 3, 2, 0, 5).reshape(own_rows, experts, 2 * ff)
+        outer_grad = outer_grad.transpose(2, 0, 1, 3).reshape(-1, experts, width)
+        attn_term = jnp.sum(grad_normed * unit1, axis=0)
+        hidden_grad = grad_middle + norm_back(grad_normed * gain_attn, unit1, scale1)
+
+        router_term = dot(normed2, grad_logits, ((0,), (0,)))
+        qk_full = jnp.zeros((2, width), F32)
+        qk_full = lax.dynamic_update_slice(qk_full, qk_term, (0, here))
+        terms = jnp.concatenate([attn_term[None], qk_full, ffn_term[None]])
+        terms = terms.reshape(4, n, own_rows).transpose(1, 0, 2).reshape(n, 4 * own_rows)
+        terms = jnp.concatenate(
+            [
+                terms,
+                router_term.reshape(n, own_rows * experts),
+                jnp.broadcast_to(squares[None], (n, 3)),
+            ],
+            axis=1,
+        )
+        term_size = terms.shape[1]
+        term_rows = -(-term_size // 1024) * 8
+        terms = jnp.pad(terms, ((0, 0), (0, term_rows * 128 - term_size)))
+        terms = exchange(terms.reshape(n, term_rows, 128), BOTH, 7, True)
+        terms = jnp.sum(terms, axis=0).reshape(-1)
+        gain_grads = terms[: 4 * own_rows].reshape(4, own_rows)
+        router_grad = terms[4 * own_rows : 4 * own_rows + own_rows * experts]
+        router_grad = router_grad.reshape(own_rows, experts)
+        square_sums = terms[term_size - 3 : term_size]
     attn_grad = attn_grad.reshape(fsdp, own_rows, 4, cols).transpose(1, 2, 0, 3).astype(F32)
     attn_grad = attn_grad.reshape(own_rows, 4 * width)
-    attn_term = jnp.sum(grad_normed * unit1, axis=0)
-    hidden_grad = grad_middle + norm_back(grad_normed * gain_attn, unit1, scale1)
-
-    qk_full = jnp.zeros((2, width), F32)
-    qk_full = lax.dynamic_update_slice(qk_full, qk_term, (0, here))
-    terms = jnp.concatenate([attn_term[None], qk_full, ffn_term[None]])
-    terms = terms.reshape(4, n, own_rows).transpose(1, 0, 2).reshape(n, 4 * own_rows)
-    terms = jnp.concatenate(
-        [
-            terms,
-            router_term.reshape(n, own_rows * experts),
-            jnp.broadcast_to(squares[None], (n, 3)),
-        ],
-        axis=1,
-    )
-    term_size = terms.shape[1]
-    term_rows = -(-term_size // 1024) * 8
-    terms = jnp.pad(terms, ((0, 0), (0, term_rows * 128 - term_size)))
-    terms = exchange(terms.reshape(n, term_rows, 128), BOTH, 7, True)
-    terms = jnp.sum(terms, axis=0).reshape(-1)
-    gain_grads = terms[: 4 * own_rows].reshape(4, own_rows)
-    router_grad = terms[4 * own_rows : 4 * own_rows + own_rows * experts]
     valid_cells = jnp.sum(lengths).astype(F32) * width
-    stats = jnp.sqrt(terms[term_size - 3 : term_size] / valid_cells)
+    stats = jnp.sqrt(square_sums / valid_cells)
 
     return (
         block_total.astype(BF16),
@@ -1868,7 +2163,7 @@
         gain_grads[3],
         attn_grad[:, : 3 * width],
         attn_grad[:, 3 * width :],
-        router_grad.reshape(own_rows, experts),
+        router_grad,
         inner_grad.astype(F32),
         outer_grad.astype(F32),
         stats,

time: 944 us -> 872 us (0.924)
  local copies, waits for them, and re-layouts: 76.3 us -> 24 us
  Pallas kernels: 829 us -> 800 us
    pallas_call x4 -> x1, Pallas kernels: 94.8 us -> 11.1 us  [exchange(): pl.pallas_call(functools.partial(exchange_kernel, axes, n, fsdp, spread),...]
    pallas_call x1, Pallas kernels: 205 us -> 238 us  [attention_back(): pl.pallas_call(functools.partial(attention_back_kernel, dp, fsdp), out_sh...]
    pallas_call x1, Pallas kernels: 278 us -> 303 us  [expert_pass(): pl.pallas_call(functools.partial(expert_kernel, dp, fsdp), out_shape=(sha...]
    convert_element_type x2 -> x0, local copies, waits for them, and re-layouts: 23.1 us -> none  [body(): inner_grad.astype(F32)]
    reshape x7 -> x0, local copies, waits for them, and re-layouts: 16.4 us -> none  [the longest x2 14.6 us: body(): expert_in.reshape(own_rows, fsdp, experts_here, 2, dp, ff_here)]
    unnamed x47 -> x33, local copies, waits for them, and re-layouts: 14.8 us -> 5.09 us
where the time goes in v4:
time: 872 us; the launch traced here: 857 us
  Pallas kernels  800 us (92%)
  other arithmetic  24.7 us (3%)
  local copies, waits for them, and re-layouts  24 us (3%)
    pallas_call x1, Pallas kernels, expert_pass(): pl.pallas_call(functools.partial(expert_kernel, dp, fsdp), out_shape=(sha...  303 us
    pallas_call x1, Pallas kernels, attention_forward(): pl.pallas_call(functools.partial(attention_kernel, dp, fsdp), out_shape=(...  248 us
    pallas_call x1, Pallas kernels, attention_back(): pl.pallas_call(functools.partial(attention_back_kernel, dp, fsdp), out_sh...  238 us

profile of v4, /device:TPU:0, one launch (start us, length us, event | category | flops | bytes accessed | tf_op | source)
XLA Modules:
  0.0 856.6 jit_solution(8646328875648459904)
XLA Ops:
  0.6 0.8 copy.36
  1.5 2.8 concatenate.16
  4.9 11.1 %shard_map.220 = bf16[32,16,128]{2,1,0:T(8,128)(2,1)} custom-call(bf16[16,128]{1,0:T(8,128)(2,1)} %pad_bitcast_fusion.x), custom_call_target="tpu_custom_call" | custom-call | tf_op jit(solution)/shard_map/pallas_call | solution.py:80
  16.0 0.9 copy.44
  18.1 1.2 dynamic_slice.12
  20.0 2.0 fusion.3.cot
  22.0 1.9 multiply_cosine_fusion
  24.2 1.0 pad_maximum_fusion.turn
  25.3 0.7 fusion.9
  28.3 1.1 maximum_bitcast_fusion
  29.4 2.1 reshape.266.weight_in
  31.5 248.0 %shard_map.221 = (bf16[128,2048]{1,0:T(8,128)(2,1)}, bf16[3,1024,256]{2,1,0:T(8,128)(2,1)}, f32[1024,512]{1,0:T(8,128)}, f32[1024,128]{1,0:T(8,128)}, bf16[1024,...) custom-call(bf16[128,2048]{1,0:T(8,128)(2,1)} %hidden.3, ...), custom_call_target="tpu_custom_call" | custom-call | tf_op jit(solution)/shard_map/pallas_call | solution.py:736
  279.5 1.3 multiply_reduce_fusion.2
  280.9 1.3 multiply_convert_fusion.x_in
  284.5 303.5 %shard_map.222 = (f32[2,128,2048]{2,1,0:T(8,128)}, f32[8,8,128]{2,1,0:T(8,128)}, bf16[32,4,64,256]{3,2,1,0:T(8,128)(2,1)}, bf16[8,2,32,2048]{3,2,1,0:T(8,128)(2,...) custom-call(bf16[128,2048]{1,0:T(8,128)(2,1)} %copy-done.1, bf16[4,1024,2048]{2,1,0:T(8,128)(2,1)} %bitcast.73, ...), custom_call_target="tpu_custom_call" | custom-call | tf_op jit(solution)/shard_map/pallas_call | solution.py:1753
  588.0 0.8 slice.74
  588.9 1.2 fusion.14
  590.1 4.1 fusion
  594.2 2.0 pad_maximum_fusion.1
  596.3 1.3 concatenate.19.terms
  597.7 1.6 fusion.12
  599.3 237.8 %shard_map.223 = (f32[128,2048]{1,0:T(8,128)}, f32[24,128]{1,0:T(8,128)}, bf16[8,64,1024]{2,1,0:T(8,128)(2,1)}, bf16[1024,2048]{1,0:T(8,128)(2,1)}, bf16[4,128,2...) custom-call(bf16[128,2048]{1,0:T(8,128)(2,1)} %get-tuple-element.61.grad_rows, ...), custom_call_target="tpu_custom_call" | custom-call | tf_op jit(solution)/shard_map/pallas_call | solution.py:1218
  837.2 6.7 convert.7
  843.9 1.1 reshape.288
  845.0 1.2 copy.37
  846.2 1.2 copy.42
  847.5 1.2 slice.89
  848.7 0.8 slice.90
  849.6 2.5 convert.8
  852.2 0.7 dynamic-slice_bitcast_fusion
  854.7 0.7 sqrt_reduce_fusion
  855.4 1.0 copy.46
  (66 shorter events, 8.9 us)
Async XLA Ops:
  23.9 3.4 copy-start.8
  25.3 2.6 copy-start.9
  31.5 248.0 %copy-start = (bf16[128,2048]{1,0:T(8,128)(2,1)S(1)}, bf16[128,2048]{1,0:T(8,128)(2,1)}, u32[]{:S(2)}) copy-start(bf16[128,2048]{1,0:T(8,128)(2,1)} %hidden.3) | copy-start | bytes 1572868
  279.5 4.3 copy-start.11
  282.2 0.8 copy-start.1
  283.0 0.8 copy-start.5
  590.1 7.6 copy-start.2
  590.1 7.6 copy-start.4
  837.1 6.8 copy-start.6
  847.5 2.2 copy-start.3
  849.6 2.5 copy-start.10
  849.6 3.8 copy-start.12
  849.6 5.8 copy-start.7

commit v5 on v4

--- a/solution.py
+++ b/solution.py
@@ -389,9 +389,58 @@
             {"fsdp": target},
         )
 
-    def slab_copy(p, near, far, send, recv):
-        ref = w_v.at[pl.ds(pl.multiple_of(p * slab, slab), slab)]
-        return remote(ref, ref, send.at[near], recv.at[near], {"dp": far})
+    qkv_cols = pl.ds(0, 3 * cols)
+    out_cols = pl.ds(3 * cols, cols)
+
+    def slab_copy(part, p, near, far, send, recv):
+        lanes = (qkv_cols, out_cols)[part]
+        ref = w_v.at[pl.ds(pl.multiple_of(p * slab, slab), slab), lanes]
+        return remote(ref, ref, send.at[part, near], recv.at[part, near], {"dp": far})
+
+    def slab_start(part):
+        @pl.when(z < dp - 1)
+        def _():
+            slab_copy(part, z, 1, z + 1, right_send, right_recv).start()
+
+        @pl.when(z > 0)
+        def _():
+            slab_copy(part, z, 1, z - 1, left_send, left_recv).start()
+
+    def slab_pass(part, d):
+        @pl.when(z >= d)
+        def _():
+            slab_copy(part, z - d, d, 0, right_send, right_recv).wait_recv()
+
+            @pl.when(z < dp - 1)
+            def _():
+                slab_copy(part, z - d, d + 1, z + 1, right_send, right_recv).start()
+
+        @pl.when(z + d < dp)
+        def _():
+            slab_copy(part, z + d, d, 0, left_send, left_recv).wait_recv()
+
+            @pl.when(z > 0)
+            def _():
+                slab_copy(part, z + d, d + 1, z - 1, left_send, left_recv).start()
+
+    def slab_settle(part):
+        @pl.when(z < dp - 1)
+        def _():
+            slab_copy(part, z, 1, z + 1, right_send, right_recv).wait_send()
+
+        @pl.when(z > 0)
+        def _():
+            slab_copy(part, z, 1, z - 1, left_send, left_recv).wait_send()
+
+        for d in range(1, dp):
+
+            @pl.when((z >= d) & (z < dp - 1))
+            def _(d=d):
+                slab_copy(part, z - d, d + 1, z + 1, right_send, right_recv).wait_send()
+
+            @pl.when((z + d < dp) & (z > 0))
+            def _(d=d):
+                slab_copy(part, z + d, d + 1, z - 1, left_send, left_recv).wait_send()
 
     experts = inner_v.shape[0]
     here = experts // fsdp
@@ -461,20 +510,15 @@
         copy.start()
     for k in range(1, fsdp):
         weight_copy(k).start()
+    for i in range(1, dp):
+        cot_copy(i).start()
     keeps[0].wait()
     hidden_gather.start()
     keeps[1].wait()
     for k in range(1, fsdp):
         weight_copy(k).wait_recv()
 
-    @pl.when(z < dp - 1)
-    def _():
-        slab_copy(z, 1, z + 1, right_send, right_recv).start()
-
-    @pl.when(z > 0)
-    def _():
-        slab_copy(z, 1, z - 1, left_send, left_recv).start()
-
+    slab_start(0)
     hidden_gather.middle()
     keeps[2].wait()
     cot_gather[dp - 1].start()
@@ -517,36 +561,23 @@
     normed_store = pltpu.make_async_copy(normed_v, normed, local.at[0])
     normed_store.start()
 
+    def cot_begin(s):
+        cot_copy(s + 1).wait_recv()
+        cot_gather[s].start()
+
     for d in range(1, dp):
-
-        @pl.when(z >= d)
-        def _(d=d):
-            slab_copy(z - d, d, 0, right_send, right_recv).wait_recv()
-
-            @pl.when(z < dp - 1)
-            def _():
-                slab_copy(z - d, d + 1, z + 1, right_send, right_recv).start()
-
-        @pl.when(z + d < dp)
-        def _(d=d):
-            slab_copy(z + d, d, 0, left_send, left_recv).wait_recv()
-
-            @pl.when(z > 0)
-            def _():
-                slab_copy(z + d, d + 1, z - 1, left_send, left_recv).start()
-
+        slab_pass(0, d)
         if d == 1:
             cot_gather[dp - 1].middle()
-        if d == 2:
+            cot_begin(0)
+        elif d == 2:
             cot_gather[dp - 1].finish()
-
-    for i in range(1, dp):
-        cot_copy(i).start()
+            cot_gather[0].middle()
+            cot_begin(1)
+    slab_start(1)
     for k in range(1, n):
         for copy in inner_copies(k):
             copy.start()
-    weight_store = pltpu.make_async_copy(w_v, weight, local.at[1])
-    weight_store.start()
 
     tile = 256
 
@@ -581,6 +612,9 @@
     for k in range(1, fsdp):
         stat_copy(k).start()
     stat_in[f] = stat[...]
+    cot_gather[0].finish()
+    cot_gather[1].middle()
+    cot_begin(2)
     for k in range(1, fsdp):
         stat_copy(k).wait_recv()
     sums = stat_in[0]
@@ -594,6 +628,9 @@
     means = lax.dot_general(
         sums, corner, (((0,), (0,)), ((), ())), precision=HIGH, preferred_element_type=F32
     )
+    slab_pass(1, 1)
+    cot_gather[1].finish()
+    cot_gather[2].middle()
     scale[...] = lax.rsqrt(means + EPS)
     for i in range(2):
         wide = pl.ds(i * cols, cols)
@@ -625,20 +662,18 @@
 
     lax.fori_loop(0, cols // HEAD_DIM, head, 0)
     attended_gather.start()
-    for s in range(dp - 1):
-        cot_copy(s + 1).wait_recv()
-        cot_gather[s].start()
-        if s == 0:
-            attended_gather.middle()
-    cot_gather[0].middle()
+    slab_pass(1, 2)
+    attended_gather.middle()
+    cot_gather[2].finish()
+    slab_pass(1, 3)
     attended_gather.finish()
-    for s in range(1, dp - 1):
-        cot_gather[s].middle()
     attended_gather.wait()
     attended_store = pltpu.make_async_copy(att_v, attended, local.at[2])
     attended_store.start()
 
-    out_cols = pl.ds(3 * cols, cols)
+    weight_store = pltpu.make_async_copy(w_v, weight, local.at[1])
+    weight_store.start()
+
 
     def project_out(i, carry):
         r = pl.ds(pl.multiple_of(i * tile, tile), tile)
@@ -663,8 +698,6 @@
     for k in range(1, fsdp):
         branch_copy(k).start()
     rows_v[f] = cols_v[pl.ds(pl.multiple_of(f * rows, rows), rows), :]
-    for s in range(dp - 1):
-        cot_gather[s].finish()
     for k in range(1, fsdp):
         branch_copy(k).wait()
     for i in range(fsdp):
@@ -678,24 +711,8 @@
     for i in range(1, dp):
         cot_copy(i).wait_send()
 
-    @pl.when(z < dp - 1)
-    def _():
-        slab_copy(z, 1, z + 1, right_send, right_recv).wait_send()
-
-    @pl.when(z > 0)
-    def _():
-        slab_copy(z, 1, z - 1, left_send, left_recv).wait_send()
-
-    for d in range(1, dp):
-
-        @pl.when((z >= d) & (z < dp - 1))
-        def _(d=d):
-            slab_copy(z - d, d + 1, z + 1, right_send, right_recv).wait_send()
-
-        @pl.when((z + d < dp) & (z > 0))
-        def _(d=d):
-            slab_copy(z + d, d + 1, z - 1, left_send, left_recv).wait_send()
-
+    slab_settle(0)
+    slab_settle(1)
     for k in range(1, fsdp):
         weight_copy(k).wait_send()
         stat_copy(k).wait_send()
@@ -724,9 +741,8 @@
     vmem = pltpu.VMEM
     anywhere = pl.BlockSpec(memory_space=pl.ANY)
     inside = pl.BlockSpec(memory_space=pltpu.VMEM)
-    pairs = [fsdp, dp + 1, dp + 1, 10, fsdp, 10, fsdp]
-    sems = []
-    for size in pairs:
+    sems = [dma((fsdp,)), dma((fsdp,))] + [dma((2, dp + 1))] * 4
+    for size in (10, fsdp, 10, fsdp):
         sems += [dma((size,)), dma((size,))]
     sems += [dma((dp, 10)), dma((dp, 10)), dma((dp,)), dma((dp,))]
     sems += [dma((n, 2)), dma((n, 2)), dma((fsdp,)), dma((fsdp,))]
@@ -799,6 +815,7 @@
     hidden,
     gain_attn,
     terms,
+    first_in,
     inner_in,
     outer_in,
     hidden_grad,
@@ -850,10 +867,10 @@
     s2_recv,
     t_send,
     t_recv,
-    zo_send,
-    zo_recv,
-    zq_send,
-    zq_recv,
+    r_send,
+    r_recv,
+    l_send,
+    l_recv,
     w_send,
     w_recv,
 ):
@@ -871,9 +888,7 @@
     ff = width // 2
     ff_here = ff // dp
 
-    def inner_place(half):
-        lanes = pl.ds(pl.multiple_of(half * ff + z * ff_here, ff_here), ff_here)
-        return inner_out.at[f, :, lanes]
+    inner_place = inner_out.at[f, :, pl.ds(pl.multiple_of(z * ff_here, ff_here), ff_here)]
 
     pair = outer_in.shape[1]
     outer_place = outer_out.at[f // 2, pl.ds(pl.multiple_of(lax.rem(f, 2) * pair, pair), pair)]
@@ -889,8 +904,7 @@
         ),
     ]
     keeps = [
-        pltpu.make_async_copy(inner_in.at[me, 0], inner_place(0), local.at[4]),
-        pltpu.make_async_copy(inner_in.at[me, 1], inner_place(1), local.at[5]),
+        pltpu.make_async_copy(inner_in.at[me], inner_place, local.at[4]),
         pltpu.make_async_copy(outer_in.at[f], outer_place, local.at[6]),
     ]
     for copy in loads:
@@ -906,18 +920,15 @@
             {"fsdp": target},
         )
 
-    def inner_copies(k):
+    def inner_copy(k):
         target = lax.rem(me + k, n)
-        return [
-            remote(
-                inner_in.at[target, half],
-                inner_place(half),
-                in_send.at[k, half],
-                in_recv.at[k, half],
-                place(BOTH, fsdp, target),
-            )
-            for half in range(2)
-        ]
+        return remote(
+            inner_in.at[target],
+            inner_place,
+            in_send.at[k],
+            in_recv.at[k],
+            place(BOTH, fsdp, target),
+        )
 
     def outer_copy(k):
         target = lax.rem(f + k, fsdp)
@@ -928,11 +939,57 @@
     def slab_rows(p):
         return pl.ds(pl.multiple_of(p * slab, slab), slab)
 
-    def far_copy(i, col, send, recv):
-        p = lax.rem(z + i, dp)
+    def right_copy(part, d):
+        lanes = (qkv_cols, out_cols)[part]
         return remote(
-            wgrad.at[slab_rows(p), col], z_in.at[i, :, col], send.at[i], recv.at[i], {"dp": p}
-        )
+            wgrad.at[slab_rows(z + d), lanes],
+            z_in.at[z + d, :, lanes],
+            r_send.at[part, d],
+            r_recv.at[part, d - 1],
+            {"dp": z + 1},
+        )
+
+    def left_copy(part, d):
+        lanes = (qkv_cols, out_cols)[part]
+        return remote(
+            wgrad.at[slab_rows(z - d), lanes],
+            z_in.at[dp if d == 1 else z - d, :, lanes],
+            l_send.at[part, d],
+            l_recv.at[part, d - 1],
+            {"dp": z - 1},
+        )
+
+    def arrived(part, slot, sem):
+        lanes = (qkv_cols, out_cols)[part]
+        ref = z_in.at[slot, :, lanes]
+        remote(ref, ref, sem, sem, plane.to_x).wait_recv()
+
+    def pass_along(part, d):
+        lanes = (qkv_cols, out_cols)[part]
+
+        def add(p):
+            block = slab_rows(p)
+            wgrad[block, lanes] = (
+                wgrad[block, lanes].astype(F32) + z_in[p, :, lanes].astype(F32)
+            ).astype(BF16)
+
+        @pl.when(z + d < dp)
+        def _():
+            @pl.when(z > 0)
+            def _():
+                arrived(part, z + d, r_recv.at[part, d])
+                add(z + d)
+
+            right_copy(part, d).start()
+
+        @pl.when(z >= d)
+        def _():
+            @pl.when(z < dp - 1)
+            def _():
+                arrived(part, z - d, l_recv.at[part, d])
+                add(z - d)
+
+            left_copy(part, d).start()
 
     qkv_cols = pl.ds(0, 3 * cols)
     out_cols = pl.ds(3 * cols, cols)
@@ -940,8 +997,7 @@
     for k in range(1, fsdp):
         cols_copy(k).start()
     for k in range(1, n):
-        for copy in inner_copies(k):
-            copy.start()
+        inner_copy(k).start()
     for k in range(1, fsdp):
         outer_copy(k).start()
     for copy in keeps:
@@ -969,9 +1025,8 @@
     lax.fori_loop(0, fsdp // 2, out_grads, 0)
     sum1.add_core()
     lax.fori_loop(fsdp // 2, fsdp, out_grads, 0)
-    for i in range(1, dp):
-        far_copy(i, out_cols, zo_send, zo_recv).start()
     sum1.pass_on()
+    pass_along(1, 3)
     gk[...] = jnp.zeros_like(gk)
     gval[...] = jnp.zeros_like(gval)
     gatt[...] = sum1.total().astype(BF16)
@@ -1006,6 +1061,8 @@
 
     lax.fori_loop(0, cols // HEAD_DIM, head, 0)
 
+    pass_along(1, 2)
+
     heads_here = cols // HEAD_DIM
     for i, source in enumerate((gq, gk)):
         for h in range(heads_here):
@@ -1074,16 +1131,16 @@
             block = pl.ds(pl.multiple_of(p * slab + i * (slab // 2), slab // 2), slab // 2)
             wgrad[block, qkv_cols] = dot(normed_v[:, block], gqkv[...], ((0,), (0,))).astype(BF16)
 
-    for i in range(1, dp):
-        qkv_grads(lax.rem(z + i, dp))
-        far_copy(i, qkv_cols, zq_send, zq_recv).start()
-        if i == 1:
-            sum2.add_core()
-        if i == 2:
-            sum2.pass_on()
-    qkv_grads(z)
+    for p in range(dp):
+        qkv_grads(p)
+    pass_along(0, 3)
+    sum2.add_core()
+    pass_along(1, 1)
+    pass_along(0, 2)
+    sum2.pass_on()
 
     grad = sum2.total()
+    pass_along(0, 1)
     values = hidden[...].astype(F32)
     scale1 = lax.rsqrt(jnp.mean(values * values, axis=-1, keepdims=True) + EPS)
     values = values * scale1
@@ -1114,11 +1171,14 @@
     outer_load = pltpu.make_async_copy(outer_out, core2, local.at[0])
     outer_load.start()
     for k in range(1, n):
-        for copy in inner_copies(k):
-            copy.wait()
-    inner_load = pltpu.make_async_copy(inner_out, part2, local.at[1])
-    inner_load.start()
-    experts = fsdp * (inner_in.shape[2] // own_rows)
+        inner_copy(k).wait()
+    inner_loads = [
+        pltpu.make_async_copy(first_in, part2.at[:, :, pl.ds(0, ff)], local.at[1]),
+        pltpu.make_async_copy(inner_out, part2.at[:, :, pl.ds(ff, ff)], local.at[2]),
+    ]
+    for copy in inner_loads:
+        copy.start()
+    experts = fsdp * (inner_in.shape[1] // own_rows)
     outer_load.wait()
     outer_rows = core2.shape[0] * core2.shape[1]
     inner_rows = part2.shape[0] * part2.shape[1]
@@ -1133,7 +1193,8 @@
         experts,
         outer_rows // experts,
     )
-    inner_load.wait()
+    for copy in inner_loads:
+        copy.wait()
 
     def put_inner(i, tile, lanes, value):
         normed_v[pl.ds(pl.multiple_of(i * tile, tile), tile), lanes] = value
@@ -1151,13 +1212,32 @@
     for store in stores:
         store.start()
 
-    for i in range(1, dp):
-        far_copy(i, out_cols, zo_send, zo_recv).wait()
-    for i in range(1, dp):
-        far_copy(i, qkv_cols, zq_send, zq_recv).wait()
-    total = wgrad[slab_rows(z), :].astype(F32)
-    for i in range(1, dp):
-        total += z_in[i].astype(F32)
+    @pl.when(z > 0)
+    def _():
+        for part in range(2):
+            arrived(part, z, r_recv.at[part, 0])
+        total = wgrad[slab_rows(z), :].astype(F32) + z_in[z].astype(F32)
+        wgrad[slab_rows(z), :] = total.astype(BF16)
+
+    @pl.when(z < dp - 1)
+    def _():
+        for part in range(2):
+            arrived(part, dp, l_recv.at[part, 0])
+        total = wgrad[slab_rows(z), :].astype(F32) + z_in[dp].astype(F32)
+        wgrad[slab_rows(z), :] = total.astype(BF16)
+
+    for part in range(2):
+        for d in range(1, dp):
+
+            @pl.when(z + d < dp)
+            def _(part=part, d=d):
+                right_copy(part, d).wait_send()
+
+            @pl.when(z >= d)
+            def _(part=part, d=d):
+                left_copy(part, d).wait_send()
+
+    total = wgrad[slab_rows(z), :]
     wsum[...] = total.astype(BF16).reshape(wsum.shape)
 
     def owner_copy(k):
@@ -1199,6 +1279,7 @@
     hidden,
     gain_attn,
     terms,
+    first_in,
     inner_in,
     outer_in,
     ident,
@@ -1223,10 +1304,10 @@
             shape((fsdp, own_rows, 4 * cols), BF16),
             shape((seq, width), BF16),
             shape((4, rows, width), BF16),
-            shape((fsdp, rows, width), BF16),
+            shape((fsdp, rows, width // 2), BF16),
             shape((4, rows, width), BF16),
         ),
-        in_specs=[anywhere] * 4 + [inside] * 10 + [anywhere] * 2,
+        in_specs=[anywhere] * 4 + [inside] * 10 + [anywhere] * 3,
         out_specs=(inside,) * 3 + (anywhere,) * 4,
         scratch_shapes=[
             vmem((fsdp, seq, cols), BF16),
@@ -1252,15 +1333,15 @@
             vmem((8, seq), F32),
             vmem((fsdp, 8, seq), F32),
             vmem((width, 4 * cols), BF16),
-            vmem((dp, fsdp * own_rows, 4 * cols), BF16),
+            vmem((dp + 1, fsdp * own_rows, 4 * cols), BF16),
             vmem((fsdp, own_rows, 4 * cols), BF16),
             vmem(terms.shape, F32),
             vmem((n, terms.shape[0], 128), F32),
             dma((7,)),
             dma((n,)),
             dma((n,)),
-            dma((n, 2)),
-            dma((n, 2)),
+            dma((n,)),
+            dma((n,)),
             dma((fsdp,)),
             dma((fsdp,)),
             dma((fsdp,)),
@@ -1271,10 +1352,10 @@
             dma((8,)),
             dma((fsdp,)),
             dma((fsdp,)),
-            dma((dp,)),
-            dma((dp,)),
-            dma((dp,)),
-            dma((dp,)),
+            dma((2, dp)),
+            dma((2, dp)),
+            dma((2, dp)),
+            dma((2, dp)),
             dma((fsdp,)),
             dma((fsdp,)),
         ],
@@ -1296,6 +1377,7 @@
         hidden,
         gain_attn,
         terms,
+        first_in,
         inner_in,
         outer_in,
     )
@@ -1311,6 +1393,7 @@
     outer_in,
     sums,
     gate_sum,
+    first_out,
     inner_out,
     outer_out,
     gathered,
@@ -1329,6 +1412,7 @@
     core_in,
     half_in,
     full_in,
+    leaving,
     gates_in,
     grads_out,
     grads_in,
@@ -1337,6 +1421,8 @@
     g_recv,
     gg_send,
     gg_recv,
+    f_send,
+    f_recv,
     z_send,
     z_recv,
     a_send,
@@ -1448,25 +1534,28 @@
 
     def out_copy(s, k):
         return remote(
-            held.at[k, chip], far.at[k, z], o_send.at[s, k], o_recv.at[s, k], {"dp": plane_at(s)}
+            leaving.at[lax.rem(s, 2), k],
+            far.at[k, z],
+            o_send.at[s, k],
+            o_recv.at[s, k],
+            {"dp": plane_at(s)},
         )
 
     def add_core():
+        def add_block(k, j):
+            core_copy(k, j).wait()
+            held[k, j] = (
+                part[k, block_rows(j * 2 + core)].astype(F32) + core_in[k, j].astype(F32)
+            ).astype(BF16)
+
         for k in range(2):
-            for j in range(4):
-                core_copy(k, j).wait()
-            def one(j, carry):
-                held[k, j] = (
-                    part[k, block_rows(j * 2 + core)].astype(F32) + core_in[k, j].astype(F32)
-                ).astype(BF16)
-                return carry
-            lax.fori_loop(0, 4, one, 0)
-        pl.semaphore_signal(credit, inc=1, device_id=to_c, device_id_type=MESH_ID)
-
-    def start_half():
-        for k in range(2):
+            add_block(k, chip_d)
             for copy in half_copies(k):
                 copy.start()
+        for k in range(2):
+            for j in (chip_x, chip_y, chip):
+                add_block(k, j)
+        pl.semaphore_signal(credit, inc=1, device_id=to_c, device_id_type=MESH_ID)
 
     def pass_full():
         for k in range(2):
@@ -1507,6 +1596,22 @@
             grads_in.at[me],
             gg_send.at[k],
             gg_recv.at[k],
+            place(BOTH, fsdp, target),
+        )
+
+    own_rows = wi.shape[2]
+    first_lanes = pl.ds(pl.multiple_of(z * wi.shape[3], wi.shape[3]), wi.shape[3])
+
+    def first_ref(e):
+        return first_out.at[f, pl.ds(e * own_rows, own_rows), first_lanes]
+
+    def first_copy(k, e):
+        target = lax.rem(me + k, n)
+        return remote(
+            wi.at[e, target],
+            first_ref(e),
+            f_send.at[k, e],
+            f_recv.at[k, e],
             place(BOTH, fsdp, target),
         )
 
@@ -1551,6 +1656,7 @@
         far_copy(i).start()
     middle_gather(0)
     end_gather(0)
+    begin_gather(1)
     for k in range(1, n):
         gate_copy(k).wait()
 
@@ -1630,7 +1736,7 @@
             ).wait()
         @pl.when(s < dp - 1)
         def _():
-            begin_gather(s + 1)
+            middle_gather(s + 1)
 
         tile_step(0)
 
@@ -1638,9 +1744,9 @@
         def _():
             pass_full()
 
-        @pl.when(s < dp - 1)
+        @pl.when(s < dp - 2)
         def _():
-            middle_gather(s + 1)
+            begin_gather(s + 2)
 
         tile_step(1)
 
@@ -1661,18 +1767,28 @@
 
         @pl.when(s > 0)
         def _():
+            @pl.when(s > 2)
+            def _():
+                for k in range(2):
+                    out_copy(s - 3, k).wait_send()
+
             for k in range(2):
-                held[k, chip] = total_here(k).astype(BF16)
+                leaving[lax.rem(s - 1, 2), k] = total_here(k).astype(BF16)
                 out_copy(s - 1, k).start()
-            for k in range(2):
-                out_copy(s - 1, k).wait_send()
 
         add_core()
-        start_half()
 
         @pl.when(s < dp - 1)
         def _():
             end_gather(s + 1)
+
+        @pl.when(s == dp - 1)
+        def _():
+            for e in range(2):
+                wi[e] = gi[e].astype(BF16).reshape(wi.shape[1:])
+            for k in range(1, n):
+                for e in range(2):
+                    first_copy(k, e).start()
 
         return carry
 
@@ -1682,13 +1798,14 @@
     for k in range(1, n):
         gate_grad_copy(k).start()
     grads_in[me] = grads_out[me]
-    for q in range(4):
+    for q in range(2, 4):
         wi[q] = gi[q].astype(BF16).reshape(wi.shape[1:])
     for e in range(2):
         wo[e] = go[e].astype(BF16).reshape(wo.shape[1:])
     stores = []
-    for q in range(4):
-        stores.append(pltpu.make_async_copy(wi.at[q], inner_out.at[:, q], local.at[q]))
+    for e in range(2):
+        stores.append(pltpu.make_async_copy(wi.at[e, me], first_ref(e), local.at[e]))
+        stores.append(pltpu.make_async_copy(wi.at[2 + e], inner_out.at[:, e], local.at[2 + e]))
     for e in range(2):
         stores.append(pltpu.make_async_copy(wo.at[e], outer_out.at[:, e], local.at[4 + e]))
     for store in stores:
@@ -1696,6 +1813,8 @@
     pl.semaphore_wait(credit, 1)
     for i in range(1, dp):
         for k in range(2):
+            if i > dp - 3:
+                out_copy(i - 1, k).wait_send()
             remote(
                 held.at[k, chip],
                 far.at[k, lax.rem(z + dp - i, dp)],
@@ -1722,6 +1841,8 @@
         sums[k] = total
     for k in range(1, n):
         gate_grad_copy(k).wait()
+        for e in range(2):
+            first_copy(k, e).wait()
     for j in range(fsdp):
         total = grads_in[j]
         for i in range(1, dp):
@@ -1755,13 +1876,14 @@
         out_shape=(
             shape((2, rows, width), F32),
             shape((fsdp, 8, 128), F32),
-            shape(inner_in.shape, BF16),
+            shape((fsdp, 2 * own_rows, dp * ff_here), BF16),
+            shape((n, 2, own_rows, ff_here), BF16),
             shape(outer_in.shape, BF16),
             shape((dp, fsdp, rows, width), BF16),
             shape((2, dp, rows, width), BF16),
         ),
         in_specs=[anywhere] * 5,
-        out_specs=(pl.BlockSpec(memory_space=pltpu.VMEM),) * 2 + (anywhere,) * 4,
+        out_specs=(pl.BlockSpec(memory_space=pltpu.VMEM),) * 2 + (anywhere,) * 5,
         scratch_shapes=[
             pltpu.VMEM((chunk, width), BF16),
             pltpu.VMEM((chunk, width), BF16),
@@ -1777,6 +1899,7 @@
             pltpu.VMEM((2, 4, rows, width), BF16),
             pltpu.VMEM((2, 2, rows // 2, width), BF16),
             pltpu.VMEM((2, 2, rows, width), BF16),
+            pltpu.VMEM((2, 2, rows, width), BF16),
             pltpu.VMEM((n, 8, 128), F32),
             pltpu.VMEM((n, 8, 128), F32),
             pltpu.VMEM((n, 8, 128), F32),
@@ -1785,6 +1908,8 @@
             dma((n,)),
             dma((n,)),
             dma((n,)),
+            dma((n, 2)),
+            dma((n, 2)),
             dma((dp,)),
             dma((dp,)),
             dma((dp, 2)),
@@ -1807,7 +1932,7 @@
             collective_id=ident, has_side_effects=True, vmem_limit_bytes=63 * 1024 * 1024
         ),
     )(x_in, c_all, gates, inner_in, outer_in)
-    return got[:4]
+    return got[:5]
 
 
 def expert_pass_dense(normed2, grad_all, gates, inner_weight, outer_weight):
@@ -2016,7 +2141,7 @@
     gates = gates.reshape(n, experts_here, rows)
     gates = jnp.pad(gates, ((0, 0), (0, 8 - experts_here), (0, 0)))
     if fused:
-        sums, grad_gates, inner_grad, outer_grad = expert_pass(
+        sums, grad_gates, first_grad, inner_grad, outer_grad = expert_pass(
             normed2, grad_all.reshape(dp, seq, width), gates, inner_weight, outer_weight, 8
         )
         expert_sum = sums[0]
@@ -2076,7 +2201,8 @@
             hidden_in,
             jnp.broadcast_to(gain_attn[None], (8, width)),
             terms,
-            inner_grad.reshape(n, 2, experts_here * own_rows, ff_here),
+            first_grad,
+            inner_grad.reshape(n, experts_here * own_rows, ff_here),
             outer_grad.reshape(fsdp, -1, width),
             9,
         )

time: 872 us -> 800 us (0.917)
  Pallas kernels: 800 us -> 735 us
    pallas_call x1, Pallas kernels: 238 us -> 191 us  [attention_back(): pl.pallas_call(functools.partial(attention_back_kernel, dp, fsdp), out_sh...]
    pallas_call x1, Pallas kernels: 303 us -> 290 us  [expert_pass(): pl.pallas_call(functools.partial(expert_kernel, dp, fsdp), out_shape=(sha...]
where the time goes in v5:
time: 800 us; the launch traced here: 791 us
  Pallas kernels  735 us (92%)
  other arithmetic  24.7 us (3%)
  local copies, waits for them, and re-layouts  23.3 us (3%)
    pallas_call x1, Pallas kernels, expert_pass(): pl.pallas_call(functools.partial(expert_kernel, dp, fsdp), out_shape=(sha...  290 us
    pallas_call x1, Pallas kernels, attention_forward(): pl.pallas_call(functools.partial(attention_kernel, dp, fsdp), out_shape=(...  242 us
    pallas_call x1, Pallas kernels, attention_back(): pl.pallas_call(functools.partial(attention_back_kernel, dp, fsdp), out_sh...  191 us

profile of v5, /device:TPU:0, one launch (start us, length us, event | category | flops | bytes accessed | tf_op | source)
XLA Modules:
  0.0 790.8 jit_solution(12749866611903870204)
XLA Ops:
  0.6 0.8 copy.36
  1.5 2.8 concatenate.16
  4.9 11.1 %shard_map.220 = bf16[32,16,128]{2,1,0:T(8,128)(2,1)} custom-call(bf16[16,128]{1,0:T(8,128)(2,1)} %pad_bitcast_fusion.x), custom_call_target="tpu_custom_call" | custom-call | tf_op jit(solution)/shard_map/pallas_call | solution.py:80
  16.0 0.9 copy.44
  18.1 1.2 dynamic_slice.12
  20.0 2.0 fusion.3.cot
  22.0 1.9 multiply_cosine_fusion
  24.2 1.0 pad_maximum_fusion.turn
  25.3 0.7 fusion.9
  28.3 1.1 maximum_bitcast_fusion
  29.4 1.5 reshape.266.weight_in
  31.0 242.4 %shard_map.221 = (bf16[128,2048]{1,0:T(8,128)(2,1)}, bf16[3,1024,256]{2,1,0:T(8,128)(2,1)}, f32[1024,512]{1,0:T(8,128)}, f32[1024,128]{1,0:T(8,128)}, bf16[1024,...) custom-call(bf16[128,2048]{1,0:T(8,128)(2,1)} %hidden.3, ...), custom_call_target="tpu_custom_call" | custom-call | tf_op jit(solution)/shard_map/pallas_call | solution.py:752
  273.4 1.3 multiply_reduce_fusion.2
  274.8 1.3 multiply_convert_fusion.x_in
  278.5 290.1 %shard_map.222 = (f32[2,128,2048]{2,1,0:T(8,128)}, f32[8,8,128]{2,1,0:T(8,128)}, bf16[8,128,1024]{2,1,0:T(8,128)(2,1)}, bf16[32,2,64,256]{3,2,1,0:T(8,128)(2,1)}...) custom-call(bf16[128,2048]{1,0:T(8,128)(2,1)} %copy-done.1, ...), custom_call_target="tpu_custom_call" | custom-call | tf_op jit(solution)/shard_map/pallas_call | solution.py:1874
  568.6 0.8 slice.74
  569.4 1.2 fusion.14
  570.6 4.1 fusion
  574.7 2.0 pad_maximum_fusion.1
  576.9 1.3 concatenate.19.terms
  578.2 1.6 fusion.12
  579.8 191.4 %shard_map.223 = (f32[128,2048]{1,0:T(8,128)}, f32[24,128]{1,0:T(8,128)}, bf16[8,64,1024]{2,1,0:T(8,128)(2,1)}, bf16[1024,2048]{1,0:T(8,128)(2,1)}, bf16[4,128,2...) custom-call(bf16[128,2048]{1,0:T(8,128)(2,1)} %get-tuple-element.63.grad_rows, ...), custom_call_target="tpu_custom_call" | custom-call | tf_op jit(solution)/shard_map/pallas_call | solution.py:1299
  771.2 6.7 convert.7
  778.0 0.9 reshape.288
  779.0 1.2 copy.37
  780.2 1.2 copy.42
  781.4 1.2 slice.89
  782.6 0.8 slice.90
  783.5 2.5 convert.8
  786.1 0.7 dynamic-slice_bitcast_fusion
  788.6 0.7 sqrt_reduce_fusion
  789.4 1.0 copy.46
  (66 shorter events, 8.9 us)
Async XLA Ops:
  23.9 3.4 copy-start.8
  25.3 2.6 copy-start.9
  31.0 242.4 %copy-start = (bf16[128,2048]{1,0:T(8,128)(2,1)S(1)}, bf16[128,2048]{1,0:T(8,128)(2,1)}, u32[]{:S(2)}) copy-start(bf16[128,2048]{1,0:T(8,128)(2,1)} %hidden.3) | copy-start | bytes 1572868
  273.4 4.3 copy-start.11
  276.1 0.8 copy-start.1
  276.9 0.8 copy-start.5
  570.6 7.6 copy-start.2
  570.6 7.6 copy-start.4
  771.2 6.8 copy-start.6
  781.4 2.2 copy-start.3
  783.5 2.5 copy-start.10
  783.5 3.8 copy-start.12
  783.5 5.8 copy-start.7

commit v6 on v5

--- a/solution.py
+++ b/solution.py
@@ -113,6 +113,12 @@
     return pltpu.make_async_remote_copy(
         src, dst, send, recv, device_id=device, device_id_type=MESH_ID
     )
+
+
+def spread(z, f, dp, fsdp, k):
+    step = k % dp
+    step = (step + 1) // 2 if step % 2 else dp - step // 2
+    return lax.rem(z + step, dp) * fsdp + lax.rem(f + k // dp, fsdp)
 
 
 def greet_all(n, fsdp, me):
@@ -453,7 +459,7 @@
         return inner_v.at[owned, :, lanes], inner_out.at[me, pl.ds(half * here, here)]
 
     def inner_copies(k):
-        target = lax.rem(me + k, n)
+        target = spread(z, f, dp, fsdp, k)
         return [
             remote(
                 *inner_block(target, half),
@@ -840,8 +846,6 @@
     half2,
     full2,
     gatt,
-    gq,
-    gk,
     gval,
     gqk,
     gqkv,
@@ -849,7 +853,6 @@
     stat_in,
     wgrad,
     z_in,
-    wsum,
     term_v,
     term_in,
     local,
@@ -921,7 +924,7 @@
         )
 
     def inner_copy(k):
-        target = lax.rem(me + k, n)
+        target = spread(z, f, dp, fsdp, k)
         return remote(
             inner_in.at[target],
             inner_place,
@@ -940,7 +943,7 @@
         return pl.ds(pl.multiple_of(p * slab, slab), slab)
 
     def right_copy(part, d):
-        lanes = (qkv_cols, out_cols)[part]
+        lanes = parts[part]
         return remote(
             wgrad.at[slab_rows(z + d), lanes],
             z_in.at[z + d, :, lanes],
@@ -950,7 +953,7 @@
         )
 
     def left_copy(part, d):
-        lanes = (qkv_cols, out_cols)[part]
+        lanes = parts[part]
         return remote(
             wgrad.at[slab_rows(z - d), lanes],
             z_in.at[dp if d == 1 else z - d, :, lanes],
@@ -960,12 +963,12 @@
         )
 
     def arrived(part, slot, sem):
-        lanes = (qkv_cols, out_cols)[part]
+        lanes = parts[part]
         ref = z_in.at[slot, :, lanes]
         remote(ref, ref, sem, sem, plane.to_x).wait_recv()
 
     def pass_along(part, d):
-        lanes = (qkv_cols, out_cols)[part]
+        lanes = parts[part]
 
         def add(p):
             block = slab_rows(p)
@@ -993,6 +996,7 @@
 
     qkv_cols = pl.ds(0, 3 * cols)
     out_cols = pl.ds(3 * cols, cols)
+    parts = (pl.ds(0, 2 * cols), out_cols, pl.ds(2 * cols, cols))
 
     for k in range(1, fsdp):
         cols_copy(k).start()
@@ -1027,7 +1031,7 @@
     lax.fori_loop(fsdp // 2, fsdp, out_grads, 0)
     sum1.pass_on()
     pass_along(1, 3)
-    gk[...] = jnp.zeros_like(gk)
+    gqk[...] = jnp.zeros_like(gqk)
     gval[...] = jnp.zeros_like(gval)
     gatt[...] = sum1.total().astype(BF16)
 
@@ -1035,6 +1039,7 @@
 
     def head(h, carry):
         lane = pl.ds(pl.multiple_of(h * HEAD_DIM, HEAD_DIM), HEAD_DIM)
+        key_lane = pl.ds(pl.multiple_of(cols + h * HEAD_DIM, HEAD_DIM), HEAD_DIM)
         for t in range(seq // tile):
             r = pl.ds(t * tile, tile)
             extent = (t + 1) * tile
@@ -1054,21 +1059,33 @@
             grad_probs = dot(grad, value, ((1,), (1,)))
             mean = jnp.sum(probs * grad_probs, axis=-1, keepdims=True)
             grad_scores = (probs * (grad_probs - mean)).astype(BF16)
-            gq[r, lane] = dot(grad_scores, key, ((1,), (0,)))
-            gk[upto, lane] += dot(grad_scores, query, ((0,), (0,)))
+            gqk[r, lane] = dot(grad_scores, key, ((1,), (0,)))
+            gqk[upto, key_lane] += dot(grad_scores, query, ((0,), (0,)))
             gval[upto, lane] += dot(probs.astype(BF16), grad, ((0,), (0,)))
         return carry
 
     lax.fori_loop(0, cols // HEAD_DIM, head, 0)
 
+    def column_grads(part):
+        lanes = parts[part]
+
+        def one(i, carry):
+            block = pl.ds(pl.multiple_of(i * 256, 256), 256)
+            wgrad[block, lanes] = dot(normed_v[:, block], gqkv[:, lanes], ((0,), (0,))).astype(BF16)
+            return carry
+
+        lax.fori_loop(0, width // 256, one, 0)
+
+    gqkv[:, parts[2]] = gval[...].astype(BF16)
+    column_grads(2)
     pass_along(1, 2)
+    pass_along(2, 3)
 
     heads_here = cols // HEAD_DIM
-    for i, source in enumerate((gq, gk)):
+    for i in range(2):
         for h in range(heads_here):
-            lane = pl.ds(h * HEAD_DIM, HEAD_DIM)
             wide = pl.ds(i * cols + h * HEAD_DIM, HEAD_DIM)
-            grad = source[:, lane] * scaling
+            grad = gqk[:, wide] * scaling
             grad = grad * turn[0] + pltpu.roll(grad, HEAD_DIM // 2, 1) * turn[1]
             place_lanes = pl.ds(pl.multiple_of(f * cols + h * HEAD_DIM, HEAD_DIM), HEAD_DIM)
             term_v[1 + i : 2 + i, place_lanes] = jnp.sum(
@@ -1094,7 +1111,8 @@
     for k in range(1, fsdp):
         stat_copy(k).start()
     stat_in[f] = stat[...]
-    gqkv[:, pl.ds(2 * cols, cols)] = gval[...].astype(BF16)
+    pass_along(1, 1)
+    pass_along(2, 2)
     for k in range(1, fsdp):
         stat_copy(k).wait_recv()
     sums = stat_in[0]
@@ -1126,16 +1144,10 @@
     sum2 = PlaneSum(plane, part2, held2, core2, half2, full2, s2_send, s2_recv)
     sum2.start()
 
-    def qkv_grads(p):
-        for i in range(2):
-            block = pl.ds(pl.multiple_of(p * slab + i * (slab // 2), slab // 2), slab // 2)
-            wgrad[block, qkv_cols] = dot(normed_v[:, block], gqkv[...], ((0,), (0,))).astype(BF16)
-
-    for p in range(dp):
-        qkv_grads(p)
+    column_grads(0)
     pass_along(0, 3)
     sum2.add_core()
-    pass_along(1, 1)
+    pass_along(2, 1)
     pass_along(0, 2)
     sum2.pass_on()
 
@@ -1214,19 +1226,19 @@
 
     @pl.when(z > 0)
     def _():
-        for part in range(2):
+        for part in range(3):
             arrived(part, z, r_recv.at[part, 0])
         total = wgrad[slab_rows(z), :].astype(F32) + z_in[z].astype(F32)
         wgrad[slab_rows(z), :] = total.astype(BF16)
 
     @pl.when(z < dp - 1)
     def _():
-        for part in range(2):
+        for part in range(3):
             arrived(part, dp, l_recv.at[part, 0])
         total = wgrad[slab_rows(z), :].astype(F32) + z_in[dp].astype(F32)
         wgrad[slab_rows(z), :] = total.astype(BF16)
 
-    for part in range(2):
+    for part in range(3):
         for d in range(1, dp):
 
             @pl.when(z + d < dp)
@@ -1237,18 +1249,19 @@
             def _(part=part, d=d):
                 left_copy(part, d).wait_send()
 
-    total = wgrad[slab_rows(z), :]
-    wsum[...] = total.astype(BF16).reshape(wsum.shape)
+    def owner_rows(target):
+        return wgrad.at[pl.ds(pl.multiple_of(z * slab + target * own_rows, own_rows), own_rows)]
 
     def owner_copy(k):
         target = lax.rem(f + k, fsdp)
         return remote(
-            wsum.at[target], owned.at[f], w_send.at[k], w_recv.at[k], {"fsdp": target}
+            owner_rows(target), owned.at[f], w_send.at[k], w_recv.at[k], {"fsdp": target}
         )
 
     for k in range(1, fsdp):
         owner_copy(k).start()
-    owned[f] = wsum[f]
+    own_block = pl.multiple_of(z * slab + f * own_rows, own_rows)
+    owned[f] = wgrad[pl.ds(own_block, own_rows), :]
     for k in range(1, fsdp):
         owner_copy(k).wait()
     for k in range(1, fsdp):
@@ -1326,15 +1339,12 @@
             vmem((2, rows, width), BF16),
             vmem((seq, cols), BF16),
             vmem((seq, cols), F32),
-            vmem((seq, cols), F32),
-            vmem((seq, cols), F32),
             vmem((seq, 2 * cols), F32),
             vmem((seq, 3 * cols), BF16),
             vmem((8, seq), F32),
             vmem((fsdp, 8, seq), F32),
             vmem((width, 4 * cols), BF16),
             vmem((dp + 1, fsdp * own_rows, 4 * cols), BF16),
-            vmem((fsdp, own_rows, 4 * cols), BF16),
             vmem(terms.shape, F32),
             vmem((n, terms.shape[0], 128), F32),
             dma((7,)),
@@ -1352,10 +1362,10 @@
             dma((8,)),
             dma((fsdp,)),
             dma((fsdp,)),
-            dma((2, dp)),
-            dma((2, dp)),
-            dma((2, dp)),
-            dma((2, dp)),
+            dma((3, dp)),
+            dma((3, dp)),
+            dma((3, dp)),
+            dma((3, dp)),
             dma((fsdp,)),
             dma((fsdp,)),
         ],
@@ -1606,7 +1616,7 @@
         return first_out.at[f, pl.ds(e * own_rows, own_rows), first_lanes]
 
     def first_copy(k, e):
-        target = lax.rem(me + k, n)
+        target = spread(z, f, dp, fsdp, k)
         return remote(
             wi.at[e, target],
             first_ref(e),

time: 800 us -> 765 us (0.956)
  Pallas kernels: 735 us -> 700 us
    pallas_call x1, Pallas kernels: 191 us -> 173 us  [attention_back(): pl.pallas_call(functools.partial(attention_back_kernel, dp, fsdp), out_sh...]
    pallas_call x1, Pallas kernels: 242 us -> 225 us  [attention_forward(): pl.pallas_call(functools.partial(attention_kernel, dp, fsdp), out_shape=(...]
where the time goes in v6:
time: 765 us; the launch traced here: 756 us
  Pallas kernels  700 us (92%)
  other arithmetic  24.7 us (3%)
  local copies, waits for them, and re-layouts  23.3 us (3%)
    pallas_call x1, Pallas kernels, expert_pass(): pl.pallas_call(functools.partial(expert_kernel, dp, fsdp), out_shape=(sha...  291 us
    pallas_call x1, Pallas kernels, attention_forward(): pl.pallas_call(functools.partial(attention_kernel, dp, fsdp), out_shape=(...  225 us
    pallas_call x1, Pallas kernels, attention_back(): pl.pallas_call(functools.partial(attention_back_kernel, dp, fsdp), out_sh...  173 us

profile of v6, /device:TPU:0, one launch (start us, length us, event | category | flops | bytes accessed | tf_op | source)
XLA Modules:
  0.0 756.0 jit_solution(5658340745580380489)
XLA Ops:
  0.6 0.8 copy.36
  1.5 2.8 concatenate.16
  4.9 11.1 %shard_map.220 = bf16[32,16,128]{2,1,0:T(8,128)(2,1)} custom-call(bf16[16,128]{1,0:T(8,128)(2,1)} %pad_bitcast_fusion.x), custom_call_target="tpu_custom_call" | custom-call | tf_op jit(solution)/shard_map/pallas_call | solution.py:80
  16.0 0.9 copy.44
  18.1 1.2 dynamic_slice.12
  20.0 2.0 fusion.3.cot
  22.0 1.9 multiply_cosine_fusion
  24.2 1.0 pad_maximum_fusion.turn
  25.3 0.7 fusion.9
  28.3 1.1 maximum_bitcast_fusion
  29.4 1.5 reshape.266.weight_in
  31.0 224.6 %shard_map.221 = (bf16[128,2048]{1,0:T(8,128)(2,1)}, bf16[3,1024,256]{2,1,0:T(8,128)(2,1)}, f32[1024,512]{1,0:T(8,128)}, f32[1024,128]{1,0:T(8,128)}, bf16[1024,...) custom-call(bf16[128,2048]{1,0:T(8,128)(2,1)} %hidden.3, ...), custom_call_target="tpu_custom_call" | custom-call | tf_op jit(solution)/shard_map/pallas_call | solution.py:758
  255.6 1.3 multiply_reduce_fusion.2
  257.0 1.3 multiply_convert_fusion.x_in
  260.6 291.4 %shard_map.222 = (f32[2,128,2048]{2,1,0:T(8,128)}, f32[8,8,128]{2,1,0:T(8,128)}, bf16[8,128,1024]{2,1,0:T(8,128)(2,1)}, bf16[32,2,64,256]{3,2,1,0:T(8,128)(2,1)}...) custom-call(bf16[128,2048]{1,0:T(8,128)(2,1)} %copy-done.1, ...), custom_call_target="tpu_custom_call" | custom-call | tf_op jit(solution)/shard_map/pallas_call | solution.py:1884
  552.0 0.8 slice.74
  552.8 1.2 fusion.14
  554.1 4.1 fusion
  558.2 2.0 pad_maximum_fusion.1
  560.3 1.3 concatenate.19.terms
  561.7 1.6 fusion.12
  563.3 173.2 %shard_map.223 = (f32[128,2048]{1,0:T(8,128)}, f32[24,128]{1,0:T(8,128)}, bf16[8,64,1024]{2,1,0:T(8,128)(2,1)}, bf16[1024,2048]{1,0:T(8,128)(2,1)}, bf16[4,128,2...) custom-call(bf16[128,2048]{1,0:T(8,128)(2,1)} %get-tuple-element.63.grad_rows, ...), custom_call_target="tpu_custom_call" | custom-call | tf_op jit(solution)/shard_map/pallas_call | solution.py:1312
  736.5 6.7 convert.7
  743.2 0.9 reshape.288
  744.2 1.2 copy.37
  745.4 1.2 copy.42
  746.6 1.2 slice.89
  747.9 0.8 slice.90
  748.8 2.5 convert.8
  751.3 0.7 dynamic-slice_bitcast_fusion
  753.9 0.7 sqrt_reduce_fusion
  754.6 1.0 copy.46
  (66 shorter events, 8.9 us)
Async XLA Ops:
  23.9 3.4 copy-start.8
  25.3 2.6 copy-start.9
  31.0 224.6 %copy-start = (bf16[128,2048]{1,0:T(8,128)(2,1)S(1)}, bf16[128,2048]{1,0:T(8,128)(2,1)}, u32[]{:S(2)}) copy-start(bf16[128,2048]{1,0:T(8,128)(2,1)} %hidden.3) | copy-start | bytes 1572868
  255.6 4.3 copy-start.11
  258.3 0.8 copy-start.1
  259.1 0.8 copy-start.5
  554.1 7.6 %copy-start.2 = (bf16[128,2048]{1,0:T(8,128)(2,1)S(1)}, bf16[128,2048]{1,0:T(8,128)(2,1)}, u32[]{:S(2)}) copy-start(bf16[128,2048]{1,0:T(8,128)(2,1)} %get-tuple-element.32) | copy-start | bytes 1572868
  554.1 7.6 %copy-start.4 = (bf16[128,2048]{1,0:T(8,128)(2,1)S(1)}, bf16[128,2048]{1,0:T(8,128)(2,1)}, u32[]{:S(2)}) copy-start(bf16[128,2048]{1,0:T(8,128)(2,1)} %param.25) | copy-start | bytes 1572868
  736.5 6.8 copy-start.6
  746.6 2.2 copy-start.3
  748.8 2.5 copy-start.10
  748.8 3.8 copy-start.12
  748.8 5.8 copy-start.7

commit v7 on v6

--- a/solution.py
+++ b/solution.py
@@ -319,10 +319,10 @@
     weight_in,
     inner_in,
     outer_in,
-    gain_attn,
-    gain,
+    small,
     turn,
     live,
+    gains,
     branch,
     qkv,
     unit,
@@ -334,6 +334,7 @@
     inner_out,
     outer_out,
     hid_v,
+    small_in,
     normed_v,
     w_v,
     raw,
@@ -347,6 +348,8 @@
     outer_raw,
     outer_v,
     local,
+    m_send,
+    m_recv,
     w_send,
     w_recv,
     right_send,
@@ -514,6 +517,16 @@
     ]
     for copy in keeps:
         copy.start()
+
+    def small_copy(k):
+        target = spread(z, f, dp, fsdp, k)
+        return remote(
+            small, small_in.at[me], m_send.at[k], m_recv.at[k], place(BOTH, fsdp, target)
+        )
+
+    for k in range(1, n):
+        small_copy(k).start()
+    small_in[me] = small[...]
     for k in range(1, fsdp):
         weight_copy(k).start()
     for i in range(1, dp):
@@ -555,12 +568,17 @@
     for copy in owns:
         copy.start()
     hidden_gather.wait()
+    for k in range(1, n):
+        small_copy(k).wait()
+    for c in range(n // 2):
+        pair = small_in[2 * c].astype(F32) + small_in[2 * c + 1].astype(F32)
+        gains[:, pl.ds(c * 128, 128)] = pair
 
     def norm_rows(i, carry):
         values = hid_v[i].astype(F32)
         values = values * lax.rsqrt(jnp.mean(values * values, axis=-1, keepdims=True) + EPS)
         r = pl.ds(pl.multiple_of(i * rows, rows), rows)
-        normed_v[r, :] = (values * gain_attn[0:1, :]).astype(BF16)
+        normed_v[r, :] = (values * gains[0:1, :]).astype(BF16)
         return carry
 
     lax.fori_loop(0, fsdp, norm_rows, 0)
@@ -643,7 +661,8 @@
         unit[:, wide] = raw[:, wide] * scale[:, i : i + 1]
         for h in range(cols // HEAD_DIM):
             lane = pl.ds(i * cols + h * HEAD_DIM, HEAD_DIM)
-            values = unit[:, lane] * gain[0:1, lane]
+            own = pl.ds(pl.multiple_of(f * cols + h * HEAD_DIM, HEAD_DIM), HEAD_DIM)
+            values = unit[:, lane] * gains[1 + i : 2 + i, own]
             values = values * turn[0] - pltpu.roll(values, HEAD_DIM // 2, 1) * turn[1]
             qkv[i, :, pl.ds(h * HEAD_DIM, HEAD_DIM)] = values.astype(BF16)
 
@@ -734,7 +753,7 @@
 
 
 def attention_forward(
-    hidden, cot, weight_in, inner_in, outer_in, gain_attn, gain, turn, live, ident
+    hidden, cot, weight_in, inner_in, outer_in, small, turn, live, ident
 ):
     dp = lax.axis_size("dp")
     fsdp = lax.axis_size("fsdp")
@@ -747,7 +766,7 @@
     vmem = pltpu.VMEM
     anywhere = pl.BlockSpec(memory_space=pl.ANY)
     inside = pl.BlockSpec(memory_space=pltpu.VMEM)
-    sems = [dma((fsdp,)), dma((fsdp,))] + [dma((2, dp + 1))] * 4
+    sems = [dma((n,)), dma((n,)), dma((fsdp,)), dma((fsdp,))] + [dma((2, dp + 1))] * 4
     for size in (10, fsdp, 10, fsdp):
         sems += [dma((size,)), dma((size,))]
     sems += [dma((dp, 10)), dma((dp, 10)), dma((dp,)), dma((dp,))]
@@ -758,6 +777,7 @@
     return pl.pallas_call(
         functools.partial(attention_kernel, dp, fsdp),
         out_shape=(
+            shape((small.shape[0], width), F32),
             shape((rows, width), BF16),
             shape((3, seq, cols), BF16),
             shape((seq, 2 * cols), F32),
@@ -769,10 +789,11 @@
             shape((n, 2 * here, width // n, width // 2 // dp), BF16),
             shape((fsdp, here, out_rows, width), BF16),
         ),
-        in_specs=[anywhere] * 5 + [inside] * 4,
-        out_specs=(inside,) * 4 + (anywhere,) * 6,
+        in_specs=[anywhere] * 5 + [inside] * 3,
+        out_specs=(inside,) * 5 + (anywhere,) * 6,
         scratch_shapes=[
             vmem((fsdp, rows, width), BF16),
+            vmem((n,) + small.shape, BF16),
             vmem((seq, width), BF16),
             vmem((width, 4 * cols), BF16),
             vmem((seq, 2 * cols), F32),
@@ -797,8 +818,7 @@
         weight_in,
         inner_in.reshape(-1, width),
         outer_in.reshape(-1, width),
-        gain_attn,
-        gain,
+        small,
         turn,
         live,
     )
@@ -814,12 +834,11 @@
     qkv,
     unit,
     scale,
-    gain,
+    gains,
     turn,
     live,
     grad_middle,
     hidden,
-    gain_attn,
     terms,
     first_in,
     inner_in,
@@ -1091,7 +1110,7 @@
             term_v[1 + i : 2 + i, place_lanes] = jnp.sum(
                 grad * unit[:, wide], axis=0, keepdims=True
             )
-            gqk[:, wide] = grad * gain[0:1, wide]
+            gqk[:, wide] = grad * gains[1 + i : 2 + i, place_lanes]
     row = lax.broadcasted_iota(jnp.int32, (8, 2 * cols), 0)
     lane_of = lax.broadcasted_iota(jnp.int32, (8, 2 * cols), 1)
     chooser = jnp.where(lane_of // cols == row, 1.0, 0.0).astype(F32)
@@ -1157,7 +1176,7 @@
     scale1 = lax.rsqrt(jnp.mean(values * values, axis=-1, keepdims=True) + EPS)
     values = values * scale1
     term_v[0:1, :] = jnp.sum(grad * values, axis=0, keepdims=True)
-    grad = grad * gain_attn[0:1, :]
+    grad = grad * gains[0:1, :]
     grad = scale1 * (grad - values * jnp.mean(grad * values, axis=-1, keepdims=True))
     hidden_grad[...] = grad_middle[...] + grad
 
@@ -1285,12 +1304,11 @@
     qkv,
     unit,
     scale,
-    gain,
+    gains,
     turn,
     live,
     grad_middle,
     hidden,
-    gain_attn,
     terms,
     first_in,
     inner_in,
@@ -1320,7 +1338,7 @@
             shape((fsdp, rows, width // 2), BF16),
             shape((4, rows, width), BF16),
         ),
-        in_specs=[anywhere] * 4 + [inside] * 10 + [anywhere] * 3,
+        in_specs=[anywhere] * 4 + [inside] * 9 + [anywhere] * 3,
         out_specs=(inside,) * 3 + (anywhere,) * 4,
         scratch_shapes=[
             vmem((fsdp, seq, cols), BF16),
@@ -1380,12 +1398,11 @@
         qkv,
         unit,
         scale,
-        gain,
+        gains,
         turn,
         live,
         grad_middle,
         hidden,
-        gain_attn,
         terms,
         first_in,
         inner_in,
@@ -2019,16 +2036,26 @@
     valid = lengths[z]
     scaling = HEAD_DIM ** (-0.5)
 
-    small = jnp.concatenate(
-        [attn_gain, query_gain, key_gain, ffn_gain, router_weight.reshape(-1)]
-    )
-    small_rows = -(-small.size // 2048) * 16
-    small = exchange(tiles_of(small, small_rows), BOTH, 0, False).reshape(n, -1)
-    gains = small[:, : 4 * own_rows].reshape(n, 4, own_rows).transpose(1, 0, 2)
-    gains = gains.reshape(4, width).astype(F32)
-    router_full = small[:, 4 * own_rows : 4 * own_rows + own_rows * experts]
-    router_full = router_full.reshape(width, experts)
-    gain_attn, gain_query, gain_key, gain_ffn = gains[0], gains[1], gains[2], gains[3]
+    if fused:
+        small = jnp.stack([attn_gain, query_gain, key_gain, ffn_gain])
+        blank = jnp.zeros((-(4 + experts) % 16, own_rows), BF16)
+        small = jnp.concatenate([small, router_weight.transpose(1, 0), blank])
+        odd = lax.rem(f, 2) == 1
+        zero = jnp.zeros((), BF16)
+        small = jnp.concatenate(
+            [jnp.where(odd, zero, small), jnp.where(odd, small, zero)], axis=1
+        )
+    else:
+        small = jnp.concatenate(
+            [attn_gain, query_gain, key_gain, ffn_gain, router_weight.reshape(-1)]
+        )
+        small_rows = -(-small.size // 2048) * 16
+        small = exchange(tiles_of(small, small_rows), BOTH, 0, False).reshape(n, -1)
+        gains = small[:, : 4 * own_rows].reshape(n, 4, own_rows).transpose(1, 0, 2)
+        gains = gains.reshape(4, width).astype(F32)
+        router_full = small[:, 4 * own_rows : 4 * own_rows + own_rows * experts]
+        router_full = router_full.reshape(width, experts)
+        gain_attn, gain_query, gain_key, gain_ffn = gains[0], gains[1], gains[2], gains[3]
 
     attn_weight = jnp.concatenate(
         [
@@ -2042,12 +2069,6 @@
     grad_total = cotangent.astype(F32) * live_mask
 
     here = f * cols
-    qk_gain = jnp.stack(
-        [
-            lax.dynamic_slice(gain_query, (here,), (cols,)),
-            lax.dynamic_slice(gain_key, (here,), (cols,)),
-        ]
-    )
     pos = jnp.arange(seq, dtype=jnp.int32)
     frequency = jnp.power(10000.0, -jnp.arange(HEAD_DIM // 2, dtype=F32) * 2.0 / HEAD_DIM)
     angles = pos.astype(F32)[:, None] * frequency[None, :]
@@ -2055,7 +2076,6 @@
     sine = jnp.sin(angles)[:, None, None, :]
 
     if fused:
-        gain_wide = jnp.broadcast_to(qk_gain.reshape(1, 2 * cols), (8, 2 * cols))
         turn = jnp.stack(
             [
                 jnp.concatenate([cosine, cosine], axis=-1).reshape(seq, HEAD_DIM),
@@ -2064,6 +2084,7 @@
         )
         live_keys = jnp.broadcast_to((pos < valid).astype(F32)[None], (8, seq))
         (
+            gains,
             branch,
             qkv,
             qk_unit,
@@ -2080,14 +2101,21 @@
             attn_weight,
             expert_in,
             expert_out,
-            jnp.broadcast_to(gain_attn[None], (8, width)),
-            gain_wide,
+            small,
             turn,
             live_keys,
             10,
         )
         branch = branch.astype(F32)
+        gain_ffn = gains[3]
+        router_full = gains[4 : 4 + experts].transpose(1, 0).astype(BF16)
     else:
+        qk_gain = jnp.stack(
+            [
+                lax.dynamic_slice(gain_query, (here,), (cols,)),
+                lax.dynamic_slice(gain_key, (here,), (cols,)),
+            ]
+        )
         attn_weight = lax.all_to_all(attn_weight, "fsdp", 0, 0, tiled=True)
         attn_weight = lax.all_gather(
             attn_weight.reshape(fsdp * own_rows, 4 * cols), "dp", axis=0, tiled=True
@@ -2204,12 +2232,11 @@
             qkv,
             qk_unit,
             qk_scale,
-            gain_wide,
+            gains,
             turn,
             live_keys,
             grad_middle,
             hidden_in,
-            jnp.broadcast_to(gain_attn[None], (8, width)),
             terms,
             first_grad,
             inner_grad.reshape(n, experts_here * own_rows, ff_here),

time: 765 us -> 756 us (0.988)
    pallas_call x1 -> x0, Pallas kernels: 11.1 us -> none  [exchange(): pl.pallas_call(functools.partial(exchange_kernel, axes, n, fsdp, spread),...]
where the time goes in v7:
time: 756 us; the launch traced here: 746 us
  Pallas kernels  695 us (92%)
  other arithmetic  25.3 us (3%)
  local copies, waits for them, and re-layouts  18.4 us (2%)
    pallas_call x1, Pallas kernels, expert_pass(): pl.pallas_call(functools.partial(expert_kernel, dp, fsdp), out_shape=(sha...  292 us
    pallas_call x1, Pallas kernels, attention_forward(): pl.pallas_call(functools.partial(attention_kernel, dp, fsdp), out_shape=(...  232 us
    pallas_call x1, Pallas kernels, attention_back(): pl.pallas_call(functools.partial(attention_back_kernel, dp, fsdp), out_sh...  172 us

profile of v7, /device:TPU:0, one launch (start us, length us, event | category | flops | bytes accessed | tf_op | source)
XLA Modules:
  0.0 746.4 jit_solution(9404199683474074524)
XLA Ops:
  0.7 1.6 concatenate.19
  2.3 0.7 pad_maximum_fusion.1.small
  3.0 1.2 dynamic_slice.6
  4.9 2.0 fusion.3.cot
  6.9 1.9 multiply_cosine_fusion
  9.1 1.0 pad_maximum_fusion.turn
  10.2 0.7 fusion.10
  12.6 1.1 maximum_bitcast_fusion
  13.7 1.5 reshape.237.weight_in
  15.2 231.6 %shard_map.220 = (f32[32,2048]{1,0:T(8,128)}, bf16[128,2048]{1,0:T(8,128)(2,1)}, bf16[3,1024,256]{2,1,0:T(8,128)(2,1)}, f32[1024,512]{1,0:T(8,128)}, f32[1024,12...) custom-call(bf16[128,2048]{1,0:T(8,128)(2,1)} %hidden.3, ...), custom_call_target="tpu_custom_call" | custom-call | tf_op jit(solution)/shard_map/pallas_call | solution.py:777
  246.9 0.9 slice.45
  247.8 1.3 multiply_reduce_fusion.2
  249.1 1.3 multiply_convert_fusion.x_in
  250.4 0.8 copy-done.1
  252.2 291.8 %shard_map.221 = (f32[2,128,2048]{2,1,0:T(8,128)}, f32[8,8,128]{2,1,0:T(8,128)}, bf16[8,128,1024]{2,1,0:T(8,128)(2,1)}, bf16[32,2,64,256]{3,2,1,0:T(8,128)(2,1)}...) custom-call(bf16[128,2048]{1,0:T(8,128)(2,1)} %copy-done.1, ...), custom_call_target="tpu_custom_call" | custom-call | tf_op jit(solution)/shard_map/pallas_call | solution.py:1901
  544.1 0.8 slice.49
  544.9 1.2 fusion.14
  546.1 4.0 fusion
  550.1 2.0 pad_maximum_fusion.2
  552.2 1.3 concatenate.23.terms
  553.5 1.6 fusion.12
  555.1 171.7 %shard_map.222 = (f32[128,2048]{1,0:T(8,128)}, f32[24,128]{1,0:T(8,128)}, bf16[8,64,1024]{2,1,0:T(8,128)(2,1)}, bf16[1024,2048]{1,0:T(8,128)(2,1)}, bf16[4,128,2...) custom-call(bf16[128,2048]{1,0:T(8,128)(2,1)} %get-tuple-element.61.grad_rows, ...), custom_call_target="tpu_custom_call" | custom-call | tf_op jit(solution)/shard_map/pallas_call | solution.py:1330
  726.8 6.7 convert.9
  733.6 0.9 reshape.254
  734.6 1.2 copy.35
  735.8 1.2 copy.38
  737.0 1.2 slice.59
  738.2 0.8 slice.60
  739.1 2.5 convert.10
  741.7 0.7 dynamic-slice_bitcast_fusion
  744.2 0.7 sqrt_reduce_fusion
  745.0 1.0 copy.40
  (51 shorter events, 5.1 us)
Async XLA Ops:
  8.8 2.7 copy-start.7
  10.2 1.9 copy-start.9
  15.2 232.6 %copy-start = (bf16[128,2048]{1,0:T(8,128)(2,1)S(1)}, bf16[128,2048]{1,0:T(8,128)(2,1)}, u32[]{:S(2)}) copy-start(bf16[128,2048]{1,0:T(8,128)(2,1)} %hidden.3) | copy-start | bytes 1572868
  246.9 4.3 copy-start.8
  246.9 4.6 copy-start.11
  250.4 0.8 copy-start.1
  546.1 7.4 copy-start.2
  546.1 7.4 copy-start.4
  726.8 6.8 copy-start.5
  737.0 2.2 copy-start.3
  739.1 2.5 copy-start.10
  739.1 3.8 copy-start.12
  739.1 5.8 copy-start.6

commit v8 on v7

--- a/solution.py
+++ b/solution.py
@@ -2,6 +2,7 @@
 
 import jax
 import jax.numpy as jnp
+import numpy as np
 from jax import lax
 from jax.experimental import pallas as pl
 from jax.experimental.pallas import tpu as pltpu
@@ -35,6 +36,16 @@
         ],
         axis=-1,
     )
+
+
+def turning(seq):
+    steps = np.arange(HEAD_DIM // 2, dtype=np.float32) * np.float32(2.0) / np.float32(HEAD_DIM)
+    frequency = np.power(np.float32(10000.0), -steps)
+    angles = np.arange(seq, dtype=np.float32)[:, None] * frequency[None, :]
+    cosine = np.cos(angles)
+    sine = np.sin(angles)
+    both = [np.concatenate([cosine, cosine], axis=1), np.concatenate([sine, -sine], axis=1)]
+    return np.stack(both).astype(np.float32)
 
 
 def place(axes, fsdp, index):
@@ -2076,12 +2087,7 @@
     sine = jnp.sin(angles)[:, None, None, :]
 
     if fused:
-        turn = jnp.stack(
-            [
-                jnp.concatenate([cosine, cosine], axis=-1).reshape(seq, HEAD_DIM),
-                jnp.concatenate([sine, -sine], axis=-1).reshape(seq, HEAD_DIM),
-            ]
-        )
+        turn = jnp.asarray(turning(seq))
         live_keys = jnp.broadcast_to((pos < valid).astype(F32)[None], (8, seq))
         (
             gains,

time: 756 us -> 754 us (level)
  no operation moved by 1% of the time
where the time goes in v8:
time: 754 us; the launch traced here: 746 us
  Pallas kernels  697 us (92%)
  other arithmetic  22 us (3%)
  local copies, waits for them, and re-layouts  19.5 us (3%)
    pallas_call x1, Pallas kernels, expert_pass(): pl.pallas_call(functools.partial(expert_kernel, dp, fsdp), out_shape=(sha...  292 us
    pallas_call x1, Pallas kernels, attention_forward(): pl.pallas_call(functools.partial(attention_kernel, dp, fsdp), out_shape=(...  232 us
    pallas_call x1, Pallas kernels, attention_back(): pl.pallas_call(functools.partial(attention_back_kernel, dp, fsdp), out_sh...  173 us

profile of v8, /device:TPU:0, one launch (start us, length us, event | category | flops | bytes accessed | tf_op | source)
XLA Modules:
  0.0 745.6 jit_solution(18361639256872951632)
XLA Ops:
  0.7 1.6 concatenate.13
  2.3 0.7 pad_maximum_fusion.small
  3.0 1.2 dynamic_slice.6
  4.2 0.6 compare_convert_fusion
  4.9 2.0 fusion.3.cot
  8.2 1.3 copy.37
  10.4 1.1 maximum_bitcast_fusion
  11.5 1.5 reshape.106.weight_in
  13.0 231.6 %shard_map.229 = (f32[32,2048]{1,0:T(8,128)}, bf16[128,2048]{1,0:T(8,128)(2,1)}, bf16[3,1024,256]{2,1,0:T(8,128)(2,1)}, f32[1024,512]{1,0:T(8,128)}, f32[1024,12...) custom-call(bf16[128,2048]{1,0:T(8,128)(2,1)} %hidden.3, ...), custom_call_target="tpu_custom_call" | custom-call | tf_op jit(solution)/shard_map/pallas_call | solution.py:788
  244.7 0.9 slice.45
  245.6 1.3 multiply_reduce_fusion.2
  246.9 1.3 multiply_convert_fusion.x_in
  248.2 0.8 copy-done.1
  249.4 0.7 pad.4.gates
  250.1 291.8 %shard_map.230 = (f32[2,128,2048]{2,1,0:T(8,128)}, f32[8,8,128]{2,1,0:T(8,128)}, bf16[8,128,1024]{2,1,0:T(8,128)(2,1)}, bf16[32,2,64,256]{3,2,1,0:T(8,128)(2,1)}...) custom-call(bf16[128,2048]{1,0:T(8,128)(2,1)} %copy-done.1, ...), custom_call_target="tpu_custom_call" | custom-call | tf_op jit(solution)/shard_map/pallas_call | solution.py:1912
  541.9 0.8 slice.49
  542.7 1.2 fusion.13
  543.9 4.0 fusion
  547.9 2.0 pad_maximum_fusion.1
  550.0 1.3 concatenate.15.terms
  551.3 1.6 fusion.11
  552.9 173.1 %shard_map.231 = (f32[128,2048]{1,0:T(8,128)}, f32[24,128]{1,0:T(8,128)}, bf16[8,64,1024]{2,1,0:T(8,128)(2,1)}, bf16[1024,2048]{1,0:T(8,128)(2,1)}, bf16[4,128,2...) custom-call(bf16[128,2048]{1,0:T(8,128)(2,1)} %get-tuple-element.61.grad_rows, ...), custom_call_target="tpu_custom_call" | custom-call | tf_op jit(solution)/shard_map/pallas_call | solution.py:1341
  726.0 6.7 convert.9
  732.8 0.9 reshape.123
  733.7 1.2 copy.36
  735.0 1.2 copy.39
  736.2 1.2 slice.59
  737.4 0.8 slice.60
  738.3 2.5 convert.10
  740.9 0.7 dynamic-slice_bitcast_fusion
  743.4 0.7 sqrt_reduce_fusion
  744.2 1.0 copy.41
  (44 shorter events, 4.0 us)
Async XLA Ops:
  4.9 5.0 copy-start.8
  13.0 232.6 %copy-start = (bf16[128,2048]{1,0:T(8,128)(2,1)S(1)}, bf16[128,2048]{1,0:T(8,128)(2,1)}, u32[]{:S(2)}) copy-start(bf16[128,2048]{1,0:T(8,128)(2,1)} %hidden.3) | copy-start | bytes 1572868
  244.7 4.3 copy-start.7
  244.7 4.6 copy-start.10
  248.2 0.8 copy-start.1
  543.9 7.4 copy-start.2
  543.9 7.4 copy-start.4
  726.0 6.8 copy-start.5
  736.2 2.2 copy-start.3
  738.3 2.5 copy-start.9
  738.3 3.8 copy-start.11
  738.3 5.8 copy-start.6
